TPU v7x, 512 devices: a whole 4x4x16 slice. The times are simulated.
512 devices in a mesh: row: 32 (over y, x, core), col: 16 (over z).
Axes of the slice: x: 4, y: 4, z: 16, core: 2. Of those that a mesh axis runs over, the one named last changes fastest.
Arguments:
- matrix: float32 [2, 32, 4, 16, 256, 256], P(None, 'row', None, 'col'), may hold values from -8 to 392
- structure: int32 [2, 64], replicated, may hold values from 0 to 1, as said below
Outputs:
- factored: float32 [2, 32, 4, 16, 256, 256], P(None, 'row', None, 'col')
Inputs may be any that keep to these rules, and one draw needn't show every extreme that they name: structure[k, i] = 0 for i <= k; structure[0, 1] = 1; structure[1, i] >= structure[0, i] for i >= 2.
All inputs are finite; a program needn't handle non-finite values.
Results may differ from a plain program's by a relative error of at most 0.0001.
Values sent between devices are 32-bit elements; how exact they have to be, the bound alone decides.
No kernel may reach another device: no remote copies, remote signals or barrier semaphores. Data moves between devices by JAX's collectives and lax.ppermute only.
A program may use at most 64 MiB of HBM per device.

v0:
```python
import jax
import jax.numpy as jnp
from jax import lax
from jax.sharding import PartitionSpec as P

SUPERNODES = 2


def from_root(block, axis, owner):
    block = jnp.where(lax.axis_index(axis) == owner, block, jnp.zeros_like(block))
    return lax.psum(block, axis)


def column_operand(own_rows, nrow, ncol, col_id):
    ratio = nrow // ncol
    lbr = own_rows.shape[0]
    width = own_rows.shape[1]
    pieces = [from_root(own_rows, "row", index * ncol + col_id) for index in range(ratio)]
    return jnp.stack(pieces, 1).reshape(lbr * ratio, width, width)


def factor_step(first_column, structure, step, rows_glob, nrow, ncol, col_id):
    lbr = first_column.shape[0]
    width = first_column.shape[1]
    nblocks = structure.shape[1]
    diag_raw = from_root(first_column[0], "row", step % nrow)
    sym = jnp.tril(diag_raw) + jnp.tril(diag_raw, -1).T
    factor = jnp.linalg.cholesky(sym)
    stack = first_column.reshape(lbr * width, width)
    solved = lax.linalg.triangular_solve(
        factor, stack, left_side=False, lower=True, transpose_a=True
    )
    solved = solved.reshape(lbr, width, width)
    picker = (jnp.arange(nblocks, dtype=jnp.int32)[None, :] == rows_glob[:, None]).astype(jnp.int32)
    keep = jnp.sum(picker * structure[step][None, :], axis=1).astype(jnp.float32)
    panel = solved * keep[:, None, None]
    column = jnp.where(
        (rows_glob == step)[:, None, None],
        jnp.tril(factor)[None],
        jnp.where((rows_glob > step)[:, None, None], panel, first_column),
    )
    own_rows = from_root(panel, "col", step % ncol)
    other_cols = column_operand(own_rows, nrow, ncol, col_id)
    return (column, own_rows, other_cols)


def outer_terms(own_rows, other_cols):
    return jnp.einsum("las,mbs->lmab", own_rows, other_cols, precision=lax.Precision.HIGHEST)


def on_device(matrix, structure):
    lbr = matrix.shape[0]
    lbc = matrix.shape[2]
    width = matrix.shape[4]
    blocks = matrix.reshape(lbr, lbc, width, width)
    nrow = lax.axis_size("row")
    ncol = lax.axis_size("col")
    row_id = lax.axis_index("row")
    col_id = lax.axis_index("col")
    rows_glob = jnp.arange(lbr, dtype=jnp.int32) * nrow + row_id
    cols_glob = jnp.arange(lbc, dtype=jnp.int32) * ncol + col_id
    lower = (rows_glob[:, None] >= cols_glob[None, :]).astype(jnp.float32)[:, :, None, None]
    for step in range(SUPERNODES):
        column, own_rows, other_cols = factor_step(
            blocks[:, 0], structure, step, rows_glob, nrow, ncol, col_id
        )
        blocks = blocks - lower * outer_terms(own_rows, other_cols)
        blocks = blocks.at[:, 0].set(jnp.where(col_id == step % ncol, column, blocks[:, 0]))
    return blocks.reshape(matrix.shape)


def solution(mesh):
    in_specs = (P(None, "row", None, "col", None, None), P())
    out_specs = P(None, "row", None, "col", None, None)
    return jax.shard_map(
        on_device, mesh=mesh, in_specs=in_specs, out_specs=out_specs, check_vma=False
    )
```

profile of v0, /device:TPU:6, one launch (start us, length us, event | category | flops | bytes accessed | tf_op | source)
XLA Modules:
  0.0 982.1 jit_solution(15823435262278763749)
XLA Ops:
  6.5 1.7 fusion.17
  10.6 137.3 %all-reduce.10.cloned.1.call-done = f32[256,256]{1,0:T(8,128)} async-done(((f32[256,256]{1,0:T(8,128)}), f32[256,256]{1,0:T(8,128)}) %all-reduce.10.cloned.1.call-update) | async-done | bytes 262160 | tf_op jit(solution)/shard_map/psum | solution.py:11
  150.2 11.7 %cholesky.130 = f32[128,128]{1,0:T(8,128)S(1)} custom-call(f32[128,128]{1,0:T(8,128)S(1)} %cholesky.194), custom_call_target="Cholesky" | custom-call | tf_op jit(solution)/shard_map/jit(cholesky)/cholesky | solution.py:28
  161.9 9.8 custom-call.13
  172.2 11.7 %cholesky.147 = f32[128,128]{1,0:T(8,128)S(1)} custom-call(f32[128,128]{1,0:T(8,128)S(1)} %convolution_subtract_fusion.3), custom_call_target="Cholesky" | custom-call | tf_op jit(solution)/shard_map/jit(cholesky)/cholesky | solution.py:28
  186.1 4.2 while.6
  186.9 1.4 bitcast_dynamic-update-slice_fusion.5
  188.9 1.4 bitcast_dynamic-update-slice_fusion.5
  190.2 19.7 %custom-call.14 = f32[2,128,128]{1,2,0:T(8,128)S(1)} custom-call(f32[2,128,128]{2,1,0:T(8,128)S(1)} %get-tuple-element.45), custom_call_target="InvertDiagBlocksLowerTriangular" | custom-call | tf_op jit(solution)/shard_map/triangular_solve/custom-call.0 | solution.py:30
  213.8 134.7 %all-reduce.12.cloned.1.call-done = f32[2,256,256]{2,1,0:T(8,128)} async-done(((f32[2,256,256]{2,1,0:T(8,128)}), f32[2,256,256]{2,1,0:T(8,128)}) %all-reduce.12.cloned.1.call-update) | async-done | bytes 524304 | tf_op jit(solution)/shard_map/psum | solution.py:11
  348.5 2.1 select_bitcast_fusion.3
  352.0 133.0 %all-reduce.20.cloned.1.call-done = (f32[2,1,256,256]{3,2,0,1:T(8,128)}, f32[2,1,256,256]{3,2,0,1:T(8,128)}) async-done(((f32[2,1,256,256]{3,2,0,1:T(8,128)}, f32[2,1,256,256]{3,2,0,1:T(8,128)}), (f32[2,1,256,256]{3,2,0,1:T(8,128)}, f32[2,1,256,256]{3,2,0,1:T(8,128)})) %all-reduce.20.cloned.1.call-update) | async-done | bytes 1048592 | tf_op jit(solution)/shard_map/psum | solution.py:11
  485.0 1.4 pad_maximum_fusion
  487.0 2.0 fusion.1
  492.4 2.3 fusion.33
  494.7 2.0 copy.64
  496.7 2.2 select_select_fusion
  498.9 124.9 %all-reduce.14.cloned.1.call-done = f32[256,256]{1,0:T(8,128)} async-done(((f32[256,256]{1,0:T(8,128)}), f32[256,256]{1,0:T(8,128)}) %all-reduce.14.cloned.1.call-update) | async-done | bytes 262160 | tf_op jit(solution)/shard_map/psum | solution.py:11
  626.9 11.7 %cholesky.164 = f32[128,128]{1,0:T(8,128)S(1)} custom-call(f32[128,128]{1,0:T(8,128)S(1)} %cholesky.197), custom_call_target="Cholesky" | custom-call | tf_op jit(solution)/shard_map/jit(cholesky)/cholesky | solution.py:28
  639.3 9.8 custom-call.15
  651.3 11.7 %cholesky.181 = f32[128,128]{1,0:T(8,128)S(1)} custom-call(f32[128,128]{1,0:T(8,128)S(1)} %convolution_subtract_fusion.2), custom_call_target="Cholesky" | custom-call | tf_op jit(solution)/shard_map/jit(cholesky)/cholesky | solution.py:28
  664.9 4.3 while.7
  665.8 1.4 bitcast_dynamic-update-slice_fusion.6
  667.8 1.4 bitcast_dynamic-update-slice_fusion.6
  669.2 19.7 %custom-call.16 = f32[2,128,128]{1,2,0:T(8,128)S(1)} custom-call(f32[2,128,128]{2,1,0:T(8,128)S(1)} %get-tuple-element.46), custom_call_target="InvertDiagBlocksLowerTriangular" | custom-call | tf_op jit(solution)/shard_map/triangular_solve/custom-call.0 | solution.py:30
  688.9 1.4 fusion.11
  690.3 1.3 convolution_subtract_fusion
  695.1 135.8 %all-reduce.16.cloned.1.call-done = f32[2,256,256]{2,1,0:T(8,128)} async-done(((f32[2,256,256]{2,1,0:T(8,128)}), f32[2,256,256]{2,1,0:T(8,128)}) %all-reduce.16.cloned.1.call-update) | async-done | bytes 524304 | tf_op jit(solution)/shard_map/psum | solution.py:11
  830.9 2.1 select_bitcast_fusion.1
  833.0 134.6 %all-reduce.18.cloned.1.call-done = (f32[2,1,256,256]{3,2,0,1:T(8,128)}, f32[2,1,256,256]{3,2,0,1:T(8,128)}) async-done(((f32[2,1,256,256]{3,2,0,1:T(8,128)}, f32[2,1,256,256]{3,2,0,1:T(8,128)}), (f32[2,1,256,256]{3,2,0,1:T(8,128)}, f32[2,1,256,256]{3,2,0,1:T(8,128)})) %all-reduce.18.cloned.1.call-update) | async-done | bytes 1048592 | tf_op jit(solution)/shard_map/psum | solution.py:11
  967.7 1.4 pad_maximum_fusion.1
  969.7 2.0 fusion
  (108 shorter events, 31.5 us)
Async XLA Ops:
  6.5 141.3 %all-reduce.10.cloned.1.call-start = ((), (), s32[]{:S(2)}) async-start(), calls=%async_computation | async-start | bytes 524288 | tf_op jit(solution)/shard_map/psum | solution.py:11
  8.2 340.3 %all-reduce.12.cloned.1.call-start = ((), (), s32[]{:S(2)}) async-start(), calls=%async_computation.1 | async-start | bytes 1048576 | tf_op jit(solution)/shard_map/psum | solution.py:11
  212.5 272.5 %all-reduce.20.cloned.1.call-start = ((), (), s32[]{:S(2)}) async-start(), calls=%async_computation.5 | async-start | bytes 2097152 | tf_op jit(solution)/shard_map/psum | solution.py:11
  350.6 273.2 %all-reduce.14.cloned.1.call-start = ((), (), s32[]{:S(2)}) async-start(), calls=%async_computation.2 | async-start | bytes 524288 | tf_op jit(solution)/shard_map/psum | solution.py:11
  485.0 1.9 copy-start.1
  485.0 2.0 copy-start.6
  490.6 0.8 copy-start.2
  492.1 338.8 %all-reduce.16.cloned.1.call-start = ((), (), s32[]{:S(2)}) async-start(), calls=%async_computation.3 | async-start | bytes 1048576 | tf_op jit(solution)/shard_map/psum | solution.py:11
  626.2 0.7 copy-start.8
  669.2 22.8 %copy-start.3 = (f32[256,256]{1,0:T(8,128)}, f32[256,256]{1,0:T(8,128)S(1)}, u32[]{:S(2)}) copy-start(f32[256,256]{1,0:T(8,128)S(1)} %get-tuple-element.200) | copy-start | bytes 786436
  695.0 272.7 %all-reduce.18.cloned.1.call-start = ((), (), s32[]{:S(2)}) async-start(), calls=%async_computation.4 | async-start | bytes 2097152 | tf_op jit(solution)/shard_map/psum | solution.py:11
  967.7 1.9 copy-start
  967.7 2.0 copy-start.7
  971.7 1.0 copy-start.4
  974.0 1.3 copy-start.5
Sparse Core Ops, SparseCore 0:
  10.6 137.1 all-reduce.9
  212.7 135.7 all-reduce.11
  351.8 133.2 all-reduce.19
  492.2 131.5 all-reduce.13
  695.1 135.7 all-reduce.15
  834.3 133.2 all-reduce.17
where the time goes:
time: 983 us; the launch traced here: 982 us
  waiting for transfers between devices  800 us (81%)
  other arithmetic  127 us (13%)
  local copies, waits for them, and re-layouts  25.8 us (3%)
  between operations  16.4 us (2%)
  matrix products  11.2 us (1%)
    psum x6, waiting for transfers between devices, from_root(): return lax.psum(block, axis)  800 us
    another operation x13, other arithmetic, factor_step(): factor = jnp.linalg.cholesky(sym)  68.6 us
    another operation x8, other arithmetic, factor_step(): lax.linalg.triangular_solve(factor, stack, left_side=False, lower=True, t...  40.3 us
  transfers between devices with their start and end apart: 6, of which 6 were waited for; matrix products, arithmetic and copies ran while one was open for 1% of the time, Pallas kernels for 0%

commit v1 on v0

v1 whole, which is shorter than its diff:
```python
import jax
import jax.numpy as jnp
from jax import lax
from jax.experimental import pallas as pl
from jax.experimental.pallas import tpu as pltpu
from jax.sharding import PartitionSpec as P

HIGHEST = lax.Precision.HIGHEST
NX, NY = 4, 4


def row_of(x, y, core):
    return (y % NY) * 2 * NX + (x % NX) * 2 + core


def place_of(row):
    return (row // 2) % NX, row // (2 * NX), row % 2


def plane_shift(dx, dy):
    pairs = []
    for row in range(2 * NX * NY):
        x, y, core = place_of(row)
        pairs.append((row, row_of(x + dx, y + dy, core)))
    return pairs


def mm_t(a, b):
    return lax.dot_general(a, b, (((1,), (1,)), ((), ())), precision=HIGHEST,
                           preferred_element_type=jnp.float32)


def factor_both(a00, a10, a11, keep):
    eye = jnp.eye(a00.shape[0], dtype=jnp.float32)

    def one(block):
        sym = jnp.tril(block) + jnp.tril(block, -1).T
        low = jnp.linalg.cholesky(sym)
        inv = lax.linalg.triangular_solve(low, eye, left_side=True, lower=True)
        return low, inv

    low0, inv0 = one(a00)
    p10 = mm_t(a10, inv0) * keep
    low1, inv1 = one(a11 - mm_t(p10, p10))
    return jnp.concatenate([inv0, p10, inv1]), low0, low1


def spread_diagonal(stacked, col_id):
    nrow = lax.axis_size("row")
    total, width = stacked.shape
    part = lax.all_to_all(stacked.reshape(nrow, total // nrow, width), "row", 0, 0)[0]
    part = jnp.where(col_id == 0, part, 0.0)
    for sources, steps in (((0,), (4, 12, 8)), ((0, 4, 8, 12), (1, 15, 2))):
        sent = [lax.ppermute(part, "col", [(s, (s + d) % 16) for s in sources]) for d in steps]
        part = part + sent[0] + sent[1] + sent[2]
    part = lax.all_to_all(jnp.broadcast_to(part[None], (nrow,) + part.shape), "row", 0, 0)
    return part.reshape(total, width)


def spread_rows(mine, col_id, ncol):
    far = lax.ppermute(mine, "col", [(0, 8), (1, 9)])
    have = jnp.where(col_id < 2, mine, far)
    for step in (4, 2):
        sources = [s for s in range(ncol) if s % (2 * step) < 2]
        up = lax.ppermute(have[0], "col", [(s, (s + step) % ncol) for s in sources])
        down = lax.ppermute(have[1], "col", [(s, (s - step) % ncol) for s in sources])
        have = jnp.where(lax.rem(col_id, 2 * step) < 2, have, jnp.stack([up, down]))
    up = lax.ppermute(have[0], "col", [(s, (s + 1) % ncol) for s in range(ncol)])
    down = lax.ppermute(have[1], "col", [(s, (s - 1) % ncol) for s in range(ncol)])
    near = jnp.stack([up, down])
    even = lax.rem(col_id, 2) == 0
    return jnp.where(even, have, near), jnp.where(even, near, have)


def spread_columns(mine, row_id, nrow, ncol):
    width = mine.shape[-1]
    xpos, ypos, core = place_of(row_id)
    quarter = width // 4
    part = 0.0
    for k in range(4):
        pairs = []
        for row in range(nrow):
            for column in (0, 1):
                target = row_of(k, column + 2 * (row // ncol), 0)
                pairs.append((row * ncol + column, target * ncol + row % ncol))
        part = part + lax.ppermute(mine[:, k * quarter:(k + 1) * quarter], ("row", "col"), pairs)
    swap = [(row, row ^ 1) for row in range(nrow)]
    piece = jnp.where(core == 0, part[0], lax.ppermute(part[1], "row", swap))
    line = jnp.zeros((4, quarter, width), jnp.float32)
    line = lax.dynamic_update_slice(line, piece[None], (xpos, 0, 0))
    for d in (1, 3, 2):
        got = lax.ppermute(piece, "row", plane_shift(d, 0))
        line = lax.dynamic_update_slice(line, got[None], (lax.rem(xpos - d + 4, 4), 0, 0))
    block = line.reshape(width, width)
    got = {d: lax.ppermute(block, "row", plane_shift(0, d)) for d in (1, 3, 2)}
    own = jnp.stack([block, got[1], got[2], got[3]])
    return own, lax.ppermute(own, "row", swap)


def tail_kernel(ids, struct, diag, low0, low1, rows0, rows1, own, other, mat, out, prow, pcol):
    row, col, ypos, core = ids[0], ids[1], ids[2], ids[3]
    width = mat.shape[-1]
    inv0 = diag[0:width, :]
    p10 = diag[width:2 * width, :]
    inv1 = diag[2 * width:3 * width, :]

    def solve(a0, a1, glob):
        keep0 = struct[0, glob].astype(jnp.float32)
        keep1 = struct[1, glob].astype(jnp.float32)
        p0 = mm_t(a0, inv0) * keep0
        p1 = mm_t(a1 - mm_t(p0, p10), inv1) * keep1
        return p0, p1

    for p in range(2):
        p0, p1 = solve(rows0[p], rows1[p], p * 32 + row)
        prow[p, 0] = p0
        prow[p, 1] = p1
    for q in range(4):
        half, high = q % 2, q // 2
        slot0 = lax.rem(ypos - 2 * half + 4, 4)
        slot1 = lax.rem(ypos - 2 * half + 3, 4)
        is_own = core == high
        a0 = jnp.where(is_own, own[slot0], other[slot0])
        a1 = jnp.where(is_own, own[slot1], other[slot1])
        p0, p1 = solve(a0, a1, q * 16 + col)
        pcol[q, 0] = p0
        pcol[q, 1] = p1
    for p in range(2):
        for q in range(4):
            i = p * 32 + row
            j = q * 16 + col
            out[p, q] = mat[p, q]

            @pl.when(i >= j)
            def _():
                out[p, q] = (mat[p, q] - mm_t(prow[p, 0], pcol[q, 0])) - mm_t(prow[p, 1], pcol[q, 1])

            if q == 0:
                @pl.when((j == 0) & (i > 0))
                def _():
                    out[p, q] = prow[p, 0]

                @pl.when((j == 1) & (i > 1))
                def _():
                    out[p, q] = prow[p, 1]

            if p == 0 and q == 0:
                @pl.when((j == 0) & (i == 0))
                def _():
                    out[p, q] = low0[...]

                @pl.when((j == 1) & (i == 1))
                def _():
                    out[p, q] = low1[...]


def on_device(matrix, structure):
    lbr = matrix.shape[0]
    lbc = matrix.shape[2]
    width = matrix.shape[4]
    blocks = matrix.reshape(lbr, lbc, width, width)
    nrow = lax.axis_size("row")
    ncol = lax.axis_size("col")
    row_id = lax.axis_index("row")
    col_id = lax.axis_index("col")
    both = ("row", "col")
    mine = blocks[:, 0]

    a10 = lax.ppermute(mine[0], both, [(ncol, 0)])
    a11 = lax.ppermute(mine[0], both, [(ncol + 1, 0)])
    own, other = spread_columns(mine, row_id, nrow, ncol)
    rows0, rows1 = spread_rows(mine, col_id, ncol)

    block = jax.ShapeDtypeStruct((width, width), jnp.float32)
    stacked, low0, low1 = lax.cond(
        (row_id == 0) & (col_id == 0),
        lambda: factor_both(mine[0], a10, a11, structure[0, 1].astype(jnp.float32)),
        lambda: (jnp.zeros((3 * width, width), jnp.float32),) + (jnp.zeros(block.shape, jnp.float32),) * 2,
    )
    low1 = lax.ppermute(low1, both, [(0, ncol + 1)])
    diag = spread_diagonal(stacked, col_id)

    _, ypos, core = place_of(row_id)
    ids = jnp.stack([row_id, col_id, ypos, core]).astype(jnp.int32)
    vmem = pl.BlockSpec(memory_space=pltpu.VMEM)
    smem = pl.BlockSpec(memory_space=pltpu.SMEM)
    result = pl.pallas_call(
        tail_kernel,
        out_shape=jax.ShapeDtypeStruct(blocks.shape, jnp.float32),
        in_specs=[smem] * 2 + [vmem] * 8,
        out_specs=vmem,
        scratch_shapes=[
            pltpu.VMEM((2, 2, width, width), jnp.float32),
            pltpu.VMEM((4, 2, width, width), jnp.float32),
        ],
        compiler_params=pltpu.CompilerParams(vmem_limit_bytes=40 * 2**20),
    )(ids, structure, diag, low0, low1, rows0, rows1, own, other, blocks)
    return result.reshape(matrix.shape)


def solution(mesh):
    in_specs = (P(None, "row", None, "col", None, None), P())
    out_specs = P(None, "row", None, "col", None, None)
    return jax.shard_map(
        on_device, mesh=mesh, in_specs=in_specs, out_specs=out_specs, check_vma=False
    )
```

time: 983 us -> 296 us (0.30)
  waiting for transfers between devices: 800 us -> 16.9 us
  starting transfers between devices: 0.43 us -> 238 us
  other arithmetic: 127 us -> 7.49 us
  between operations: 16.4 us -> 0.59 us
  Pallas kernels: 0 us -> 11.6 us
  matrix products: 11.2 us -> 0 us
    psum x6 -> x0, waiting for transfers between devices: 800 us -> none  [from_root(): return lax.psum(block, axis)]
    all_to_all x0 -> x2, starting transfers between devices: none -> 161 us  [the longest x1 155 us: spread_diagonal(): lax.all_to_all(stacked.reshape(nrow, total // nrow, width), 'row', 0, 0)[0]]
    another operation x25 -> x2, other arithmetic: 116 us -> 1.34 us  [the longest x1 1.26 us: spread_columns(): own = jnp.stack([block, got[1], got[2], got[3]])]
    ppermute x0 -> x28, starting transfers between devices: none -> 77.5 us  [the longest x4 17.2 us: spread_columns(): lax.ppermute(mine[:, k * quarter:(k + 1) * quarter], ('row', 'col'), pairs)]
    ppermute x0 -> x28, waiting for transfers between devices: none -> 16.9 us  [the longest x4 7.04 us: spread_columns(): lax.ppermute(mine[:, k * quarter:(k + 1) * quarter], ('row', 'col'), pairs)]
    pallas_call x0 -> x1, Pallas kernels: none -> 11.6 us  [on_device(): pl.pallas_call(tail_kernel, out_shape=jax.ShapeDtypeStruct(blocks.shape,...]
  transfers between devices with their start and end apart: 6 -> 30, of which waited for: 6 -> 7; matrix products, arithmetic and copies ran while one was open for 1% -> 6% of each run, Pallas kernels for 0% -> 0%
where the time goes in v1:
time: 296 us; the launch traced here: 291 us
  starting transfers between devices  238 us (80%)
  waiting for transfers between devices  16.9 us (6%)
  local copies, waits for them, and re-layouts  16.5 us (6%)
  Pallas kernels  11.6 us (4%)
  other arithmetic  7.49 us (3%)
    all_to_all x1, starting transfers between devices, spread_diagonal(): lax.all_to_all(stacked.reshape(nrow, total // nrow, width), 'row', 0, 0)[0]  155 us
    ppermute x4, starting transfers between devices, spread_columns(): lax.ppermute(mine[:, k * quarter:(k + 1) * quarter], ('row', 'col'), pairs)  17.2 us
    ppermute x1, starting transfers between devices, spread_rows(): far = lax.ppermute(mine, 'col', [(0, 8), (1, 9)])  14.3 us
    pallas_call x1, Pallas kernels, on_device(): pl.pallas_call(tail_kernel, out_shape=jax.ShapeDtypeStruct(blocks.shape,...  11.6 us
    ppermute x3, starting transfers between devices, spread_columns(): got = {d: lax.ppermute(block, 'row', plane_shift(0, d)) for d in (1, 3, 2)}  10.2 us
    ppermute x3, starting transfers between devices, spread_columns(): got = lax.ppermute(piece, 'row', plane_shift(d, 0))  7.75 us
    ppermute x6, starting transfers between devices, spread_diagonal(): lax.ppermute(part, 'col', [(s, (s + d) % 16) for s in sources])  7.71 us
    ppermute x4, waiting for transfers between devices, spread_columns(): lax.ppermute(mine[:, k * quarter:(k + 1) * quarter], ('row', 'col'), pairs)  7.04 us
  transfers between devices with their start and end apart: 30, of which 7 were waited for; matrix products, arithmetic and copies ran while one was open for 6% of the time, Pallas kernels for 0%

profile of v1, /device:TPU:6, one launch (start us, length us, event | category | flops | bytes accessed | tf_op | source)
XLA Modules:
  0.0 291.2 jit_solution(11599671169637156753)
XLA Ops:
  0.0 2.0 slice_bitcast_fusion.9
  3.2 12.7 %collective-permute-start.17 = (f32[2,64,256]{2,1,0:T(8,128)S(1)}, f32[2,64,256]{2,1,0:T(8,128)S(1)}, u32[]{:S(2)}, u32[]{:S(2)}) collective-permute-start(f32[2,64,256]{2,1,0:T(8,128)S(1)} %get-tuple-element.89), channel_id=1, source_target_pairs={{0,32},{1,160},{16,33},{17,161},{32,34},{33,162},{48,35},{49,163},... | collective-permute-start | bytes 393224 | tf_op jit(solution)/shard_map/ppermute | solution.py:86
  18.4 1.9 collective-permute-start.19
  20.4 1.4 collective-permute-done.18
  21.8 2.8 collective-permute-done.16
  24.6 2.8 collective-permute-done.19
  27.5 2.8 collective-permute-start.20
  31.6 14.3 %collective-permute-start.9 = (f32[2,256,256]{2,1,0:T(8,128)}, f32[2,256,256]{2,1,0:T(8,128)}, u32[]{:S(2)}, u32[]{:S(2)}) collective-permute-start(f32[2,256,256]{2,1,0:T(8,128)} %slice_bitcast_fusion.9), channel_id=1, source_target_pairs={{0,8},{1,9},{16,24},{17,25},{32,40},{33,41},{48,56},{49,57},{64,72... | collective-permute-start | bytes 1572872 | tf_op jit(solution)/shard_map/ppermute | solution.py:61
  47.4 1.9 collective-permute-start.21
  49.4 3.9 %collective-permute-start.22 = (f32[64,256]{1,0:T(8,128)}, f32[64,256]{1,0:T(8,128)}, u32[]{:S(2)}, u32[]{:S(2)}) collective-permute-start(f32[64,256]{1,0:T(8,128)} %get-tuple-element.66), channel_id=1, source_target_pairs={{0,96},{16,112},{32,0},{48,16},{64,32},{80,48},{96,64},{112,80},{1... | collective-permute-start | bytes 196616 | tf_op jit(solution)/shard_map/ppermute | solution.py:92
  53.3 1.9 collective-permute-start.23
  55.3 1.7 conditional.1
  57.0 155.3 %all-to-all-start = ((f32[32,24,256]{2,1,0:T(8,128)}), f32[32,24,256]{2,1,0:T(8,128)S(1)}, u32[]{:S(2)}, u32[]{:S(2)}) async-start(f32[32,24,256]{2,1,0:T(8,128)} %bitcast.22), calls=%async_computation | async-start | bytes 1572864 | tf_op jit(solution)/shard_map/all_to_all | solution.py:51
  212.2 1.5 bitcast_dynamic-update-slice_fusion.4
  216.5 1.5 bitcast_dynamic-update-slice_fusion.3
  218.0 1.5 bitcast_dynamic-update-slice_fusion.2
  219.4 4.7 %collective-permute-start.26 = (f32[256,256]{1,0:T(8,128)}, f32[256,256]{1,0:T(8,128)}, u32[]{:S(2)}, u32[]{:S(2)}) collective-permute-start(f32[256,256]{1,0:T(8,128)} %bitcast.44), channel_id=1, source_target_pairs={{0,384},{16,400},{32,416},{48,432},{64,448},{80,464},{96,480},{112... | collective-permute-start | bytes 786440 | tf_op jit(solution)/shard_map/ppermute | solution.py:95
  224.2 2.7 collective-permute-start.25
  226.9 2.8 collective-permute-start.24
  231.3 2.0 collective-permute-start.12
  233.3 2.0 collective-permute-start.13
  238.6 3.0 %collective-permute-done.24 = f32[256,256]{1,0:T(8,128)} collective-permute-done((f32[256,256]{1,0:T(8,128)}, f32[256,256]{1,0:T(8,128)}, u32[]{:S(2)}, u32[]{:S(2)}) %collective-permute-start.24) | collective-permute-done | bytes 262176 | tf_op jit(solution)/shard_map/ppermute | solution.py:95
  244.2 1.9 collective-permute-start.27
  250.8 1.9 maximum_select_fusion.1
  253.7 5.3 %all-to-all-start.1 = ((f32[32,24,256]{2,1,0:T(8,128)}), f32[32,24,256]{2,1,0:T(8,128)}, u32[]{:S(2)}, u32[]{:S(2)}) async-start(f32[32,24,256]{2,1,0:T(8,128)} %broadcast_in_dim.35), calls=%async_computation.1 | async-start | bytes 1572864 | tf_op jit(solution)/shard_map/all_to_all | solution.py:56
  259.0 1.9 slice_bitcast_fusion.11
  260.9 3.7 %collective-permute-start.14 = (f32[256,256]{1,0:T(8,128)}, f32[256,256]{1,0:T(8,128)}, u32[]{:S(2)}, u32[]{:S(2)}) collective-permute-start(f32[256,256]{1,0:T(8,128)} %get-tuple-element.93), channel_id=1, source_target_pairs={{0,1},{1,2},{2,3},{3,4},{4,5},{5,6},{6,7},{7,8},{8,9},{9,10},{10,1... | collective-permute-start | bytes 786440 | tf_op jit(solution)/shard_map/ppermute | solution.py:68
  264.6 3.4 %collective-permute-start.15 = (f32[256,256]{1,0:T(8,128)}, f32[256,256]{1,0:T(8,128)}, u32[]{:S(2)}, u32[]{:S(2)}) collective-permute-start(f32[256,256]{1,0:T(8,128)} %get-tuple-element.94), channel_id=1, source_target_pairs={{0,15},{1,0},{2,1},{3,2},{4,3},{5,4},{6,5},{7,6},{8,7},{9,8},{10,9... | collective-permute-start | bytes 786440 | tf_op jit(solution)/shard_map/ppermute | solution.py:69
  268.7 3.9 %collective-permute-done.14 = f32[256,256]{1,0:T(8,128)} collective-permute-done((f32[256,256]{1,0:T(8,128)}, f32[256,256]{1,0:T(8,128)}, u32[]{:S(2)}, u32[]{:S(2)}) %collective-permute-start.14) | collective-permute-done | bytes 262176 | tf_op jit(solution)/shard_map/ppermute | solution.py:68
  272.7 2.2 collective-permute-done.15
  274.9 2.6 fusion.26
  279.6 11.6 %shard_map.28 = f32[2,4,256,256]{3,2,1,0:T(8,128)} custom-call(s32[4]{0:T(128)S(1)} %pad_add_fusion.ids, s32[2,64]{1,0:T(2,128)S(1)} %copy-done.15, f32[768,256]{1,0:T(8,128)} %bitcast.24.diag, f32[256,256]{1,0:T(8,128)} %copy-done.8, f32[256,256]{1,0:T(8,128)S(1)} %collective-permute-done.8.low1, f32[2,256,256]{2,1,0:T(8,128)S(1)} %copy-done.2, ...), custom_call_target="tpu_custom_call" | custom-call | tf_op jit(solution)/shard_map/pallas_call | solution.py:187
  (78 shorter events, 26.7 us)
Async XLA Ops:
  0.0 55.3 %copy-start.15 = (s32[2,64]{1,0:T(2,128)S(1)}, s32[2,64]{1,0:T(2,128)}, u32[]{:S(2)}) copy-start(s32[2,64]{1,0:T(2,128)} %struct.1) | copy-start | bytes 1540
  3.2 17.2 %collective-permute-start.17 = (f32[2,64,256]{2,1,0:T(8,128)S(1)}, f32[2,64,256]{2,1,0:T(8,128)S(1)}, u32[]{:S(2)}, u32[]{:S(2)}) collective-permute-start(f32[2,64,256]{2,1,0:T(8,128)S(1)} %get-tuple-element.89), channel_id=1, source_target_pairs={{0,32},{1,160},{16,33},{17,161},{32,34},{33,162},{48,35},{49,163},... | collective-permute-start | bytes 393224 | tf_op jit(solution)/shard_map/ppermute | solution.py:86
  15.8 6.0 %collective-permute-start.18 = (f32[2,64,256]{2,1,0:T(8,128)S(1)}, f32[2,64,256]{2,1,0:T(8,128)S(1)}, u32[]{:S(2)}, u32[]{:S(2)}) collective-permute-start(f32[2,64,256]{2,1,0:T(8,128)S(1)} %get-tuple-element.90), channel_id=1, source_target_pairs={{0,64},{1,192},{16,65},{17,193},{32,66},{33,194},{48,67},{49,195},... | collective-permute-start | bytes 393224 | tf_op jit(solution)/shard_map/ppermute | solution.py:86
  17.1 7.5 %collective-permute-start.16 = (f32[2,64,256]{2,1,0:T(8,128)S(1)}, f32[2,64,256]{2,1,0:T(8,128)S(1)}, u32[]{:S(2)}, u32[]{:S(2)}) collective-permute-start(f32[2,64,256]{2,1,0:T(8,128)S(1)} %get-tuple-element.91), channel_id=1, source_target_pairs={{0,0},{1,128},{16,1},{17,129},{32,2},{33,130},{48,3},{49,131},{64,... | collective-permute-start | bytes 393224 | tf_op jit(solution)/shard_map/ppermute | solution.py:86
  18.4 9.0 %collective-permute-start.19 = (f32[2,64,256]{2,1,0:T(8,128)S(1)}, f32[2,64,256]{2,1,0:T(8,128)S(1)}, u32[]{:S(2)}, u32[]{:S(2)}) collective-permute-start(f32[2,64,256]{2,1,0:T(8,128)S(1)} %get-tuple-element.92), channel_id=1, source_target_pairs={{0,96},{1,224},{16,97},{17,225},{32,98},{33,226},{48,99},{49,227},... | collective-permute-start | bytes 393224 | tf_op jit(solution)/shard_map/ppermute | solution.py:86
  27.5 18.5 %collective-permute-start.20 = (f32[64,256]{1,0:T(8,128)S(1)}, f32[64,256]{1,0:T(8,128)S(1)}, u32[]{:S(2)}, u32[]{:S(2)}) collective-permute-start(f32[64,256]{1,0:T(8,128)S(1)} %slice_bitcast_fusion.17), channel_id=1, source_target_pairs={{0,16},{16,0},{32,48},{48,32},{64,80},{80,64},{96,112},{112,96},{1... | collective-permute-start | bytes 196616 | tf_op jit(solution)/shard_map/ppermute | solution.py:88
  30.3 23.0 %collective-permute-start.1 = (f32[256,256]{1,0:T(8,128)S(1)}, f32[256,256]{1,0:T(8,128)S(1)}, u32[]{:S(2)}, u32[]{:S(2)}) collective-permute-start(f32[256,256]{1,0:T(8,128)S(1)} %slice_bitcast_fusion.16), channel_id=1, source_target_pairs={{17,0}} | collective-permute-start | bytes 786440 | tf_op jit(solution)/shard_map/ppermute | solution.py:170
  31.0 24.3 %collective-permute-start = (f32[256,256]{1,0:T(8,128)S(1)}, f32[256,256]{1,0:T(8,128)S(1)}, u32[]{:S(2)}, u32[]{:S(2)}) collective-permute-start(f32[256,256]{1,0:T(8,128)S(1)} %slice_bitcast_fusion.16), channel_id=1, source_target_pairs={{16,0}} | collective-permute-start | bytes 786440 | tf_op jit(solution)/shard_map/ppermute | solution.py:169
  31.6 182.1 %collective-permute-start.9 = (f32[2,256,256]{2,1,0:T(8,128)}, f32[2,256,256]{2,1,0:T(8,128)}, u32[]{:S(2)}, u32[]{:S(2)}) collective-permute-start(f32[2,256,256]{2,1,0:T(8,128)} %slice_bitcast_fusion.9), channel_id=1, source_target_pairs={{0,8},{1,9},{16,24},{17,25},{32,40},{33,41},{48,56},{49,57},{64,72... | collective-permute-start | bytes 1572872 | tf_op jit(solution)/shard_map/ppermute | solution.py:61
  47.4 164.8 %collective-permute-start.21 = (f32[64,256]{1,0:T(8,128)}, f32[64,256]{1,0:T(8,128)}, u32[]{:S(2)}, u32[]{:S(2)}) collective-permute-start(f32[64,256]{1,0:T(8,128)} %get-tuple-element.66), channel_id=1, source_target_pairs={{0,32},{16,48},{32,64},{48,80},{64,96},{80,112},{96,0},{112,16},{1... | collective-permute-start | bytes 196616 | tf_op jit(solution)/shard_map/ppermute | solution.py:92
  49.4 167.1 %collective-permute-start.22 = (f32[64,256]{1,0:T(8,128)}, f32[64,256]{1,0:T(8,128)}, u32[]{:S(2)}, u32[]{:S(2)}) collective-permute-start(f32[64,256]{1,0:T(8,128)} %get-tuple-element.66), channel_id=1, source_target_pairs={{0,96},{16,112},{32,0},{48,16},{64,32},{80,48},{96,64},{112,80},{1... | collective-permute-start | bytes 196616 | tf_op jit(solution)/shard_map/ppermute | solution.py:92
  53.3 164.7 %collective-permute-start.23 = (f32[64,256]{1,0:T(8,128)}, f32[64,256]{1,0:T(8,128)}, u32[]{:S(2)}, u32[]{:S(2)}) collective-permute-start(f32[64,256]{1,0:T(8,128)} %get-tuple-element.66), channel_id=1, source_target_pairs={{0,64},{16,80},{32,96},{48,112},{64,0},{80,16},{96,32},{112,48},{1... | collective-permute-start | bytes 196616 | tf_op jit(solution)/shard_map/ppermute | solution.py:92
  57.0 156.9 %copy-start.8 = (f32[256,256]{1,0:T(8,128)}, f32[256,256]{1,0:T(8,128)S(1)}, u32[]{:S(2)}) copy-start(f32[256,256]{1,0:T(8,128)S(1)} %get-tuple-element.23.low0) | copy-start | bytes 786436
  57.0 178.4 %all-to-all-start = ((f32[32,24,256]{2,1,0:T(8,128)}), f32[32,24,256]{2,1,0:T(8,128)S(1)}, u32[]{:S(2)}, u32[]{:S(2)}) async-start(f32[32,24,256]{2,1,0:T(8,128)} %bitcast.22), calls=%async_computation | async-start | bytes 1572864 | tf_op jit(solution)/shard_map/all_to_all | solution.py:51
  213.9 15.8 %collective-permute-start.10 = (f32[256,256]{1,0:T(8,128)S(1)}, f32[256,256]{1,0:T(8,128)S(1)}, u32[]{:S(2)}, u32[]{:S(2)}) collective-permute-start(f32[256,256]{1,0:T(8,128)S(1)} %get-tuple-element.97), channel_id=1, source_target_pairs={{0,4},{1,5},{8,12},{9,13},{16,20},{17,21},{24,28},{25,29},{32,36},... | collective-permute-start | bytes 786440 | tf_op jit(solution)/shard_map/ppermute | solution.py:65
  215.2 14.5 %collective-permute-start.11 = (f32[256,256]{1,0:T(8,128)S(1)}, f32[256,256]{1,0:T(8,128)S(1)}, u32[]{:S(2)}, u32[]{:S(2)}) collective-permute-start(f32[256,256]{1,0:T(8,128)S(1)} %get-tuple-element.98), channel_id=1, source_target_pairs={{0,12},{1,13},{8,4},{9,5},{16,28},{17,29},{24,20},{25,21},{32,44},... | collective-permute-start | bytes 786440 | tf_op jit(solution)/shard_map/ppermute | solution.py:66
  219.4 16.5 %collective-permute-start.26 = (f32[256,256]{1,0:T(8,128)}, f32[256,256]{1,0:T(8,128)}, u32[]{:S(2)}, u32[]{:S(2)}) collective-permute-start(f32[256,256]{1,0:T(8,128)} %bitcast.44), channel_id=1, source_target_pairs={{0,384},{16,400},{32,416},{48,432},{64,448},{80,464},{96,480},{112... | collective-permute-start | bytes 786440 | tf_op jit(solution)/shard_map/ppermute | solution.py:95
  224.2 13.1 %collective-permute-start.25 = (f32[256,256]{1,0:T(8,128)}, f32[256,256]{1,0:T(8,128)}, u32[]{:S(2)}, u32[]{:S(2)}) collective-permute-start(f32[256,256]{1,0:T(8,128)} %bitcast.44), channel_id=1, source_target_pairs={{0,256},{16,272},{32,288},{48,304},{64,320},{80,336},{96,352},{112... | collective-permute-start | bytes 786440 | tf_op jit(solution)/shard_map/ppermute | solution.py:95
  226.9 14.7 %collective-permute-start.24 = (f32[256,256]{1,0:T(8,128)}, f32[256,256]{1,0:T(8,128)}, u32[]{:S(2)}, u32[]{:S(2)}) collective-permute-start(f32[256,256]{1,0:T(8,128)} %bitcast.44), channel_id=1, source_target_pairs={{0,128},{16,144},{32,160},{48,176},{64,192},{80,208},{96,224},{112... | collective-permute-start | bytes 786440 | tf_op jit(solution)/shard_map/ppermute | solution.py:95
  231.3 18.1 %collective-permute-start.12 = (f32[256,256]{1,0:T(8,128)}, f32[256,256]{1,0:T(8,128)}, u32[]{:S(2)}, u32[]{:S(2)}) collective-permute-start(f32[256,256]{1,0:T(8,128)} %get-tuple-element.95), channel_id=1, source_target_pairs={{0,2},{1,3},{4,6},{5,7},{8,10},{9,11},{12,14},{13,15},{16,18},{17,... | collective-permute-start | bytes 786440 | tf_op jit(solution)/shard_map/ppermute | solution.py:65
  233.3 17.4 %collective-permute-start.13 = (f32[256,256]{1,0:T(8,128)}, f32[256,256]{1,0:T(8,128)}, u32[]{:S(2)}, u32[]{:S(2)}) collective-permute-start(f32[256,256]{1,0:T(8,128)} %get-tuple-element.96), channel_id=1, source_target_pairs={{0,14},{1,15},{4,2},{5,3},{8,6},{9,7},{12,10},{13,11},{16,30},{17,... | collective-permute-start | bytes 786440 | tf_op jit(solution)/shard_map/ppermute | solution.py:66
  236.0 8.2 %collective-permute-start.3 = (f32[24,256]{1,0:T(8,128)S(1)}, f32[24,256]{1,0:T(8,128)S(1)}, u32[]{:S(2)}, u32[]{:S(2)}) collective-permute-start(f32[24,256]{1,0:T(8,128)S(1)} %fusion.29), channel_id=1, source_target_pairs={{0,12},{16,28},{32,44},{48,60},{64,76},{80,92},{96,108},{112,124},... | collective-permute-start | bytes 73736 | tf_op jit(solution)/shard_map/ppermute | solution.py:54
  237.3 8.8 %collective-permute-start.4 = (f32[24,256]{1,0:T(8,128)S(1)}, f32[24,256]{1,0:T(8,128)S(1)}, u32[]{:S(2)}, u32[]{:S(2)}) collective-permute-start(f32[24,256]{1,0:T(8,128)S(1)} %fusion.29), channel_id=1, source_target_pairs={{0,8},{16,24},{32,40},{48,56},{64,72},{80,88},{96,104},{112,120},{... | collective-permute-start | bytes 73736 | tf_op jit(solution)/shard_map/ppermute | solution.py:54
  241.6 4.5 %collective-permute-start.2 = (f32[24,256]{1,0:T(8,128)S(1)}, f32[24,256]{1,0:T(8,128)S(1)}, u32[]{:S(2)}, u32[]{:S(2)}) collective-permute-start(f32[24,256]{1,0:T(8,128)S(1)} %fusion.29), channel_id=1, source_target_pairs={{0,4},{16,20},{32,36},{48,52},{64,68},{80,84},{96,100},{112,116},{... | collective-permute-start | bytes 73736 | tf_op jit(solution)/shard_map/ppermute | solution.py:54
  244.2 33.3 %collective-permute-start.27 = (f32[4,256,256]{2,1,0:T(8,128)S(1)}, f32[4,256,256]{2,1,0:T(8,128)}, u32[]{:S(2)}, u32[]{:S(2)}) collective-permute-start(f32[4,256,256]{2,1,0:T(8,128)S(1)} %pad_maximum_fusion.own), channel_id=1, source_target_pairs={{0,16},{16,0},{32,48},{48,32},{64,80},{80,64},{96,112},{112,96},{1... | collective-permute-start | bytes 3145736 | tf_op jit(solution)/shard_map/ppermute | solution.py:97
  246.9 5.9 %collective-permute-start.7 = (f32[24,256]{1,0:T(8,128)S(1)}, f32[24,256]{1,0:T(8,128)S(1)}, u32[]{:S(2)}, u32[]{:S(2)}) collective-permute-start(f32[24,256]{1,0:T(8,128)S(1)} %add_add_fusion.2), channel_id=1, source_target_pairs={{0,2},{4,6},{8,10},{12,14},{16,18},{20,22},{24,26},{28,30},{32,34}... | collective-permute-start | bytes 73736 | tf_op jit(solution)/shard_map/ppermute | solution.py:54
  248.2 4.6 %collective-permute-start.6 = (f32[24,256]{1,0:T(8,128)S(1)}, f32[24,256]{1,0:T(8,128)S(1)}, u32[]{:S(2)}, u32[]{:S(2)}) collective-permute-start(f32[24,256]{1,0:T(8,128)S(1)} %add_add_fusion.2), channel_id=1, source_target_pairs={{0,15},{4,3},{8,7},{12,11},{16,31},{20,19},{24,23},{28,27},{32,47}... | collective-permute-start | bytes 73736 | tf_op jit(solution)/shard_map/ppermute | solution.py:54
  249.5 3.3 %collective-permute-start.5 = (f32[24,256]{1,0:T(8,128)S(1)}, f32[24,256]{1,0:T(8,128)S(1)}, u32[]{:S(2)}, u32[]{:S(2)}) collective-permute-start(f32[24,256]{1,0:T(8,128)S(1)} %add_add_fusion.2), channel_id=1, source_target_pairs={{0,1},{4,5},{8,9},{12,13},{16,17},{20,21},{24,25},{28,29},{32,33},... | collective-permute-start | bytes 73736 | tf_op jit(solution)/shard_map/ppermute | solution.py:54
  253.7 23.8 %all-to-all-start.1 = ((f32[32,24,256]{2,1,0:T(8,128)}), f32[32,24,256]{2,1,0:T(8,128)}, u32[]{:S(2)}, u32[]{:S(2)}) async-start(f32[32,24,256]{2,1,0:T(8,128)} %broadcast_in_dim.35), calls=%async_computation.1 | async-start | bytes 1572864 | tf_op jit(solution)/shard_map/all_to_all | solution.py:56
  260.9 11.8 %collective-permute-start.14 = (f32[256,256]{1,0:T(8,128)}, f32[256,256]{1,0:T(8,128)}, u32[]{:S(2)}, u32[]{:S(2)}) collective-permute-start(f32[256,256]{1,0:T(8,128)} %get-tuple-element.93), channel_id=1, source_target_pairs={{0,1},{1,2},{2,3},{3,4},{4,5},{5,6},{6,7},{7,8},{8,9},{9,10},{10,1... | collective-permute-start | bytes 786440 | tf_op jit(solution)/shard_map/ppermute | solution.py:68
  264.6 10.3 %collective-permute-start.15 = (f32[256,256]{1,0:T(8,128)}, f32[256,256]{1,0:T(8,128)}, u32[]{:S(2)}, u32[]{:S(2)}) collective-permute-start(f32[256,256]{1,0:T(8,128)} %get-tuple-element.94), channel_id=1, source_target_pairs={{0,15},{1,0},{2,1},{3,2},{4,3},{5,4},{6,5},{7,6},{8,7},{9,8},{10,9... | collective-permute-start | bytes 786440 | tf_op jit(solution)/shard_map/ppermute | solution.py:69
  268.0 9.5 %collective-permute-start.8 = (f32[256,256]{1,0:T(8,128)}, f32[256,256]{1,0:T(8,128)S(1)}, u32[]{:S(2)}, u32[]{:S(2)}) collective-permute-start(f32[256,256]{1,0:T(8,128)} %get-tuple-element.24), channel_id=1, source_target_pairs={{0,17}} | collective-permute-start | bytes 786440 | tf_op jit(solution)/shard_map/ppermute | solution.py:180
  (9 other events, 108.6 us)

commit v2 on v0

v2 whole, which is shorter than its diff:
```python
import jax
import jax.numpy as jnp
from jax import lax
from jax.experimental import pallas as pl
from jax.experimental.pallas import tpu as pltpu
from jax.sharding import PartitionSpec as P

ROWS = ((1,), (0,))
BOTH = ((1,), (1,))
NX, NY = 4, 4


def row_of(x, y, core):
    return (y % NY) * 2 * NX + (x % NX) * 2 + core


def parts(a):
    high = a.astype(jnp.bfloat16)
    return high, (a - high.astype(jnp.float32)).astype(jnp.bfloat16)


def mul_parts(a, b, dims):
    def one(x, y):
        return lax.dot_general(x, y, (dims, ((), ())), preferred_element_type=jnp.float32)

    return one(a[0], b[0]) + (one(a[0], b[1]) + one(a[1], b[0]))


def mul(a, b, dims):
    return mul_parts(parts(a), parts(b), dims)


def iotas(n):
    return lax.broadcasted_iota(jnp.int32, (n, n), 0), lax.broadcasted_iota(jnp.int32, (n, n), 1)


def inverse_factor(sym, inv):
    n = sym.shape[0]
    ri, ci = iotas(n)
    eye = jnp.where(ri == ci, 1.0, 0.0)
    half = jnp.where(ri > ci, 1.0, jnp.where(ri == ci, 0.5, 0.0))
    diag = jnp.where(ri == ci, sym, 0.0)
    scale_col = lax.rsqrt(jnp.sum(diag, axis=1, keepdims=True))
    scale_row = lax.rsqrt(jnp.sum(diag, axis=0, keepdims=True))
    unit = sym * scale_col * scale_row

    def residual(t):
        return mul(mul(t, unit, ROWS), t, BOTH) - eye

    def improve(carry):
        t, err, _, count = carry
        x = err * half
        t = mul((eye - x) + mul(x, x, ROWS), t, ROWS)
        err = residual(t)
        return t, err, jnp.sum(err * err), count + 1

    x = (unit - eye) * half
    t = (eye - x) + mul(x, x, ROWS)
    err = residual(t)
    start = (t, err, jnp.sum(err * err), jnp.int32(0))
    t, err, size, _ = lax.while_loop(lambda c: (c[2] > 1e-4) & (c[3] < 8), improve, start)
    x = err * half
    near = parts(x)
    x = x - mul_parts(near, near, BOTH) * half
    t = mul((eye - x) + mul_parts(near, near, ROWS), t, ROWS)
    inv[...] = t * scale_row

    @pl.when(jnp.logical_not(size <= 1e-4))
    def _():
        def pivot(k, carry):
            left, right = carry
            row_left = jnp.sum(jnp.where(ri == k, left, 0.0), axis=0, keepdims=True)
            row_right = jnp.sum(jnp.where(ri == k, right, 0.0), axis=0, keepdims=True)
            col = jnp.sum(jnp.where((ci == k) & (ri > k), left, 0.0), axis=1, keepdims=True)
            pick = lax.broadcasted_iota(jnp.int32, (1, n), 1) == k
            col = col / jnp.sum(jnp.where(pick, row_left, 0.0), axis=1, keepdims=True)
            return left - col * row_left, right - col * row_right

        left, right = lax.fori_loop(0, n, pivot, (sym, eye))
        pivots = jnp.sum(jnp.where(ri == ci, left, 0.0), axis=1, keepdims=True)
        inv[...] = right * lax.rsqrt(pivots)


def symmetric(block):
    ri, ci = iotas(block.shape[0])
    return jnp.where(ri >= ci, block, block.T)


def solve(a0, a1, keep0, keep1, inv0, p10, inv1):
    p0 = mul_parts(parts(a0), inv0, BOTH) * keep0
    rest = a1 - mul_parts(parts(p0), p10, BOTH)
    return p0, mul_parts(parts(rest), inv1, BOTH) * keep1


def head_kernel(ids, struct, raw, own, other, inv, low, high, rest, tmp):
    row, col, core = ids[0], ids[1], ids[3]
    n = raw.shape[-1]
    ri, ci = iotas(n)
    s0 = symmetric(raw[:, 0:8, :].reshape(n, n))
    inverse_factor(s0, tmp)
    t0 = tmp[...]
    inv0 = parts(t0)
    a10 = raw[:, 8:16, :].reshape(n, n)
    p10 = mul_parts(parts(a10), inv0, BOTH) * struct[0, 1].astype(jnp.float32)
    half10 = parts(p10)
    s1 = symmetric(raw[:, 16:24, :].reshape(n, n) - mul_parts(half10, half10, BOTH))
    inverse_factor(s1, tmp)
    inv1 = parts(tmp[...])
    for k, pair in enumerate((inv0, half10, inv1)):
        inv[k, 0] = pair[0]
        inv[k, 1] = pair[1]

    @pl.when((row == 0) & (col == 0))
    def _():
        low[...] = jnp.where(ri >= ci, mul_parts(parts(s0), inv0, BOTH), 0.0)

    @pl.when((row == 1) & (col == 1))
    def _():
        low[...] = jnp.where(ri >= ci, mul_parts(parts(s1), inv1, BOTH), 0.0)

    for q in range(4):
        mine = core == q // 2
        slot = 2 * (q % 2)
        a0 = jnp.where(mine, own[slot], other[slot])
        a1 = jnp.where(mine, own[slot + 1], other[slot + 1])
        glob = q * 16 + col
        keep0 = struct[0, glob].astype(jnp.float32)
        keep1 = struct[1, glob].astype(jnp.float32)
        both = solve(a0, a1, keep0, keep1, inv0, half10, inv1)
        for k in range(2):
            top, bottom = parts(both[k])
            high[q, :, k * n:(k + 1) * n] = top
            rest[q, :, k * n:(k + 1) * n] = bottom


def tail_kernel(ids, struct, inv, low, high, rest, rows0, rows1, mat, out, row_high, row_rest):
    row, col = ids[0], ids[1]
    n = mat.shape[-1]
    inv0, p10, inv1 = ((inv[k, 0], inv[k, 1]) for k in range(3))
    for p in range(2):
        i = p * 32 + row
        keep0 = struct[0, i].astype(jnp.float32)
        keep1 = struct[1, i].astype(jnp.float32)
        both = solve(rows0[p], rows1[p], keep0, keep1, inv0, p10, inv1)
        for k in range(2):
            top, bottom = parts(both[k])
            row_high[:, k * n:(k + 1) * n] = top
            row_rest[:, k * n:(k + 1) * n] = bottom
        for q in range(4):
            j = q * 16 + col

            @pl.when(i < j)
            def _():
                out[p, q] = mat[p, q]

            @pl.when(i >= j)
            def _():
                left = (row_high[...], row_rest[...])
                out[p, q] = mat[p, q] - mul_parts(left, (high[q], rest[q]), BOTH)

        @pl.when((col == 0) & (i > 0))
        def _():
            out[p, 0] = both[0]

        @pl.when((col == 1) & (i > 1))
        def _():
            out[p, 0] = both[1]

        if p == 0:
            @pl.when((col < 2) & (row == col))
            def _():
                out[p, 0] = low[...]


def spread_diagonal(first, col_id):
    nrow = lax.axis_size("row")
    ncol = lax.axis_size("col")
    width = first.shape[-1]
    part = lax.all_to_all(first.reshape(nrow, width // nrow, width), "row", 0, 0)[0:2]
    got = [lax.ppermute(part, "col", [(s, s + d) for s in (0, 1)]) for d in (4, 12, 8)]
    part = jnp.where(col_id < 2, part, got[0] + got[1] + got[2])
    sources = [s for s in range(ncol) if s % 4 < 2]
    two_up = lax.ppermute(part, "col", [(s, s + 2) for s in sources])
    mixed = lax.ppermute(part, "col", [(s, (s - 1) % ncol if s % 4 == 0 else s + 1) for s in sources])
    one_up = lax.ppermute(part, "col", [(s, s + 1) for s in sources if s % 4 == 0])
    one_down = lax.ppermute(part[1], "col", [(s, s - 1) for s in sources if s % 4 == 1])
    place = lax.rem(col_id, 4)
    left = jnp.where(place == 0, part, jnp.where(place == 1, one_up, jnp.where(place == 2, two_up, mixed)))
    right = jnp.where(place == 0, one_down, jnp.where(place == 1, part[1], jnp.where(place == 2, mixed[1], two_up[1])))
    part = jnp.concatenate([left[0], left[1], right])
    return lax.all_to_all(jnp.broadcast_to(part[None], (nrow,) + part.shape), "row", 0, 0)


def spread_rows(mine, col_id, ncol):
    far = lax.ppermute(mine, "col", [(0, 8), (1, 9)])
    have = jnp.where(col_id < 2, mine, far)
    for step in (4, 2):
        sources = [s for s in range(ncol) if s % (2 * step) < 2]
        up = lax.ppermute(have[0], "col", [(s, (s + step) % ncol) for s in sources])
        down = lax.ppermute(have[1], "col", [(s, (s - step) % ncol) for s in sources])
        have = jnp.where(lax.rem(col_id, 2 * step) < 2, have, jnp.stack([up, down]))
    up = lax.ppermute(have[0], "col", [(s, (s + 1) % ncol) for s in range(ncol)])
    down = lax.ppermute(have[1], "col", [(s, (s - 1) % ncol) for s in range(ncol)])
    near = jnp.stack([up, down])
    even = lax.rem(col_id, 2) == 0
    return jnp.where(even, have, near), jnp.where(even, near, have)


def spread_columns(mine, row_id, nrow, ncol):
    width = mine.shape[-1]
    core = lax.rem(row_id, 2)
    quarter = width // 4
    part = 0.0
    for k in range(4):
        pairs = []
        for row in range(nrow):
            for column in (0, 1):
                target = row_of(k, column + 2 * (row // ncol), 0)
                pairs.append((row * ncol + column, target * ncol + row % ncol))
        part = part + lax.ppermute(mine[:, k * quarter:(k + 1) * quarter], ("row", "col"), pairs)
    swap = [(row, row ^ 1) for row in range(nrow)]
    piece = jnp.where(core == 0, part[0], lax.ppermute(part[1], "row", swap))
    groups = [list(range(c, nrow, 2)) for c in range(2)]
    own = jnp.broadcast_to(piece[None], (nrow // 2, quarter, width))
    own = lax.all_to_all(own, "row", 0, 0, axis_index_groups=groups).reshape(4, width, width)
    return own, lax.ppermute(own, "row", swap)


def on_device(matrix, structure):
    lbr = matrix.shape[0]
    lbc = matrix.shape[2]
    width = matrix.shape[4]
    blocks = matrix.reshape(lbr, lbc, width, width)
    nrow = lax.axis_size("row")
    ncol = lax.axis_size("col")
    row_id = lax.axis_index("row")
    col_id = lax.axis_index("col")
    mine = blocks[:, 0]

    raw = spread_diagonal(mine[0], col_id)
    own, other = spread_columns(mine, row_id, nrow, ncol)
    rows0, rows1 = spread_rows(mine, col_id, ncol)

    ids = jnp.stack([row_id, col_id, row_id // 2, lax.rem(row_id, 2)]).astype(jnp.int32)
    vmem = pl.BlockSpec(memory_space=pltpu.VMEM)
    smem = pl.BlockSpec(memory_space=pltpu.SMEM)
    params = pltpu.CompilerParams(vmem_limit_bytes=40 * 2**20)
    inv, low, high, rest = pl.pallas_call(
        head_kernel,
        out_shape=[
            jax.ShapeDtypeStruct((3, 2, width, width), jnp.bfloat16),
            jax.ShapeDtypeStruct((width, width), jnp.float32),
            jax.ShapeDtypeStruct((lbc, width, 2 * width), jnp.bfloat16),
            jax.ShapeDtypeStruct((lbc, width, 2 * width), jnp.bfloat16),
        ],
        in_specs=[smem] * 2 + [vmem] * 3,
        out_specs=[vmem] * 4,
        scratch_shapes=[pltpu.VMEM((width, width), jnp.float32)],
        compiler_params=params,
    )(ids, structure, raw, own, other)
    result = pl.pallas_call(
        tail_kernel,
        out_shape=jax.ShapeDtypeStruct(blocks.shape, jnp.float32),
        in_specs=[smem] * 2 + [vmem] * 7,
        out_specs=vmem,
        scratch_shapes=[pltpu.VMEM((width, 2 * width), jnp.bfloat16)] * 2,
        compiler_params=params,
    )(ids, structure, inv, low, high, rest, rows0, rows1, blocks)
    return result.reshape(matrix.shape)


def solution(mesh):
    in_specs = (P(None, "row", None, "col", None, None), P())
    out_specs = P(None, "row", None, "col", None, None)
    return jax.shard_map(
        on_device, mesh=mesh, in_specs=in_specs, out_specs=out_specs, check_vma=False
    )
```

time: 983 us -> 146 us (0.15)
  the two profiles are of different devices: /device:TPU:6 before, /device:TPU:18 now
where the time goes in v2:
time: 146 us; the launch traced here: 145 us
  starting transfers between devices  97.4 us (67%)
  waiting for transfers between devices  18.2 us (12%)
  Pallas kernels  17.2 us (12%)
  local copies, waits for them, and re-layouts  7.62 us (5%)
  other arithmetic  4.19 us (3%)
    all_to_all x1, starting transfers between devices, spread_diagonal(): lax.all_to_all(first.reshape(nrow, width // nrow, width), 'row', 0, 0)[0:2]  17.3 us
    ppermute x2, starting transfers between devices, spread_rows(): lax.ppermute(have[1], 'col', [(s, (s - step) % ncol) for s in sources])  11.4 us
    ppermute x4, starting transfers between devices, spread_columns(): lax.ppermute(mine[:, k * quarter:(k + 1) * quarter], ('row', 'col'), pairs)  11.3 us
    pallas_call x1, Pallas kernels, on_device(): pl.pallas_call(head_kernel, out_shape=[jax.ShapeDtypeStruct((3, 2, width,...  11.2 us
    ppermute x1, starting transfers between devices, spread_rows(): far = lax.ppermute(mine, 'col', [(0, 8), (1, 9)])  10.4 us
    ppermute x1, starting transfers between devices, spread_rows(): lax.ppermute(have[1], 'col', [(s, (s - 1) % ncol) for s in range(ncol)])  9.64 us
    ppermute x2, waiting for transfers between devices, spread_rows(): lax.ppermute(have[1], 'col', [(s, (s - step) % ncol) for s in sources])  9.07 us
    ppermute x3, starting transfers between devices, spread_diagonal(): lax.ppermute(part, 'col', [(s, s + d) for s in (0, 1)])  8.87 us
  transfers between devices with their start and end apart: 23, of which 4 were waited for; matrix products, arithmetic and copies ran while one was open for 6% of the time, Pallas kernels for 0%

profile of v2, /device:TPU:18, one launch (start us, length us, event | category | flops | bytes accessed | tf_op | source)
XLA Modules:
  0.0 145.1 jit_solution(16263301786636378118)
XLA Ops:
  0.0 2.0 %slice_bitcast_fusion = f32[2,256,256]{2,1,0:T(8,128)} fusion(f32[2,4,256,256]{3,2,1,0:T(8,128)} %bitcast.53), kind=kLoop, calls=%fused_computation | loop fusion | bytes 1048576 | tf_op jit(solution)/shard_map/squeeze | solution.py:238
  3.2 6.7 %collective-permute-start.10 = (f32[2,64,256]{2,1,0:T(8,128)S(1)}, f32[2,64,256]{2,1,0:T(8,128)S(1)}, u32[]{:S(2)}, u32[]{:S(2)}) collective-permute-start(f32[2,64,256]{2,1,0:T(8,128)S(1)} %get-tuple-element.22), channel_id=1, source_target_pairs={{0,96},{1,224},{16,97},{17,225},{32,98},{33,226},{48,99},{49,227},... | collective-permute-start | bytes 393224 | tf_op jit(solution)/shard_map/ppermute | solution.py:220
  9.9 1.3 collective-permute-start.9
  11.2 1.3 collective-permute-start.7
  12.5 1.9 %collective-permute-start.8 = (f32[2,64,256]{2,1,0:T(8,128)S(1)}, f32[2,64,256]{2,1,0:T(8,128)S(1)}, u32[]{:S(2)}, u32[]{:S(2)}) collective-permute-start(f32[2,64,256]{2,1,0:T(8,128)S(1)} %get-tuple-element.21), channel_id=1, source_target_pairs={{0,32},{1,160},{16,33},{17,161},{32,34},{33,162},{48,35},{49,163},... | collective-permute-start | bytes 393224 | tf_op jit(solution)/shard_map/ppermute | solution.py:220
  15.2 17.3 %all-to-all-start = ((f32[32,8,256]{2,1,0:T(8,128)}), f32[32,8,256]{2,1,0:T(8,128)S(1)}, u32[]{:S(2)}, u32[]{:S(2)}) async-start(f32[32,8,256]{2,1,0:T(8,128)} %slice_bitcast_fusion.7), calls=%async_computation | async-start | bytes 524288 | tf_op jit(solution)/shard_map/all_to_all | solution.py:179
  32.6 2.1 %collective-permute-start.11 = (f32[64,256]{1,0:T(8,128)S(1)}, f32[64,256]{1,0:T(8,128)S(1)}, u32[]{:S(2)}, u32[]{:S(2)}) collective-permute-start(f32[64,256]{1,0:T(8,128)S(1)} %slice_bitcast_fusion.8), channel_id=1, source_target_pairs={{0,16},{16,0},{32,48},{48,32},{64,80},{80,64},{96,112},{112,96},{1... | collective-permute-start | bytes 196616 | tf_op jit(solution)/shard_map/ppermute | solution.py:222
  34.6 10.4 %collective-permute-start.13 = (f32[2,256,256]{2,1,0:T(8,128)}, f32[2,256,256]{2,1,0:T(8,128)}, u32[]{:S(2)}, u32[]{:S(2)}) collective-permute-start(f32[2,256,256]{2,1,0:T(8,128)} %slice_bitcast_fusion), channel_id=1, source_target_pairs={{0,8},{1,9},{16,24},{17,25},{32,40},{33,41},{48,56},{49,57},{64,72... | collective-permute-start | bytes 1572872 | tf_op jit(solution)/shard_map/ppermute | solution.py:195
  45.1 1.3 collective-permute-start.2
  46.4 1.3 collective-permute-start
  47.7 6.3 %collective-permute-start.1 = (f32[2,8,256]{2,1,0:T(8,128)S(1)}, f32[2,8,256]{2,1,0:T(8,128)S(1)}, u32[]{:S(2)}, u32[]{:S(2)}) collective-permute-start(f32[2,8,256]{2,1,0:T(8,128)S(1)} %slice.84), channel_id=1, source_target_pairs={{0,12},{1,13},{16,28},{17,29},{32,44},{33,45},{48,60},{49,61},{64,... | collective-permute-start | bytes 49160 | tf_op jit(solution)/shard_map/ppermute | solution.py:180
  55.1 5.7 %all-to-all-start.2 = ((f32[16,64,256]{2,1,0:T(8,128)}), f32[16,64,256]{2,1,0:T(8,128)S(1)}, u32[]{:S(2)}, u32[]{:S(2)}) async-start(f32[16,64,256]{2,1,0:T(8,128)} %broadcast_in_dim.5), calls=%async_computation.2 | async-start | bytes 2097152 | tf_op jit(solution)/shard_map/all_to_all | solution.py:225
  60.8 1.3 collective-permute-done.1
  62.1 1.3 collective-permute-start.4
  63.4 1.3 collective-permute-start.5
  64.7 2.1 %collective-permute-start.3 = (f32[2,8,256]{2,1,0:T(8,128)S(1)}, f32[2,8,256]{2,1,0:T(8,128)S(1)}, u32[]{:S(2)}, u32[]{:S(2)}) collective-permute-start(f32[2,8,256]{2,1,0:T(8,128)S(1)} %add_select_fusion), channel_id=1, source_target_pairs={{0,1},{4,5},{8,9},{12,13},{16,17},{20,21},{24,25},{28,29},{32,33},... | collective-permute-start | bytes 49160 | tf_op jit(solution)/shard_map/ppermute | solution.py:185
  66.8 1.3 collective-permute-start.6
  68.3 9.4 %collective-permute-start.15 = (f32[256,256]{1,0:T(8,128)S(1)}, f32[256,256]{1,0:T(8,128)S(1)}, u32[]{:S(2)}, u32[]{:S(2)}) collective-permute-start(f32[256,256]{1,0:T(8,128)S(1)} %get-tuple-element.20), channel_id=1, source_target_pairs={{0,12},{1,13},{8,4},{9,5},{16,28},{17,29},{24,20},{25,21},{32,44},... | collective-permute-start | bytes 786440 | tf_op jit(solution)/shard_map/ppermute | solution.py:200
  77.7 1.3 collective-permute-start.14
  79.1 9.1 %collective-permute-done.15 = f32[256,256]{1,0:T(8,128)S(1)} collective-permute-done((f32[256,256]{1,0:T(8,128)S(1)}, f32[256,256]{1,0:T(8,128)S(1)}, u32[]{:S(2)}, u32[]{:S(2)}) %collective-permute-start.15) | collective-permute-done | bytes 262176 | tf_op jit(solution)/shard_map/ppermute | solution.py:200
  89.1 2.0 %collective-permute-start.17 = (f32[256,256]{1,0:T(8,128)}, f32[256,256]{1,0:T(8,128)}, u32[]{:S(2)}, u32[]{:S(2)}) collective-permute-start(f32[256,256]{1,0:T(8,128)} %get-tuple-element.18), channel_id=1, source_target_pairs={{0,14},{1,15},{4,2},{5,3},{8,6},{9,7},{12,10},{13,11},{16,30},{17,... | collective-permute-start | bytes 786440 | tf_op jit(solution)/shard_map/ppermute | solution.py:200
  91.1 2.0 %collective-permute-start.16 = (f32[256,256]{1,0:T(8,128)}, f32[256,256]{1,0:T(8,128)}, u32[]{:S(2)}, u32[]{:S(2)}) collective-permute-start(f32[256,256]{1,0:T(8,128)} %get-tuple-element.17), channel_id=1, source_target_pairs={{0,2},{1,3},{4,6},{5,7},{8,10},{9,11},{12,14},{13,15},{16,18},{17,... | collective-permute-start | bytes 786440 | tf_op jit(solution)/shard_map/ppermute | solution.py:199
  93.1 1.9 %collective-permute-start.12 = (f32[4,256,256]{2,1,0:T(8,128)S(1)}, f32[4,256,256]{2,1,0:T(8,128)}, u32[]{:S(2)}, u32[]{:S(2)}) collective-permute-start(f32[4,256,256]{2,1,0:T(8,128)S(1)} %bitcast.57), channel_id=1, source_target_pairs={{0,16},{16,0},{32,48},{48,32},{64,80},{80,64},{96,112},{112,96},{1... | collective-permute-start | bytes 3145736 | tf_op jit(solution)/shard_map/ppermute | solution.py:226
  95.9 6.0 %all-to-all-start.1 = ((f32[32,24,256]{2,1,0:T(8,128)}), f32[32,24,256]{2,1,0:T(8,128)}, u32[]{:S(2)}, u32[]{:S(2)}) async-start(f32[32,24,256]{2,1,0:T(8,128)} %broadcast_in_dim.4), calls=%async_computation.1 | async-start | bytes 1572864 | tf_op jit(solution)/shard_map/all_to_all | solution.py:191
  102.0 1.4 maximum_select_fusion.1
  104.2 9.6 %collective-permute-start.19 = (f32[256,256]{1,0:T(8,128)}, f32[256,256]{1,0:T(8,128)}, u32[]{:S(2)}, u32[]{:S(2)}) collective-permute-start(f32[256,256]{1,0:T(8,128)} %get-tuple-element.16), channel_id=1, source_target_pairs={{0,15},{1,0},{2,1},{3,2},{4,3},{5,4},{6,5},{7,6},{8,7},{9,8},{10,9... | collective-permute-start | bytes 786440 | tf_op jit(solution)/shard_map/ppermute | solution.py:203
  113.9 3.5 %collective-permute-start.18 = (f32[256,256]{1,0:T(8,128)}, f32[256,256]{1,0:T(8,128)}, u32[]{:S(2)}, u32[]{:S(2)}) collective-permute-start(f32[256,256]{1,0:T(8,128)} %get-tuple-element.15), channel_id=1, source_target_pairs={{0,1},{1,2},{2,3},{3,4},{4,5},{5,6},{6,7},{7,8},{8,9},{9,10},{10,1... | collective-permute-start | bytes 786440 | tf_op jit(solution)/shard_map/ppermute | solution.py:202
  117.4 4.9 %collective-permute-done.19 = f32[256,256]{1,0:T(8,128)} collective-permute-done((f32[256,256]{1,0:T(8,128)}, f32[256,256]{1,0:T(8,128)}, u32[]{:S(2)}, u32[]{:S(2)}) %collective-permute-start.19) | collective-permute-done | bytes 262176 | tf_op jit(solution)/shard_map/ppermute | solution.py:203
  122.3 2.9 %collective-permute-done.18 = f32[256,256]{1,0:T(8,128)} collective-permute-done((f32[256,256]{1,0:T(8,128)}, f32[256,256]{1,0:T(8,128)}, u32[]{:S(2)}, u32[]{:S(2)}) %collective-permute-start.18) | collective-permute-done | bytes 262176 | tf_op jit(solution)/shard_map/ppermute | solution.py:202
  125.3 2.5 %fusion = (f32[2,256,256]{2,1,0:T(8,128)}, f32[2,256,256]{2,1,0:T(8,128)}) fusion(f32[1,256,256]{2,1,0:T(8,128)} %bitcast.25, f32[1,256,256]{2,1,0:T(8,128)} %bitcast.23, pred[]{:T(512)S(6)} %eq.22, f32[1,256,256]{2,1,0:T(8,128)} %bitcast.21, f32[1,256,256]{2,1,0:T(8,128)} %bitcast.19, pred[]{:T(512)S(6)} %lt.11, f32[2,256,256]{2,1,0:T(8,128)} %copy-done.4, ...), kind=kLoop, calls=%fused_computation.4 | loop fusion | flops 917504 | bytes 3145731 | tf_op jit(solution)/shard_map/jit(_where)/select_n | solution.py:206
  127.8 11.2 %shard_map.28 = (bf16[3,2,256,256]{3,2,1,0:T(8,128)(2,1)S(1)}, f32[256,256]{1,0:T(8,128)S(1)}, bf16[4,256,512]{2,1,0:T(8,128)(2,1)S(1)}, bf16[4,256,512]{2,1,0:T(8,128)(2,1)S(1)}) custom-call(s32[4]{0:T(128)S(1)} %pad_add_fusion.ids, s32[2,64]{1,0:T(2,128)S(1)} %copy-done.3, f32[32,24,256]{2,1,0:T(8,128)} %all-to-all-done.1.raw, ...), custom_call_target="tpu_custom_call" | custom-call | tf_op jit(solution)/shard_map/pallas_call | solution.py:248
  139.0 6.1 %shard_map.29 = f32[2,4,256,256]{3,2,1,0:T(8,128)} custom-call(s32[4]{0:T(128)S(1)} %pad_add_fusion.ids, s32[2,64]{1,0:T(2,128)S(1)} %copy-done.3, bf16[3,2,256,256]{3,2,1,0:T(8,128)(2,1)S(1)} %get-tuple-element.9.inv, f32[256,256]{1,0:T(8,128)S(1)} %get-tuple-element.10.low, bf16[4,256,512]{2,1,0:T(8,128)(2,1)S(1)} %get-tuple-element.11.high, ...), custom_call_target="tpu_custom_call" | custom-call | tf_op jit(solution)/shard_map/pallas_call | solution.py:261
  (51 shorter events, 5.9 us)
Async XLA Ops:
  0.0 14.4 %copy-start = (f32[2,1,4,1,256,256]{5,4,3,2,1,0:T(8,128)S(1)}, f32[2,1,4,1,256,256]{5,4,3,2,1,0:T(8,128)}, u32[]{:S(2)}) copy-start(f32[2,1,4,1,256,256]{5,4,3,2,1,0:T(8,128)} %param.2) | copy-start | bytes 6291460
  3.2 29.3 %collective-permute-start.10 = (f32[2,64,256]{2,1,0:T(8,128)S(1)}, f32[2,64,256]{2,1,0:T(8,128)S(1)}, u32[]{:S(2)}, u32[]{:S(2)}) collective-permute-start(f32[2,64,256]{2,1,0:T(8,128)S(1)} %get-tuple-element.22), channel_id=1, source_target_pairs={{0,96},{1,224},{16,97},{17,225},{32,98},{33,226},{48,99},{49,227},... | collective-permute-start | bytes 393224 | tf_op jit(solution)/shard_map/ppermute | solution.py:220
  9.9 22.6 %collective-permute-start.9 = (f32[2,64,256]{2,1,0:T(8,128)S(1)}, f32[2,64,256]{2,1,0:T(8,128)S(1)}, u32[]{:S(2)}, u32[]{:S(2)}) collective-permute-start(f32[2,64,256]{2,1,0:T(8,128)S(1)} %get-tuple-element.23), channel_id=1, source_target_pairs={{0,64},{1,192},{16,65},{17,193},{32,66},{33,194},{48,67},{49,195},... | collective-permute-start | bytes 393224 | tf_op jit(solution)/shard_map/ppermute | solution.py:220
  11.2 21.3 %collective-permute-start.7 = (f32[2,64,256]{2,1,0:T(8,128)S(1)}, f32[2,64,256]{2,1,0:T(8,128)S(1)}, u32[]{:S(2)}, u32[]{:S(2)}) collective-permute-start(f32[2,64,256]{2,1,0:T(8,128)S(1)} %get-tuple-element.24), channel_id=1, source_target_pairs={{0,0},{1,128},{16,1},{17,129},{32,2},{33,130},{48,3},{49,131},{64,... | collective-permute-start | bytes 393224 | tf_op jit(solution)/shard_map/ppermute | solution.py:220
  12.5 20.0 %collective-permute-start.8 = (f32[2,64,256]{2,1,0:T(8,128)S(1)}, f32[2,64,256]{2,1,0:T(8,128)S(1)}, u32[]{:S(2)}, u32[]{:S(2)}) collective-permute-start(f32[2,64,256]{2,1,0:T(8,128)S(1)} %get-tuple-element.21), channel_id=1, source_target_pairs={{0,32},{1,160},{16,33},{17,161},{32,34},{33,162},{48,35},{49,163},... | collective-permute-start | bytes 393224 | tf_op jit(solution)/shard_map/ppermute | solution.py:220
  15.2 29.9 %all-to-all-start = ((f32[32,8,256]{2,1,0:T(8,128)}), f32[32,8,256]{2,1,0:T(8,128)S(1)}, u32[]{:S(2)}, u32[]{:S(2)}) async-start(f32[32,8,256]{2,1,0:T(8,128)} %slice_bitcast_fusion.7), calls=%async_computation | async-start | bytes 524288 | tf_op jit(solution)/shard_map/all_to_all | solution.py:179
  32.6 21.4 %collective-permute-start.11 = (f32[64,256]{1,0:T(8,128)S(1)}, f32[64,256]{1,0:T(8,128)S(1)}, u32[]{:S(2)}, u32[]{:S(2)}) collective-permute-start(f32[64,256]{1,0:T(8,128)S(1)} %slice_bitcast_fusion.8), channel_id=1, source_target_pairs={{0,16},{16,0},{32,48},{48,32},{64,80},{80,64},{96,112},{112,96},{1... | collective-permute-start | bytes 196616 | tf_op jit(solution)/shard_map/ppermute | solution.py:222
  34.6 33.5 %collective-permute-start.13 = (f32[2,256,256]{2,1,0:T(8,128)}, f32[2,256,256]{2,1,0:T(8,128)}, u32[]{:S(2)}, u32[]{:S(2)}) collective-permute-start(f32[2,256,256]{2,1,0:T(8,128)} %slice_bitcast_fusion), channel_id=1, source_target_pairs={{0,8},{1,9},{16,24},{17,25},{32,40},{33,41},{48,56},{49,57},{64,72... | collective-permute-start | bytes 1572872 | tf_op jit(solution)/shard_map/ppermute | solution.py:195
  45.1 15.7 %collective-permute-start.2 = (f32[2,8,256]{2,1,0:T(8,128)S(1)}, f32[2,8,256]{2,1,0:T(8,128)S(1)}, u32[]{:S(2)}, u32[]{:S(2)}) collective-permute-start(f32[2,8,256]{2,1,0:T(8,128)S(1)} %slice.84), channel_id=1, source_target_pairs={{0,8},{1,9},{16,24},{17,25},{32,40},{33,41},{48,56},{49,57},{64,72... | collective-permute-start | bytes 49160 | tf_op jit(solution)/shard_map/ppermute | solution.py:180
  46.4 14.4 %collective-permute-start = (f32[2,8,256]{2,1,0:T(8,128)S(1)}, f32[2,8,256]{2,1,0:T(8,128)S(1)}, u32[]{:S(2)}, u32[]{:S(2)}) collective-permute-start(f32[2,8,256]{2,1,0:T(8,128)S(1)} %slice.84), channel_id=1, source_target_pairs={{0,4},{1,5},{16,20},{17,21},{32,36},{33,37},{48,52},{49,53},{64,68... | collective-permute-start | bytes 49160 | tf_op jit(solution)/shard_map/ppermute | solution.py:180
  47.7 14.4 %collective-permute-start.1 = (f32[2,8,256]{2,1,0:T(8,128)S(1)}, f32[2,8,256]{2,1,0:T(8,128)S(1)}, u32[]{:S(2)}, u32[]{:S(2)}) collective-permute-start(f32[2,8,256]{2,1,0:T(8,128)S(1)} %slice.84), channel_id=1, source_target_pairs={{0,12},{1,13},{16,28},{17,29},{32,44},{33,45},{48,60},{49,61},{64,... | collective-permute-start | bytes 49160 | tf_op jit(solution)/shard_map/ppermute | solution.py:180
  55.1 38.0 %all-to-all-start.2 = ((f32[16,64,256]{2,1,0:T(8,128)}), f32[16,64,256]{2,1,0:T(8,128)S(1)}, u32[]{:S(2)}, u32[]{:S(2)}) async-start(f32[16,64,256]{2,1,0:T(8,128)} %broadcast_in_dim.5), calls=%async_computation.2 | async-start | bytes 2097152 | tf_op jit(solution)/shard_map/all_to_all | solution.py:225
  62.1 16.9 %collective-permute-start.4 = (f32[2,8,256]{2,1,0:T(8,128)S(1)}, f32[2,8,256]{2,1,0:T(8,128)S(1)}, u32[]{:S(2)}, u32[]{:S(2)}) collective-permute-start(f32[2,8,256]{2,1,0:T(8,128)S(1)} %add_select_fusion), channel_id=1, source_target_pairs={{0,2},{1,3},{4,6},{5,7},{8,10},{9,11},{12,14},{13,15},{16,18},{17,... | collective-permute-start | bytes 49160 | tf_op jit(solution)/shard_map/ppermute | solution.py:183
  63.4 15.6 %collective-permute-start.5 = (f32[2,8,256]{2,1,0:T(8,128)S(1)}, f32[2,8,256]{2,1,0:T(8,128)S(1)}, u32[]{:S(2)}, u32[]{:S(2)}) collective-permute-start(f32[2,8,256]{2,1,0:T(8,128)S(1)} %add_select_fusion), channel_id=1, source_target_pairs={{0,15},{1,2},{4,3},{5,6},{8,7},{9,10},{12,11},{13,14},{16,31},{17,... | collective-permute-start | bytes 49160 | tf_op jit(solution)/shard_map/ppermute | solution.py:184
  64.7 14.4 %collective-permute-start.3 = (f32[2,8,256]{2,1,0:T(8,128)S(1)}, f32[2,8,256]{2,1,0:T(8,128)S(1)}, u32[]{:S(2)}, u32[]{:S(2)}) collective-permute-start(f32[2,8,256]{2,1,0:T(8,128)S(1)} %add_select_fusion), channel_id=1, source_target_pairs={{0,1},{4,5},{8,9},{12,13},{16,17},{20,21},{24,25},{28,29},{32,33},... | collective-permute-start | bytes 49160 | tf_op jit(solution)/shard_map/ppermute | solution.py:185
  66.8 10.9 %collective-permute-start.6 = (f32[8,256]{1,0:T(8,128)S(1)}, f32[8,256]{1,0:T(8,128)S(1)}, u32[]{:S(2)}, u32[]{:S(2)}) collective-permute-start(f32[8,256]{1,0:T(8,128)S(1)} %slice_bitcast_fusion.10), channel_id=1, source_target_pairs={{1,0},{5,4},{9,8},{13,12},{17,16},{21,20},{25,24},{29,28},{33,32},... | collective-permute-start | bytes 24584 | tf_op jit(solution)/shard_map/ppermute | solution.py:186
  68.2 24.8 %copy-start.4 = (f32[2,256,256]{2,1,0:T(8,128)}, f32[2,256,256]{2,1,0:T(8,128)S(1)}, u32[]{:S(2)}) copy-start(f32[2,256,256]{2,1,0:T(8,128)S(1)} %broadcast_select_fusion) | copy-start | bytes 1572868
  68.3 19.9 %collective-permute-start.15 = (f32[256,256]{1,0:T(8,128)S(1)}, f32[256,256]{1,0:T(8,128)S(1)}, u32[]{:S(2)}, u32[]{:S(2)}) collective-permute-start(f32[256,256]{1,0:T(8,128)S(1)} %get-tuple-element.20), channel_id=1, source_target_pairs={{0,12},{1,13},{8,4},{9,5},{16,28},{17,29},{24,20},{25,21},{32,44},... | collective-permute-start | bytes 786440 | tf_op jit(solution)/shard_map/ppermute | solution.py:200
  77.7 10.5 %collective-permute-start.14 = (f32[256,256]{1,0:T(8,128)S(1)}, f32[256,256]{1,0:T(8,128)S(1)}, u32[]{:S(2)}, u32[]{:S(2)}) collective-permute-start(f32[256,256]{1,0:T(8,128)S(1)} %get-tuple-element.19), channel_id=1, source_target_pairs={{0,4},{1,5},{8,12},{9,13},{16,20},{17,21},{24,28},{25,29},{32,36},... | collective-permute-start | bytes 786440 | tf_op jit(solution)/shard_map/ppermute | solution.py:199
  88.1 4.9 %copy-start.5 = (f32[256,256]{1,0:T(8,128)}, f32[256,256]{1,0:T(8,128)S(1)}, u32[]{:S(2)}) copy-start(f32[256,256]{1,0:T(8,128)S(1)} %collective-permute-done.14) | copy-start | bytes 786436
  89.1 12.9 %collective-permute-start.17 = (f32[256,256]{1,0:T(8,128)}, f32[256,256]{1,0:T(8,128)}, u32[]{:S(2)}, u32[]{:S(2)}) collective-permute-start(f32[256,256]{1,0:T(8,128)} %get-tuple-element.18), channel_id=1, source_target_pairs={{0,14},{1,15},{4,2},{5,3},{8,6},{9,7},{12,10},{13,11},{16,30},{17,... | collective-permute-start | bytes 786440 | tf_op jit(solution)/shard_map/ppermute | solution.py:200
  91.1 10.9 %collective-permute-start.16 = (f32[256,256]{1,0:T(8,128)}, f32[256,256]{1,0:T(8,128)}, u32[]{:S(2)}, u32[]{:S(2)}) collective-permute-start(f32[256,256]{1,0:T(8,128)} %get-tuple-element.17), channel_id=1, source_target_pairs={{0,2},{1,3},{4,6},{5,7},{8,10},{9,11},{12,14},{13,15},{16,18},{17,... | collective-permute-start | bytes 786440 | tf_op jit(solution)/shard_map/ppermute | solution.py:199
  93.1 34.7 %collective-permute-start.12 = (f32[4,256,256]{2,1,0:T(8,128)S(1)}, f32[4,256,256]{2,1,0:T(8,128)}, u32[]{:S(2)}, u32[]{:S(2)}) collective-permute-start(f32[4,256,256]{2,1,0:T(8,128)S(1)} %bitcast.57), channel_id=1, source_target_pairs={{0,16},{16,0},{32,48},{48,32},{64,80},{80,64},{96,112},{112,96},{1... | collective-permute-start | bytes 3145736 | tf_op jit(solution)/shard_map/ppermute | solution.py:226
  95.9 31.9 %all-to-all-start.1 = ((f32[32,24,256]{2,1,0:T(8,128)}), f32[32,24,256]{2,1,0:T(8,128)}, u32[]{:S(2)}, u32[]{:S(2)}) async-start(f32[32,24,256]{2,1,0:T(8,128)} %broadcast_in_dim.4), calls=%async_computation.1 | async-start | bytes 1572864 | tf_op jit(solution)/shard_map/all_to_all | solution.py:191
  103.4 24.4 %copy-start.3 = (s32[2,64]{1,0:T(2,128)S(1)}, s32[2,64]{1,0:T(2,128)}, u32[]{:S(2)}) copy-start(s32[2,64]{1,0:T(2,128)} %struct.3) | copy-start | bytes 1540
  104.2 18.1 %collective-permute-start.19 = (f32[256,256]{1,0:T(8,128)}, f32[256,256]{1,0:T(8,128)}, u32[]{:S(2)}, u32[]{:S(2)}) collective-permute-start(f32[256,256]{1,0:T(8,128)} %get-tuple-element.16), channel_id=1, source_target_pairs={{0,15},{1,0},{2,1},{3,2},{4,3},{5,4},{6,5},{7,6},{8,7},{9,8},{10,9... | collective-permute-start | bytes 786440 | tf_op jit(solution)/shard_map/ppermute | solution.py:203
  113.9 11.4 %collective-permute-start.18 = (f32[256,256]{1,0:T(8,128)}, f32[256,256]{1,0:T(8,128)}, u32[]{:S(2)}, u32[]{:S(2)}) collective-permute-start(f32[256,256]{1,0:T(8,128)} %get-tuple-element.15), channel_id=1, source_target_pairs={{0,1},{1,2},{2,3},{3,4},{4,5},{5,6},{6,7},{7,8},{8,9},{9,10},{10,1... | collective-permute-start | bytes 786440 | tf_op jit(solution)/shard_map/ppermute | solution.py:202
  127.8 11.2 %copy-start.1 = (f32[2,256,256]{2,1,0:T(8,128)S(1)}, f32[2,256,256]{2,1,0:T(8,128)}, u32[]{:S(2)}) copy-start(f32[2,256,256]{2,1,0:T(8,128)} %get-tuple-element.13.rows1) | copy-start | bytes 1572868
  127.8 11.2 %copy-start.2 = (f32[2,256,256]{2,1,0:T(8,128)S(1)}, f32[2,256,256]{2,1,0:T(8,128)}, u32[]{:S(2)}) copy-start(f32[2,256,256]{2,1,0:T(8,128)} %get-tuple-element.14.rows0) | copy-start | bytes 1572868

commit v3 on v2

--- a/solution.py
+++ b/solution.py
@@ -93,7 +93,7 @@
 
 
 def head_kernel(ids, struct, raw, own, other, inv, low, high, rest, tmp):
-    row, col, core = ids[0], ids[1], ids[3]
+    row, col, core = ids[0], ids[1], ids[2]
     n = raw.shape[-1]
     ri, ci = iotas(n)
     s0 = symmetric(raw[:, 0:8, :].reshape(n, n))
@@ -133,15 +133,18 @@
             rest[q, :, k * n:(k + 1) * n] = bottom
 
 
-def tail_kernel(ids, struct, inv, low, high, rest, rows0, rows1, mat, out, row_high, row_rest):
+def tail_kernel(ids, struct, inv, low, high, rest, have0, have1, near0, near1, mat, out, row_high, row_rest):
     row, col = ids[0], ids[1]
+    even = lax.rem(col, 2) == 0
     n = mat.shape[-1]
     inv0, p10, inv1 = ((inv[k, 0], inv[k, 1]) for k in range(3))
-    for p in range(2):
+    for p, (have, near) in enumerate(((have0, near0), (have1, near1))):
         i = p * 32 + row
+        a0 = jnp.where(even, have[...], near[...])
+        a1 = jnp.where(even, near[...], have[...])
         keep0 = struct[0, i].astype(jnp.float32)
         keep1 = struct[1, i].astype(jnp.float32)
-        both = solve(rows0[p], rows1[p], keep0, keep1, inv0, p10, inv1)
+        both = solve(a0, a1, keep0, keep1, inv0, p10, inv1)
         for k in range(2):
             top, bottom = parts(both[k])
             row_high[:, k * n:(k + 1) * n] = top
@@ -172,58 +175,8 @@
                 out[p, 0] = low[...]
 
 
-def spread_diagonal(first, col_id):
-    nrow = lax.axis_size("row")
-    ncol = lax.axis_size("col")
-    width = first.shape[-1]
-    part = lax.all_to_all(first.reshape(nrow, width // nrow, width), "row", 0, 0)[0:2]
-    got = [lax.ppermute(part, "col", [(s, s + d) for s in (0, 1)]) for d in (4, 12, 8)]
-    part = jnp.where(col_id < 2, part, got[0] + got[1] + got[2])
-    sources = [s for s in range(ncol) if s % 4 < 2]
-    two_up = lax.ppermute(part, "col", [(s, s + 2) for s in sources])
-    mixed = lax.ppermute(part, "col", [(s, (s - 1) % ncol if s % 4 == 0 else s + 1) for s in sources])
-    one_up = lax.ppermute(part, "col", [(s, s + 1) for s in sources if s % 4 == 0])
-    one_down = lax.ppermute(part[1], "col", [(s, s - 1) for s in sources if s % 4 == 1])
-    place = lax.rem(col_id, 4)
-    left = jnp.where(place == 0, part, jnp.where(place == 1, one_up, jnp.where(place == 2, two_up, mixed)))
-    right = jnp.where(place == 0, one_down, jnp.where(place == 1, part[1], jnp.where(place == 2, mixed[1], two_up[1])))
-    part = jnp.concatenate([left[0], left[1], right])
-    return lax.all_to_all(jnp.broadcast_to(part[None], (nrow,) + part.shape), "row", 0, 0)
-
-
-def spread_rows(mine, col_id, ncol):
-    far = lax.ppermute(mine, "col", [(0, 8), (1, 9)])
-    have = jnp.where(col_id < 2, mine, far)
-    for step in (4, 2):
-        sources = [s for s in range(ncol) if s % (2 * step) < 2]
-        up = lax.ppermute(have[0], "col", [(s, (s + step) % ncol) for s in sources])
-        down = lax.ppermute(have[1], "col", [(s, (s - step) % ncol) for s in sources])
-        have = jnp.where(lax.rem(col_id, 2 * step) < 2, have, jnp.stack([up, down]))
-    up = lax.ppermute(have[0], "col", [(s, (s + 1) % ncol) for s in range(ncol)])
-    down = lax.ppermute(have[1], "col", [(s, (s - 1) % ncol) for s in range(ncol)])
-    near = jnp.stack([up, down])
-    even = lax.rem(col_id, 2) == 0
-    return jnp.where(even, have, near), jnp.where(even, near, have)
-
-
-def spread_columns(mine, row_id, nrow, ncol):
-    width = mine.shape[-1]
-    core = lax.rem(row_id, 2)
-    quarter = width // 4
-    part = 0.0
-    for k in range(4):
-        pairs = []
-        for row in range(nrow):
-            for column in (0, 1):
-                target = row_of(k, column + 2 * (row // ncol), 0)
-                pairs.append((row * ncol + column, target * ncol + row % ncol))
-        part = part + lax.ppermute(mine[:, k * quarter:(k + 1) * quarter], ("row", "col"), pairs)
-    swap = [(row, row ^ 1) for row in range(nrow)]
-    piece = jnp.where(core == 0, part[0], lax.ppermute(part[1], "row", swap))
-    groups = [list(range(c, nrow, 2)) for c in range(2)]
-    own = jnp.broadcast_to(piece[None], (nrow // 2, quarter, width))
-    own = lax.all_to_all(own, "row", 0, 0, axis_index_groups=groups).reshape(4, width, width)
-    return own, lax.ppermute(own, "row", swap)
+def after(a, *values):
+    return lax.optimization_barrier((a,) + values)[0]
 
 
 def on_device(matrix, structure):
@@ -235,13 +188,63 @@
     ncol = lax.axis_size("col")
     row_id = lax.axis_index("row")
     col_id = lax.axis_index("col")
-    mine = blocks[:, 0]
-
-    raw = spread_diagonal(mine[0], col_id)
-    own, other = spread_columns(mine, row_id, nrow, ncol)
-    rows0, rows1 = spread_rows(mine, col_id, ncol)
-
-    ids = jnp.stack([row_id, col_id, row_id // 2, lax.rem(row_id, 2)]).astype(jnp.int32)
+    quarter = width // 4
+    swap = [(row, row ^ 1) for row in range(nrow)]
+    mine = [blocks[p, 0] for p in range(lbr)]
+
+    def scatter(block):
+        return lax.all_to_all(block.reshape(nrow, width // nrow, width), "row", 0, 0)[0:2]
+
+    diag = scatter(mine[0])
+    both = jnp.stack([a for a in mine])
+    part = 0.0
+    for k in range(4):
+        pairs = []
+        for row in range(nrow):
+            for column in (0, 1):
+                target = row_of(k, column + 2 * (row // ncol), 0)
+                pairs.append((row * ncol + column, target * ncol + row % ncol))
+        part = part + lax.ppermute(both[:, k * quarter:(k + 1) * quarter], ("row", "col"), pairs)
+
+    def spread(have, step):
+        return [lax.ppermute(a, "col", sorted(((s + c) % ncol, (t + c) % ncol) for s, t in pairs for c in (0, 1)))
+                for a, pairs in zip(have, (step, [(-s, -t) for s, t in step]))]
+
+    def merged(have, near, step):
+        def took(pairs):
+            return sum((((col_id - t) % ncol) < 2) for _, t in pairs) > 0
+        return [jnp.where(took(pairs), b, a) for a, b, pairs in zip(have, near, (step, [(-s, -t) for s, t in step]))]
+
+    steps = [[(0, 6)], [(0, 2), (6, 10)], [(2, 4), (6, 8), (10, 12), (0, 14)]]
+    far = spread([a for a in mine], steps[0])
+    piece = jnp.where(lax.rem(row_id, 2) == 0, part[0], lax.ppermute(part[1], "row", swap))
+    got = [lax.ppermute(diag, "col", [(s, s + d) for s in (0, 1)]) for d in (4, 12, 8)]
+    diag = jnp.where(col_id < 2, diag, got[0] + got[1] + got[2])
+    sources = [s for s in range(ncol) if s % 4 < 2]
+    two_up = lax.ppermute(diag, "col", [(s, s + 2) for s in sources])
+    mixed = lax.ppermute(diag, "col", [(s, (s - 1) % ncol if s % 4 == 0 else s + 1) for s in sources])
+    one_up = lax.ppermute(diag, "col", [(s, s + 1) for s in sources if s % 4 == 0])
+    one_down = lax.ppermute(diag[1], "col", [(s, s - 1) for s in sources if s % 4 == 1])
+    place = lax.rem(col_id, 4)
+    left = jnp.where(place == 0, diag, jnp.where(place == 1, one_up, jnp.where(place == 2, two_up, mixed)))
+    right = jnp.where(place == 0, one_down, jnp.where(place == 1, diag[1], jnp.where(place == 2, mixed[1], two_up[1])))
+    diag = jnp.concatenate([left[0], left[1], right])
+
+    have = merged(mine, far, steps[0])
+    near = spread(have, steps[1])
+    have = merged(have, near, steps[1])
+    last = spread(have, steps[2])
+    have = merged(have, last, steps[2])
+    rows = have + [lax.ppermute(a, "col", [(s, (s + d) % ncol) for s in range(ncol)]) for a, d in zip(have, (1, -1))]
+    own = jnp.broadcast_to(piece[None], (nrow // 2,) + piece.shape)
+    groups = [list(range(c, nrow, 2)) for c in range(2)]
+    own = lax.all_to_all(own, "row", 0, 0, axis_index_groups=groups).reshape(4, width, width)
+    other = lax.ppermute(own, "row", swap)
+    raw = jnp.broadcast_to(diag[None], (nrow,) + diag.shape)
+    raw = lax.all_to_all(raw, "row", 0, 0)
+    own = own
+
+    ids = jnp.stack([row_id, col_id, lax.rem(row_id, 2)]).astype(jnp.int32)
     vmem = pl.BlockSpec(memory_space=pltpu.VMEM)
     smem = pl.BlockSpec(memory_space=pltpu.SMEM)
     params = pltpu.CompilerParams(vmem_limit_bytes=40 * 2**20)
@@ -257,15 +260,17 @@
         out_specs=[vmem] * 4,
         scratch_shapes=[pltpu.VMEM((width, width), jnp.float32)],
         compiler_params=params,
+        cost_estimate=pl.CostEstimate(flops=10000000000, bytes_accessed=2**22, transcendentals=0),
     )(ids, structure, raw, own, other)
     result = pl.pallas_call(
         tail_kernel,
         out_shape=jax.ShapeDtypeStruct(blocks.shape, jnp.float32),
-        in_specs=[smem] * 2 + [vmem] * 7,
+        in_specs=[smem] * 2 + [vmem] * 9,
         out_specs=vmem,
         scratch_shapes=[pltpu.VMEM((width, 2 * width), jnp.bfloat16)] * 2,
         compiler_params=params,
-    )(ids, structure, inv, low, high, rest, rows0, rows1, blocks)
+        cost_estimate=pl.CostEstimate(flops=3 * 10**9, bytes_accessed=2**23, transcendentals=0),
+    )(ids, structure, inv, low, high, rest, *rows, blocks)
     return result.reshape(matrix.shape)
 
 

time: 146 us -> 135 us (0.925)
  the two profiles are of different devices: /device:TPU:18 before, /device:TPU:182 now
where the time goes in v3:
time: 135 us; the launch traced here: 134 us
  starting transfers between devices  75.8 us (56%)
  waiting for transfers between devices  32.3 us (24%)
  Pallas kernels  16.7 us (12%)
  other arithmetic  5.01 us (4%)
  local copies, waits for them, and re-layouts  3.88 us (3%)
    all_to_all x1, starting transfers between devices, on_device(): lax.all_to_all(own, 'row', 0, 0, axis_index_groups=groups)  24.9 us
    ppermute x6, waiting for transfers between devices, spread(): lax.ppermute(a, 'col', sorted((((s + c) % ncol, (t + c) % ncol) for s, t...  14 us
    all_to_all x1, starting transfers between devices, on_device(): raw = lax.all_to_all(raw, 'row', 0, 0)  13.5 us
    ppermute x3, waiting for transfers between devices, on_device(): lax.ppermute(diag, 'col', [(s, s + d) for s in (0, 1)])  11.2 us
    pallas_call x1, Pallas kernels, on_device(): pl.pallas_call(head_kernel, out_shape=[jax.ShapeDtypeStruct((3, 2, width,...  10.2 us
    ppermute x2, starting transfers between devices, on_device(): lax.ppermute(a, 'col', [(s, (s + d) % ncol) for s in range(ncol)])  8.23 us
    all_to_all x1, starting transfers between devices, scatter(): lax.all_to_all(block.reshape(nrow, width // nrow, width), 'row', 0, 0)[0:2]  7.38 us
    ppermute x6, starting transfers between devices, spread(): lax.ppermute(a, 'col', sorted((((s + c) % ncol, (t + c) % ncol) for s, t...  6.65 us
  transfers between devices with their start and end apart: 24, of which 4 were waited for; matrix products, arithmetic and copies ran while one was open for 5% of the time, Pallas kernels for 8%

profile of v3, /device:TPU:182, one launch (start us, length us, event | category | flops | bytes accessed | tf_op | source)
XLA Modules:
  0.0 134.3 jit_solution(12645809392227753454)
XLA Ops:
  0.0 1.8 %slice_bitcast_fusion = (f32[256,256]{1,0:T(8,128)S(1)}, f32[1,256,256]{2,1,0:T(8,128)S(1)}, f32[256,256]{1,0:T(8,128)S(1)}, f32[1,256,256]{2,1,0:T(8,128)S(1)}, f32[32,8,256]{2,1,0:T(8,128)}) fusion(f32[2,4,256,256]{3,2,1,0:T(8,128)} %bitcast.44), kind=kLoop, calls=%fused_computation.6 | loop fusion | bytes 1835008 | tf_op jit(solution)/shard_map/squeeze | solution.py:193
  1.9 1.3 collective-permute-start.10
  5.2 7.4 %all-to-all-start = ((f32[32,8,256]{2,1,0:T(8,128)}), f32[32,8,256]{2,1,0:T(8,128)S(1)}, u32[]{:S(2)}, u32[]{:S(2)}) async-start(f32[32,8,256]{2,1,0:T(8,128)} %get-tuple-element.19), calls=%async_computation | async-start | bytes 524288 | tf_op jit(solution)/shard_map/all_to_all | solution.py:196
  12.6 2.7 %collective-permute-done.10 = f32[2,64,256]{2,1,0:T(8,128)S(1)} collective-permute-done((f32[2,64,256]{2,1,0:T(8,128)S(1)}, f32[2,64,256]{2,1,0:T(8,128)S(1)}, u32[]{:S(2)}, u32[]{:S(2)}) %collective-permute-start.10) | collective-permute-done | bytes 131104 | tf_op jit(solution)/shard_map/ppermute | solution.py:207
  15.4 1.9 %collective-permute-start.11 = (f32[64,256]{1,0:T(8,128)S(1)}, f32[64,256]{1,0:T(8,128)S(1)}, u32[]{:S(2)}, u32[]{:S(2)}) collective-permute-start(f32[64,256]{1,0:T(8,128)S(1)} %slice_bitcast_fusion.5), channel_id=1, source_target_pairs={{0,16},{16,0},{32,48},{48,32},{64,80},{80,64},{96,112},{112,96},{1... | collective-permute-start | bytes 196616 | tf_op jit(solution)/shard_map/ppermute | solution.py:220
  17.4 0.7 collective-permute-start.16
  19.5 1.3 collective-permute-start
  21.5 1.1 broadcast_in_dim.5
  22.6 24.9 %all-to-all-start.2 = ((f32[16,64,256]{2,1,0:T(8,128)}), f32[16,64,256]{2,1,0:T(8,128)S(1)}, u32[]{:S(2)}, u32[]{:S(2)}) async-start(f32[16,64,256]{2,1,0:T(8,128)} %broadcast_in_dim.5), calls=%async_computation.2 | async-start | bytes 2097152 | tf_op jit(solution)/shard_map/all_to_all | solution.py:241
  47.6 11.2 %collective-permute-done = f32[2,8,256]{2,1,0:T(8,128)S(1)} collective-permute-done((f32[2,8,256]{2,1,0:T(8,128)S(1)}, f32[2,8,256]{2,1,0:T(8,128)S(1)}, u32[]{:S(2)}, u32[]{:S(2)}) %collective-permute-start) | collective-permute-done | bytes 16416 | tf_op jit(solution)/shard_map/ppermute | solution.py:221
  58.8 1.3 collective-permute-start.4
  60.1 1.3 collective-permute-start.5
  61.4 1.3 collective-permute-start.6
  62.7 1.1 broadcast_select_fusion
  63.8 1.4 %collective-permute-start.14 = (f32[256,256]{1,0:T(8,128)S(1)}, f32[256,256]{1,0:T(8,128)}, u32[]{:S(2)}, u32[]{:S(2)}) collective-permute-start(f32[256,256]{1,0:T(8,128)S(1)} %get-tuple-element.14), channel_id=1, source_target_pairs={{0,2},{1,3},{6,10},{7,11},{16,18},{17,19},{22,26},{23,27},{32,34},... | collective-permute-start | bytes 786440 | tf_op jit(solution)/shard_map/ppermute | solution.py:210
  65.2 1.4 %collective-permute-start.17 = (f32[256,256]{1,0:T(8,128)S(1)}, f32[256,256]{1,0:T(8,128)}, u32[]{:S(2)}, u32[]{:S(2)}) collective-permute-start(f32[256,256]{1,0:T(8,128)S(1)} %get-tuple-element.13), channel_id=1, source_target_pairs={{0,14},{1,15},{10,6},{11,7},{16,30},{17,31},{26,22},{27,23},{32,46... | collective-permute-start | bytes 786440 | tf_op jit(solution)/shard_map/ppermute | solution.py:210
  66.5 1.3 collective-permute-start.3
  67.9 4.3 %collective-permute-done.3 = f32[2,8,256]{2,1,0:T(8,128)S(1)} collective-permute-done((f32[2,8,256]{2,1,0:T(8,128)S(1)}, f32[2,8,256]{2,1,0:T(8,128)S(1)}, u32[]{:S(2)}, u32[]{:S(2)}) %collective-permute-start.3) | collective-permute-done | bytes 16416 | tf_op jit(solution)/shard_map/ppermute | solution.py:226
  72.2 0.9 broadcast_in_dim.4
  73.1 13.5 %all-to-all-start.1 = ((f32[32,24,256]{2,1,0:T(8,128)}), f32[32,24,256]{2,1,0:T(8,128)S(1)}, u32[]{:S(2)}, u32[]{:S(2)}) async-start(f32[32,24,256]{2,1,0:T(8,128)} %broadcast_in_dim.4), calls=%async_computation.1 | async-start | bytes 1572864 | tf_op jit(solution)/shard_map/all_to_all | solution.py:244
  86.7 2.1 %collective-permute-start.12 = (f32[4,256,256]{2,1,0:T(8,128)S(1)}, f32[4,256,256]{2,1,0:T(8,128)S(1)}, u32[]{:S(2)}, u32[]{:S(2)}) collective-permute-start(f32[4,256,256]{2,1,0:T(8,128)S(1)} %bitcast.42), channel_id=1, source_target_pairs={{0,16},{16,0},{32,48},{48,32},{64,80},{80,64},{96,112},{112,96},{1... | collective-permute-start | bytes 3145736 | tf_op jit(solution)/shard_map/ppermute | solution.py:242
  88.7 1.0 broadcast_select_fusion.4
  89.7 1.3 collective-permute-start.15
  91.1 0.7 broadcast_select_fusion.1
  91.8 1.3 collective-permute-start.18
  93.2 14.0 %collective-permute-done.15 = f32[256,256]{1,0:T(8,128)} collective-permute-done((f32[256,256]{1,0:T(8,128)S(1)}, f32[256,256]{1,0:T(8,128)}, u32[]{:S(2)}, u32[]{:S(2)}) %collective-permute-start.15) | collective-permute-done | bytes 262176 | tf_op jit(solution)/shard_map/ppermute | solution.py:210
  107.2 1.0 broadcast_select_fusion.5.have0
  108.2 1.9 %collective-permute-start.19 = (f32[256,256]{1,0:T(8,128)S(1)}, f32[256,256]{1,0:T(8,128)}, u32[]{:S(2)}, u32[]{:S(2)}) collective-permute-start(f32[256,256]{1,0:T(8,128)S(1)} %broadcast_select_fusion.5.have0), channel_id=1, source_target_pairs={{0,1},{1,2},{2,3},{3,4},{4,5},{5,6},{6,7},{7,8},{8,9},{9,10},{10,1... | collective-permute-start | bytes 786440 | tf_op jit(solution)/shard_map/ppermute | solution.py:238
  110.1 1.0 broadcast_select_fusion.2.have1
  111.1 6.3 %collective-permute-start.20 = (f32[256,256]{1,0:T(8,128)S(1)}, f32[256,256]{1,0:T(8,128)}, u32[]{:S(2)}, u32[]{:S(2)}) collective-permute-start(f32[256,256]{1,0:T(8,128)S(1)} %broadcast_select_fusion.2.have1), channel_id=1, source_target_pairs={{0,15},{1,0},{2,1},{3,2},{4,3},{5,4},{6,5},{7,6},{8,7},{9,8},{10,9... | collective-permute-start | bytes 786440 | tf_op jit(solution)/shard_map/ppermute | solution.py:238
  117.5 10.2 %shard_map.28 = (bf16[3,2,256,256]{3,2,1,0:T(8,128)(2,1)S(1)}, f32[256,256]{1,0:T(8,128)S(1)}, bf16[4,256,512]{2,1,0:T(8,128)(2,1)S(1)}, bf16[4,256,512]{2,1,0:T(8,128)(2,1)S(1)}) custom-call(s32[3]{0:T(128)S(1)} %pad_add_fusion.ids, s32[2,64]{1,0:T(2,128)S(1)} %copy-done.1, f32[32,24,256]{2,1,0:T(8,128)S(1)} %all-to-all-done.1.raw, ...), custom_call_target="tpu_custom_call" | custom-call | flops 10000000000 | bytes 4194304 | tf_op jit(solution)/shard_map/pallas_call | solution.py:251
  127.7 6.5 %shard_map.29 = f32[2,4,256,256]{3,2,1,0:T(8,128)} custom-call(s32[3]{0:T(128)S(1)} %pad_add_fusion.ids, s32[2,64]{1,0:T(2,128)S(1)} %copy-done.1, bf16[3,2,256,256]{3,2,1,0:T(8,128)(2,1)S(1)} %get-tuple-element.9.inv, f32[256,256]{1,0:T(8,128)S(1)} %get-tuple-element.10.low, bf16[4,256,512]{2,1,0:T(8,128)(2,1)S(1)} %get-tuple-element.11.high, ...), custom_call_target="tpu_custom_call" | custom-call | flops 3000000000 | bytes 8388608 | tf_op jit(solution)/shard_map/pallas_call | solution.py:265
  (44 shorter events, 4.3 us)
Async XLA Ops:
  1.9 13.5 %collective-permute-start.10 = (f32[2,64,256]{2,1,0:T(8,128)S(1)}, f32[2,64,256]{2,1,0:T(8,128)S(1)}, u32[]{:S(2)}, u32[]{:S(2)}) collective-permute-start(f32[2,64,256]{2,1,0:T(8,128)S(1)} %get-tuple-element.22), channel_id=1, source_target_pairs={{0,96},{1,224},{16,97},{17,225},{32,98},{33,226},{48,99},{49,227},... | collective-permute-start | bytes 393224 | tf_op jit(solution)/shard_map/ppermute | solution.py:207
  3.2 12.2 %collective-permute-start.9 = (f32[2,64,256]{2,1,0:T(8,128)S(1)}, f32[2,64,256]{2,1,0:T(8,128)S(1)}, u32[]{:S(2)}, u32[]{:S(2)}) collective-permute-start(f32[2,64,256]{2,1,0:T(8,128)S(1)} %get-tuple-element.23), channel_id=1, source_target_pairs={{0,64},{1,192},{16,65},{17,193},{32,66},{33,194},{48,67},{49,195},... | collective-permute-start | bytes 393224 | tf_op jit(solution)/shard_map/ppermute | solution.py:207
  3.9 11.5 %collective-permute-start.7 = (f32[2,64,256]{2,1,0:T(8,128)S(1)}, f32[2,64,256]{2,1,0:T(8,128)S(1)}, u32[]{:S(2)}, u32[]{:S(2)}) collective-permute-start(f32[2,64,256]{2,1,0:T(8,128)S(1)} %get-tuple-element.21), channel_id=1, source_target_pairs={{0,0},{1,128},{16,1},{17,129},{32,2},{33,130},{48,3},{49,131},{64,... | collective-permute-start | bytes 393224 | tf_op jit(solution)/shard_map/ppermute | solution.py:207
  4.5 10.8 %collective-permute-start.8 = (f32[2,64,256]{2,1,0:T(8,128)S(1)}, f32[2,64,256]{2,1,0:T(8,128)S(1)}, u32[]{:S(2)}, u32[]{:S(2)}) collective-permute-start(f32[2,64,256]{2,1,0:T(8,128)S(1)} %get-tuple-element.20), channel_id=1, source_target_pairs={{0,32},{1,160},{16,33},{17,161},{32,34},{33,162},{48,35},{49,163},... | collective-permute-start | bytes 393224 | tf_op jit(solution)/shard_map/ppermute | solution.py:207
  5.2 13.6 %all-to-all-start = ((f32[32,8,256]{2,1,0:T(8,128)}), f32[32,8,256]{2,1,0:T(8,128)S(1)}, u32[]{:S(2)}, u32[]{:S(2)}) async-start(f32[32,8,256]{2,1,0:T(8,128)} %get-tuple-element.19), calls=%async_computation | async-start | bytes 524288 | tf_op jit(solution)/shard_map/all_to_all | solution.py:196
  15.4 5.4 %collective-permute-start.11 = (f32[64,256]{1,0:T(8,128)S(1)}, f32[64,256]{1,0:T(8,128)S(1)}, u32[]{:S(2)}, u32[]{:S(2)}) collective-permute-start(f32[64,256]{1,0:T(8,128)S(1)} %slice_bitcast_fusion.5), channel_id=1, source_target_pairs={{0,16},{16,0},{32,48},{48,32},{64,80},{80,64},{96,112},{112,96},{1... | collective-permute-start | bytes 196616 | tf_op jit(solution)/shard_map/ppermute | solution.py:220
  17.4 45.3 %collective-permute-start.16 = (f32[256,256]{1,0:T(8,128)S(1)}, f32[256,256]{1,0:T(8,128)S(1)}, u32[]{:S(2)}, u32[]{:S(2)}) collective-permute-start(f32[256,256]{1,0:T(8,128)S(1)} %get-tuple-element.15), channel_id=1, source_target_pairs={{0,10},{1,11},{16,26},{17,27},{32,42},{33,43},{48,58},{49,59},{64,... | collective-permute-start | bytes 786440 | tf_op jit(solution)/shard_map/ppermute | solution.py:210
  18.0 44.6 %collective-permute-start.13 = (f32[256,256]{1,0:T(8,128)S(1)}, f32[256,256]{1,0:T(8,128)S(1)}, u32[]{:S(2)}, u32[]{:S(2)}) collective-permute-start(f32[256,256]{1,0:T(8,128)S(1)} %get-tuple-element.17), channel_id=1, source_target_pairs={{0,6},{1,7},{16,22},{17,23},{32,38},{33,39},{48,54},{49,55},{64,70... | collective-permute-start | bytes 786440 | tf_op jit(solution)/shard_map/ppermute | solution.py:210
  18.9 28.7 %collective-permute-start.2 = (f32[2,8,256]{2,1,0:T(8,128)S(1)}, f32[2,8,256]{2,1,0:T(8,128)S(1)}, u32[]{:S(2)}, u32[]{:S(2)}) collective-permute-start(f32[2,8,256]{2,1,0:T(8,128)S(1)} %slice.58), channel_id=1, source_target_pairs={{0,8},{1,9},{16,24},{17,25},{32,40},{33,41},{48,56},{49,57},{64,72... | collective-permute-start | bytes 49160 | tf_op jit(solution)/shard_map/ppermute | solution.py:221
  19.5 39.2 %collective-permute-start = (f32[2,8,256]{2,1,0:T(8,128)S(1)}, f32[2,8,256]{2,1,0:T(8,128)S(1)}, u32[]{:S(2)}, u32[]{:S(2)}) collective-permute-start(f32[2,8,256]{2,1,0:T(8,128)S(1)} %slice.58), channel_id=1, source_target_pairs={{0,4},{1,5},{16,20},{17,21},{32,36},{33,37},{48,52},{49,53},{64,68... | collective-permute-start | bytes 49160 | tf_op jit(solution)/shard_map/ppermute | solution.py:221
  20.8 37.9 %collective-permute-start.1 = (f32[2,8,256]{2,1,0:T(8,128)S(1)}, f32[2,8,256]{2,1,0:T(8,128)S(1)}, u32[]{:S(2)}, u32[]{:S(2)}) collective-permute-start(f32[2,8,256]{2,1,0:T(8,128)S(1)} %slice.58), channel_id=1, source_target_pairs={{0,12},{1,13},{16,28},{17,29},{32,44},{33,45},{48,60},{49,61},{64,... | collective-permute-start | bytes 49160 | tf_op jit(solution)/shard_map/ppermute | solution.py:221
  22.6 49.6 %all-to-all-start.2 = ((f32[16,64,256]{2,1,0:T(8,128)}), f32[16,64,256]{2,1,0:T(8,128)S(1)}, u32[]{:S(2)}, u32[]{:S(2)}) async-start(f32[16,64,256]{2,1,0:T(8,128)} %broadcast_in_dim.5), calls=%async_computation.2 | async-start | bytes 2097152 | tf_op jit(solution)/shard_map/all_to_all | solution.py:241
  58.8 9.1 %collective-permute-start.4 = (f32[2,8,256]{2,1,0:T(8,128)S(1)}, f32[2,8,256]{2,1,0:T(8,128)S(1)}, u32[]{:S(2)}, u32[]{:S(2)}) collective-permute-start(f32[2,8,256]{2,1,0:T(8,128)S(1)} %add_select_fusion), channel_id=1, source_target_pairs={{0,2},{1,3},{4,6},{5,7},{8,10},{9,11},{12,14},{13,15},{16,18},{17,... | collective-permute-start | bytes 49160 | tf_op jit(solution)/shard_map/ppermute | solution.py:224
  60.1 7.8 %collective-permute-start.5 = (f32[2,8,256]{2,1,0:T(8,128)S(1)}, f32[2,8,256]{2,1,0:T(8,128)S(1)}, u32[]{:S(2)}, u32[]{:S(2)}) collective-permute-start(f32[2,8,256]{2,1,0:T(8,128)S(1)} %add_select_fusion), channel_id=1, source_target_pairs={{0,15},{1,2},{4,3},{5,6},{8,7},{9,10},{12,11},{13,14},{16,31},{17,... | collective-permute-start | bytes 49160 | tf_op jit(solution)/shard_map/ppermute | solution.py:225
  61.4 5.2 %collective-permute-start.6 = (f32[8,256]{1,0:T(8,128)S(1)}, f32[8,256]{1,0:T(8,128)S(1)}, u32[]{:S(2)}, u32[]{:S(2)}) collective-permute-start(f32[8,256]{1,0:T(8,128)S(1)} %slice_bitcast_fusion.7), channel_id=1, source_target_pairs={{1,0},{5,4},{9,8},{13,12},{17,16},{21,20},{25,24},{29,28},{33,32},... | collective-permute-start | bytes 24584 | tf_op jit(solution)/shard_map/ppermute | solution.py:227
  63.8 24.9 %copy-start.2 = (f32[256,256]{1,0:T(8,128)}, f32[256,256]{1,0:T(8,128)S(1)}, u32[]{:S(2)}) copy-start(f32[256,256]{1,0:T(8,128)S(1)} %get-tuple-element.14) | copy-start | bytes 786436
  63.8 24.9 %collective-permute-start.14 = (f32[256,256]{1,0:T(8,128)S(1)}, f32[256,256]{1,0:T(8,128)}, u32[]{:S(2)}, u32[]{:S(2)}) collective-permute-start(f32[256,256]{1,0:T(8,128)S(1)} %get-tuple-element.14), channel_id=1, source_target_pairs={{0,2},{1,3},{6,10},{7,11},{16,18},{17,19},{22,26},{23,27},{32,34},... | collective-permute-start | bytes 786440 | tf_op jit(solution)/shard_map/ppermute | solution.py:210
  65.2 25.9 %collective-permute-start.17 = (f32[256,256]{1,0:T(8,128)S(1)}, f32[256,256]{1,0:T(8,128)}, u32[]{:S(2)}, u32[]{:S(2)}) collective-permute-start(f32[256,256]{1,0:T(8,128)S(1)} %get-tuple-element.13), channel_id=1, source_target_pairs={{0,14},{1,15},{10,6},{11,7},{16,30},{17,31},{26,22},{27,23},{32,46... | collective-permute-start | bytes 786440 | tf_op jit(solution)/shard_map/ppermute | solution.py:210
  66.5 5.6 %collective-permute-start.3 = (f32[2,8,256]{2,1,0:T(8,128)S(1)}, f32[2,8,256]{2,1,0:T(8,128)S(1)}, u32[]{:S(2)}, u32[]{:S(2)}) collective-permute-start(f32[2,8,256]{2,1,0:T(8,128)S(1)} %add_select_fusion), channel_id=1, source_target_pairs={{0,1},{4,5},{8,9},{12,13},{16,17},{20,21},{24,25},{28,29},{32,33},... | collective-permute-start | bytes 49160 | tf_op jit(solution)/shard_map/ppermute | solution.py:226
  73.1 44.4 %copy-start.1 = (s32[2,64]{1,0:T(2,128)S(1)}, s32[2,64]{1,0:T(2,128)}, u32[]{:S(2)}) copy-start(s32[2,64]{1,0:T(2,128)} %struct.3) | copy-start | bytes 1540
  73.1 44.3 %all-to-all-start.1 = ((f32[32,24,256]{2,1,0:T(8,128)}), f32[32,24,256]{2,1,0:T(8,128)S(1)}, u32[]{:S(2)}, u32[]{:S(2)}) async-start(f32[32,24,256]{2,1,0:T(8,128)} %broadcast_in_dim.4), calls=%async_computation.1 | async-start | bytes 1572864 | tf_op jit(solution)/shard_map/all_to_all | solution.py:244
  86.7 30.8 %collective-permute-start.12 = (f32[4,256,256]{2,1,0:T(8,128)S(1)}, f32[4,256,256]{2,1,0:T(8,128)S(1)}, u32[]{:S(2)}, u32[]{:S(2)}) collective-permute-start(f32[4,256,256]{2,1,0:T(8,128)S(1)} %bitcast.42), channel_id=1, source_target_pairs={{0,16},{16,0},{32,48},{48,32},{64,80},{80,64},{96,112},{112,96},{1... | collective-permute-start | bytes 3145736 | tf_op jit(solution)/shard_map/ppermute | solution.py:242
  89.7 17.5 %collective-permute-start.15 = (f32[256,256]{1,0:T(8,128)S(1)}, f32[256,256]{1,0:T(8,128)}, u32[]{:S(2)}, u32[]{:S(2)}) collective-permute-start(f32[256,256]{1,0:T(8,128)S(1)} %broadcast_select_fusion.4), channel_id=1, source_target_pairs={{0,14},{1,15},{2,4},{3,5},{6,8},{7,9},{10,12},{11,13},{16,30},{17,... | collective-permute-start | bytes 786440 | tf_op jit(solution)/shard_map/ppermute | solution.py:210
  91.8 18.3 %collective-permute-start.18 = (f32[256,256]{1,0:T(8,128)}, f32[256,256]{1,0:T(8,128)}, u32[]{:S(2)}, u32[]{:S(2)}) collective-permute-start(f32[256,256]{1,0:T(8,128)} %broadcast_select_fusion.1), channel_id=1, source_target_pairs={{0,2},{1,3},{6,4},{7,5},{10,8},{11,9},{14,12},{15,13},{16,18},{17,... | collective-permute-start | bytes 786440 | tf_op jit(solution)/shard_map/ppermute | solution.py:210
  108.2 19.5 %collective-permute-start.19 = (f32[256,256]{1,0:T(8,128)S(1)}, f32[256,256]{1,0:T(8,128)}, u32[]{:S(2)}, u32[]{:S(2)}) collective-permute-start(f32[256,256]{1,0:T(8,128)S(1)} %broadcast_select_fusion.5.have0), channel_id=1, source_target_pairs={{0,1},{1,2},{2,3},{3,4},{4,5},{5,6},{6,7},{7,8},{8,9},{9,10},{10,1... | collective-permute-start | bytes 786440 | tf_op jit(solution)/shard_map/ppermute | solution.py:238
  111.1 16.6 %collective-permute-start.20 = (f32[256,256]{1,0:T(8,128)S(1)}, f32[256,256]{1,0:T(8,128)}, u32[]{:S(2)}, u32[]{:S(2)}) collective-permute-start(f32[256,256]{1,0:T(8,128)S(1)} %broadcast_select_fusion.2.have1), channel_id=1, source_target_pairs={{0,15},{1,0},{2,1},{3,2},{4,3},{5,4},{6,5},{7,6},{8,7},{9,8},{10,9... | collective-permute-start | bytes 786440 | tf_op jit(solution)/shard_map/ppermute | solution.py:238
  117.5 10.3 %copy-start = (f32[2,1,4,1,256,256]{5,4,3,2,1,0:T(8,128)S(1)}, f32[2,1,4,1,256,256]{5,4,3,2,1,0:T(8,128)}, u32[]{:S(2)}) copy-start(f32[2,1,4,1,256,256]{5,4,3,2,1,0:T(8,128)} %param.2) | copy-start | bytes 6291460

commit v4 on v3

--- a/solution.py
+++ b/solution.py
@@ -28,6 +28,11 @@
 
 def mul(a, b, dims):
     return mul_parts(parts(a), parts(b), dims)
+
+
+def mul_rough(a, b, dims):
+    a, b = a.astype(jnp.bfloat16), b.astype(jnp.bfloat16)
+    return lax.dot_general(a, b, (dims, ((), ())), preferred_element_type=jnp.float32)
 
 
 def iotas(n):
@@ -50,19 +55,19 @@
     def improve(carry):
         t, err, _, count = carry
         x = err * half
-        t = mul((eye - x) + mul(x, x, ROWS), t, ROWS)
+        t = mul((eye - x) + mul_rough(x, x, ROWS), t, ROWS)
         err = residual(t)
         return t, err, jnp.sum(err * err), count + 1
 
     x = (unit - eye) * half
-    t = (eye - x) + mul(x, x, ROWS)
+    t = (eye - x) + mul_rough(x, x, ROWS)
     err = residual(t)
     start = (t, err, jnp.sum(err * err), jnp.int32(0))
     t, err, size, _ = lax.while_loop(lambda c: (c[2] > 1e-4) & (c[3] < 8), improve, start)
     x = err * half
-    near = parts(x)
-    x = x - mul_parts(near, near, BOTH) * half
-    t = mul((eye - x) + mul_parts(near, near, ROWS), t, ROWS)
+    twice = mul_rough(x, x, ROWS)
+    x = x - mul_rough(x, x, BOTH) * half
+    t = mul((eye - x) + twice, t, ROWS)
     inv[...] = t * scale_row
 
     @pl.when(jnp.logical_not(size <= 1e-4))
@@ -118,19 +123,21 @@
     def _():
         low[...] = jnp.where(ri >= ci, mul_parts(parts(s1), inv1, BOTH), 0.0)
 
-    for q in range(4):
-        mine = core == q // 2
-        slot = 2 * (q % 2)
-        a0 = jnp.where(mine, own[slot], other[slot])
-        a1 = jnp.where(mine, own[slot + 1], other[slot + 1])
-        glob = q * 16 + col
-        keep0 = struct[0, glob].astype(jnp.float32)
-        keep1 = struct[1, glob].astype(jnp.float32)
-        both = solve(a0, a1, keep0, keep1, inv0, half10, inv1)
-        for k in range(2):
-            top, bottom = parts(both[k])
-            high[q, :, k * n:(k + 1) * n] = top
-            rest[q, :, k * n:(k + 1) * n] = bottom
+    def block(q, k):
+        slot = 2 * (q % 2) + k
+        return jnp.where(core == q // 2, own[slot], other[slot])
+
+    def keep(k):
+        return jnp.concatenate([jnp.full((n, 1), struct[k, q * 16 + col].astype(jnp.float32)) for q in range(4)])
+
+    def stack(k):
+        return jnp.concatenate([block(q, k) for q in range(4)])
+
+    both = solve(stack(0), stack(1), keep(0), keep(1), inv0, half10, inv1)
+    for k in range(2):
+        top, bottom = parts(both[k])
+        high[:, :, k * n:(k + 1) * n] = top.reshape(4, n, n)
+        rest[:, :, k * n:(k + 1) * n] = bottom.reshape(4, n, n)
 
 
 def tail_kernel(ids, struct, inv, low, high, rest, have0, have1, near0, near1, mat, out, row_high, row_rest):
@@ -196,6 +203,24 @@
         return lax.all_to_all(block.reshape(nrow, width // nrow, width), "row", 0, 0)[0:2]
 
     diag = scatter(mine[0])
+
+    def spread(have, step):
+        return [lax.ppermute(a, "col", sorted(((s + c) % ncol, (t + c) % ncol) for s, t in pairs for c in (0, 1)))
+                for a, pairs in zip(have, (step, [(-s, -t) for s, t in step]))]
+
+    def merged(have, near, step):
+        def took(pairs):
+            return sum((((col_id - t) % ncol) < 2) for _, t in pairs) > 0
+        return [jnp.where(took(pairs), b, a) for a, b, pairs in zip(have, near, (step, [(-s, -t) for s, t in step]))]
+
+    steps = [[(0, 6)], [(0, 2), (6, 10)], [(2, 4), (6, 8), (10, 12), (0, 14)]]
+    far = spread([a for a in mine], steps[0])
+    have = merged(mine, far, steps[0])
+    near = spread(have, steps[1])
+    have = merged(have, near, steps[1])
+    last = spread(have, steps[2])
+    have = merged(have, last, steps[2])
+    rows = have + [lax.ppermute(a, "col", [(s, (s + d) % ncol) for s in range(ncol)]) for a, d in zip(have, (1, -1))]
     both = jnp.stack([a for a in mine])
     part = 0.0
     for k in range(4):
@@ -205,37 +230,18 @@
                 target = row_of(k, column + 2 * (row // ncol), 0)
                 pairs.append((row * ncol + column, target * ncol + row % ncol))
         part = part + lax.ppermute(both[:, k * quarter:(k + 1) * quarter], ("row", "col"), pairs)
-
-    def spread(have, step):
-        return [lax.ppermute(a, "col", sorted(((s + c) % ncol, (t + c) % ncol) for s, t in pairs for c in (0, 1)))
-                for a, pairs in zip(have, (step, [(-s, -t) for s, t in step]))]
-
-    def merged(have, near, step):
-        def took(pairs):
-            return sum((((col_id - t) % ncol) < 2) for _, t in pairs) > 0
-        return [jnp.where(took(pairs), b, a) for a, b, pairs in zip(have, near, (step, [(-s, -t) for s, t in step]))]
-
-    steps = [[(0, 6)], [(0, 2), (6, 10)], [(2, 4), (6, 8), (10, 12), (0, 14)]]
-    far = spread([a for a in mine], steps[0])
     piece = jnp.where(lax.rem(row_id, 2) == 0, part[0], lax.ppermute(part[1], "row", swap))
     got = [lax.ppermute(diag, "col", [(s, s + d) for s in (0, 1)]) for d in (4, 12, 8)]
     diag = jnp.where(col_id < 2, diag, got[0] + got[1] + got[2])
     sources = [s for s in range(ncol) if s % 4 < 2]
     two_up = lax.ppermute(diag, "col", [(s, s + 2) for s in sources])
     mixed = lax.ppermute(diag, "col", [(s, (s - 1) % ncol if s % 4 == 0 else s + 1) for s in sources])
-    one_up = lax.ppermute(diag, "col", [(s, s + 1) for s in sources if s % 4 == 0])
-    one_down = lax.ppermute(diag[1], "col", [(s, s - 1) for s in sources if s % 4 == 1])
+    one_up = lax.ppermute(diag, "col", [(s, s ^ 1) for s in range(ncol)])
     place = lax.rem(col_id, 4)
     left = jnp.where(place == 0, diag, jnp.where(place == 1, one_up, jnp.where(place == 2, two_up, mixed)))
-    right = jnp.where(place == 0, one_down, jnp.where(place == 1, diag[1], jnp.where(place == 2, mixed[1], two_up[1])))
+    right = jnp.where(place == 0, one_up[1], jnp.where(place == 1, diag[1], jnp.where(place == 2, mixed[1], two_up[1])))
     diag = jnp.concatenate([left[0], left[1], right])
 
-    have = merged(mine, far, steps[0])
-    near = spread(have, steps[1])
-    have = merged(have, near, steps[1])
-    last = spread(have, steps[2])
-    have = merged(have, last, steps[2])
-    rows = have + [lax.ppermute(a, "col", [(s, (s + d) % ncol) for s in range(ncol)]) for a, d in zip(have, (1, -1))]
     own = jnp.broadcast_to(piece[None], (nrow // 2,) + piece.shape)
     groups = [list(range(c, nrow, 2)) for c in range(2)]
     own = lax.all_to_all(own, "row", 0, 0, axis_index_groups=groups).reshape(4, width, width)

time: 135 us -> 130 us (0.963)
  the two profiles are of different devices: /device:TPU:182 before, /device:TPU:6 now
where the time goes in v4:
time: 130 us; the launch traced here: 129 us
  starting transfers between devices  95.1 us (73%)
  Pallas kernels  14.9 us (11%)
  waiting for transfers between devices  10.1 us (8%)
  other arithmetic  4.06 us (3%)
  local copies, waits for them, and re-layouts  3.87 us (3%)
    ppermute x6, starting transfers between devices, spread(): lax.ppermute(a, 'col', sorted((((s + c) % ncol, (t + c) % ncol) for s, t...  27.7 us
    ppermute x4, starting transfers between devices, on_device(): lax.ppermute(both[:, k * quarter:(k + 1) * quarter], ('row', 'col'), pairs)  15.7 us
    all_to_all x1, starting transfers between devices, scatter(): lax.all_to_all(block.reshape(nrow, width // nrow, width), 'row', 0, 0)[0:2]  13 us
    all_to_all x1, starting transfers between devices, on_device(): lax.all_to_all(own, 'row', 0, 0, axis_index_groups=groups)  12.4 us
    pallas_call x1, Pallas kernels, on_device(): pl.pallas_call(head_kernel, out_shape=[jax.ShapeDtypeStruct((3, 2, width,...  9.09 us
    ppermute x2, starting transfers between devices, on_device(): lax.ppermute(a, 'col', [(s, (s + d) % ncol) for s in range(ncol)])  7.06 us
    all_to_all x1, starting transfers between devices, on_device(): raw = lax.all_to_all(raw, 'row', 0, 0)  6.75 us
    pallas_call x1, Pallas kernels, on_device(): pl.pallas_call(tail_kernel, out_shape=jax.ShapeDtypeStruct(blocks.shape,...  5.81 us
  transfers between devices with their start and end apart: 23, of which 2 were waited for; matrix products, arithmetic and copies ran while one was open for 5% of the time, Pallas kernels for 7%

profile of v4, /device:TPU:6, one launch (start us, length us, event | category | flops | bytes accessed | tf_op | source)
XLA Modules:
  0.0 128.7 jit_solution(2625521045402465244)
XLA Ops:
  0.0 1.8 %slice_bitcast_fusion = (f32[256,256]{1,0:T(8,128)S(1)}, f32[1,256,256]{2,1,0:T(8,128)S(1)}, f32[256,256]{1,0:T(8,128)S(1)}, f32[1,256,256]{2,1,0:T(8,128)S(1)}, f32[32,8,256]{2,1,0:T(8,128)}) fusion(f32[2,4,256,256]{3,2,1,0:T(8,128)} %bitcast.36), kind=kLoop, calls=%fused_computation.6 | loop fusion | bytes 1835008 | tf_op jit(solution)/shard_map/squeeze | solution.py:200
  1.9 11.8 %collective-permute-start.9 = (f32[2,64,256]{2,1,0:T(8,128)S(1)}, f32[2,64,256]{2,1,0:T(8,128)S(1)}, u32[]{:S(2)}, u32[]{:S(2)}) collective-permute-start(f32[2,64,256]{2,1,0:T(8,128)S(1)} %get-tuple-element.22), channel_id=1, source_target_pairs={{0,96},{1,224},{16,97},{17,225},{32,98},{33,226},{48,99},{49,227},... | collective-permute-start | bytes 393224 | tf_op jit(solution)/shard_map/ppermute | solution.py:232
  13.7 1.3 %collective-permute-start.8 = (f32[2,64,256]{2,1,0:T(8,128)S(1)}, f32[2,64,256]{2,1,0:T(8,128)S(1)}, u32[]{:S(2)}, u32[]{:S(2)}) collective-permute-start(f32[2,64,256]{2,1,0:T(8,128)S(1)} %get-tuple-element.23), channel_id=1, source_target_pairs={{0,64},{1,192},{16,65},{17,193},{32,66},{33,194},{48,67},{49,195},... | collective-permute-start | bytes 393224 | tf_op jit(solution)/shard_map/ppermute | solution.py:232
  15.0 1.3 %collective-permute-start.6 = (f32[2,64,256]{2,1,0:T(8,128)S(1)}, f32[2,64,256]{2,1,0:T(8,128)S(1)}, u32[]{:S(2)}, u32[]{:S(2)}) collective-permute-start(f32[2,64,256]{2,1,0:T(8,128)S(1)} %get-tuple-element.21), channel_id=1, source_target_pairs={{0,0},{1,128},{16,1},{17,129},{32,2},{33,130},{48,3},{49,131},{64,... | collective-permute-start | bytes 393224 | tf_op jit(solution)/shard_map/ppermute | solution.py:232
  16.3 1.3 %collective-permute-start.7 = (f32[2,64,256]{2,1,0:T(8,128)S(1)}, f32[2,64,256]{2,1,0:T(8,128)S(1)}, u32[]{:S(2)}, u32[]{:S(2)}) collective-permute-start(f32[2,64,256]{2,1,0:T(8,128)S(1)} %get-tuple-element.20), channel_id=1, source_target_pairs={{0,32},{1,160},{16,33},{17,161},{32,34},{33,162},{48,35},{49,163},... | collective-permute-start | bytes 393224 | tf_op jit(solution)/shard_map/ppermute | solution.py:232
  17.6 13.0 %all-to-all-start = ((f32[32,8,256]{2,1,0:T(8,128)}), f32[32,8,256]{2,1,0:T(8,128)S(1)}, u32[]{:S(2)}, u32[]{:S(2)}) async-start(f32[32,8,256]{2,1,0:T(8,128)} %get-tuple-element.19), calls=%async_computation | async-start | bytes 524288 | tf_op jit(solution)/shard_map/all_to_all | solution.py:203
  30.7 2.1 %collective-permute-start.10 = (f32[64,256]{1,0:T(8,128)S(1)}, f32[64,256]{1,0:T(8,128)S(1)}, u32[]{:S(2)}, u32[]{:S(2)}) collective-permute-start(f32[64,256]{1,0:T(8,128)S(1)} %slice_bitcast_fusion.5), channel_id=1, source_target_pairs={{0,16},{16,0},{32,48},{48,32},{64,80},{80,64},{96,112},{112,96},{1... | collective-permute-start | bytes 196616 | tf_op jit(solution)/shard_map/ppermute | solution.py:233
  32.8 15.6 %collective-permute-start.15 = (f32[256,256]{1,0:T(8,128)S(1)}, f32[256,256]{1,0:T(8,128)S(1)}, u32[]{:S(2)}, u32[]{:S(2)}) collective-permute-start(f32[256,256]{1,0:T(8,128)S(1)} %get-tuple-element.15), channel_id=1, source_target_pairs={{0,10},{1,11},{16,26},{17,27},{32,42},{33,43},{48,58},{49,59},{64,... | collective-permute-start | bytes 786440 | tf_op jit(solution)/shard_map/ppermute | solution.py:208
  48.5 1.3 %collective-permute-start.12 = (f32[256,256]{1,0:T(8,128)S(1)}, f32[256,256]{1,0:T(8,128)S(1)}, u32[]{:S(2)}, u32[]{:S(2)}) collective-permute-start(f32[256,256]{1,0:T(8,128)S(1)} %get-tuple-element.17), channel_id=1, source_target_pairs={{0,6},{1,7},{16,22},{17,23},{32,38},{33,39},{48,54},{49,55},{64,70... | collective-permute-start | bytes 786440 | tf_op jit(solution)/shard_map/ppermute | solution.py:208
  49.9 1.3 %collective-permute-start.2 = (f32[2,8,256]{2,1,0:T(8,128)S(1)}, f32[2,8,256]{2,1,0:T(8,128)S(1)}, u32[]{:S(2)}, u32[]{:S(2)}) collective-permute-start(f32[2,8,256]{2,1,0:T(8,128)S(1)} %slice.61), channel_id=1, source_target_pairs={{0,8},{1,9},{16,24},{17,25},{32,40},{33,41},{48,56},{49,57},{64,72... | collective-permute-start | bytes 49160 | tf_op jit(solution)/shard_map/ppermute | solution.py:234
  51.2 1.3 %collective-permute-start = (f32[2,8,256]{2,1,0:T(8,128)S(1)}, f32[2,8,256]{2,1,0:T(8,128)S(1)}, u32[]{:S(2)}, u32[]{:S(2)}) collective-permute-start(f32[2,8,256]{2,1,0:T(8,128)S(1)} %slice.61), channel_id=1, source_target_pairs={{0,4},{1,5},{16,20},{17,21},{32,36},{33,37},{48,52},{49,53},{64,68... | collective-permute-start | bytes 49160 | tf_op jit(solution)/shard_map/ppermute | solution.py:234
  52.5 1.3 %collective-permute-start.1 = (f32[2,8,256]{2,1,0:T(8,128)S(1)}, f32[2,8,256]{2,1,0:T(8,128)S(1)}, u32[]{:S(2)}, u32[]{:S(2)}) collective-permute-start(f32[2,8,256]{2,1,0:T(8,128)S(1)} %slice.61), channel_id=1, source_target_pairs={{0,12},{1,13},{16,28},{17,29},{32,44},{33,45},{48,60},{49,61},{64,... | collective-permute-start | bytes 49160 | tf_op jit(solution)/shard_map/ppermute | solution.py:234
  53.8 1.1 broadcast_in_dim.5
  54.9 12.4 %all-to-all-start.2 = ((f32[16,64,256]{2,1,0:T(8,128)}), f32[16,64,256]{2,1,0:T(8,128)S(1)}, u32[]{:S(2)}, u32[]{:S(2)}) async-start(f32[16,64,256]{2,1,0:T(8,128)} %broadcast_in_dim.5), calls=%async_computation.2 | async-start | bytes 2097152 | tf_op jit(solution)/shard_map/all_to_all | solution.py:247
  67.4 1.9 %collective-permute-start.3 = (f32[2,8,256]{2,1,0:T(8,128)S(1)}, f32[2,8,256]{2,1,0:T(8,128)S(1)}, u32[]{:S(2)}, u32[]{:S(2)}) collective-permute-start(f32[2,8,256]{2,1,0:T(8,128)S(1)} %add_select_fusion), channel_id=1, source_target_pairs={{0,1},{1,0},{2,3},{3,2},{4,5},{5,4},{6,7},{7,6},{8,9},{9,8},{10,11... | collective-permute-start | bytes 49160 | tf_op jit(solution)/shard_map/ppermute | solution.py:239
  69.3 1.3 %collective-permute-start.4 = (f32[2,8,256]{2,1,0:T(8,128)S(1)}, f32[2,8,256]{2,1,0:T(8,128)S(1)}, u32[]{:S(2)}, u32[]{:S(2)}) collective-permute-start(f32[2,8,256]{2,1,0:T(8,128)S(1)} %add_select_fusion), channel_id=1, source_target_pairs={{0,2},{1,3},{4,6},{5,7},{8,10},{9,11},{12,14},{13,15},{16,18},{17,... | collective-permute-start | bytes 49160 | tf_op jit(solution)/shard_map/ppermute | solution.py:237
  70.6 1.3 %collective-permute-start.5 = (f32[2,8,256]{2,1,0:T(8,128)S(1)}, f32[2,8,256]{2,1,0:T(8,128)S(1)}, u32[]{:S(2)}, u32[]{:S(2)}) collective-permute-start(f32[2,8,256]{2,1,0:T(8,128)S(1)} %add_select_fusion), channel_id=1, source_target_pairs={{0,15},{1,2},{4,3},{5,6},{8,7},{9,10},{12,11},{13,14},{16,31},{17,... | collective-permute-start | bytes 49160 | tf_op jit(solution)/shard_map/ppermute | solution.py:238
  71.9 1.1 broadcast_select_fusion
  73.1 2.0 %collective-permute-start.13 = (f32[256,256]{1,0:T(8,128)S(1)}, f32[256,256]{1,0:T(8,128)}, u32[]{:S(2)}, u32[]{:S(2)}) collective-permute-start(f32[256,256]{1,0:T(8,128)S(1)} %get-tuple-element.14), channel_id=1, source_target_pairs={{0,2},{1,3},{6,10},{7,11},{16,18},{17,19},{22,26},{23,27},{32,34},... | collective-permute-start | bytes 786440 | tf_op jit(solution)/shard_map/ppermute | solution.py:208
  75.0 2.0 %collective-permute-start.16 = (f32[256,256]{1,0:T(8,128)S(1)}, f32[256,256]{1,0:T(8,128)}, u32[]{:S(2)}, u32[]{:S(2)}) collective-permute-start(f32[256,256]{1,0:T(8,128)S(1)} %get-tuple-element.13), channel_id=1, source_target_pairs={{0,14},{1,15},{10,6},{11,7},{16,30},{17,31},{26,22},{27,23},{32,46... | collective-permute-start | bytes 786440 | tf_op jit(solution)/shard_map/ppermute | solution.py:208
  77.1 5.2 %all-to-all-done.2 = f32[16,64,256]{2,1,0:T(8,128)S(1)} async-done(((f32[16,64,256]{2,1,0:T(8,128)}), f32[16,64,256]{2,1,0:T(8,128)S(1)}, u32[]{:S(2)}, u32[]{:S(2)}) %all-to-all-start.2) | async-done | bytes 1048608 | tf_op jit(solution)/shard_map/all_to_all | solution.py:247
  83.2 6.8 %all-to-all-start.1 = ((f32[32,24,256]{2,1,0:T(8,128)}), f32[32,24,256]{2,1,0:T(8,128)S(1)}, u32[]{:S(2)}, u32[]{:S(2)}) async-start(f32[32,24,256]{2,1,0:T(8,128)} %broadcast_in_dim.4), calls=%async_computation.1 | async-start | bytes 1572864 | tf_op jit(solution)/shard_map/all_to_all | solution.py:250
  90.0 2.1 %collective-permute-start.11 = (f32[4,256,256]{2,1,0:T(8,128)S(1)}, f32[4,256,256]{2,1,0:T(8,128)S(1)}, u32[]{:S(2)}, u32[]{:S(2)}) collective-permute-start(f32[4,256,256]{2,1,0:T(8,128)S(1)} %bitcast.34), channel_id=1, source_target_pairs={{0,16},{16,0},{32,48},{48,32},{64,80},{80,64},{96,112},{112,96},{1... | collective-permute-start | bytes 3145736 | tf_op jit(solution)/shard_map/ppermute | solution.py:248
  92.0 1.0 broadcast_select_fusion.4
  93.0 2.0 %collective-permute-start.14 = (f32[256,256]{1,0:T(8,128)S(1)}, f32[256,256]{1,0:T(8,128)}, u32[]{:S(2)}, u32[]{:S(2)}) collective-permute-start(f32[256,256]{1,0:T(8,128)S(1)} %broadcast_select_fusion.4), channel_id=1, source_target_pairs={{0,14},{1,15},{2,4},{3,5},{6,8},{7,9},{10,12},{11,13},{16,30},{17,... | collective-permute-start | bytes 786440 | tf_op jit(solution)/shard_map/ppermute | solution.py:208
  95.8 4.8 %collective-permute-start.17 = (f32[256,256]{1,0:T(8,128)}, f32[256,256]{1,0:T(8,128)}, u32[]{:S(2)}, u32[]{:S(2)}) collective-permute-start(f32[256,256]{1,0:T(8,128)} %broadcast_select_fusion.1), channel_id=1, source_target_pairs={{0,2},{1,3},{6,4},{7,5},{10,8},{11,9},{14,12},{15,13},{16,18},{17,... | collective-permute-start | bytes 786440 | tf_op jit(solution)/shard_map/ppermute | solution.py:208
  100.7 4.9 %collective-permute-done.14 = f32[256,256]{1,0:T(8,128)} collective-permute-done((f32[256,256]{1,0:T(8,128)S(1)}, f32[256,256]{1,0:T(8,128)}, u32[]{:S(2)}, u32[]{:S(2)}) %collective-permute-start.14) | collective-permute-done | bytes 262176 | tf_op jit(solution)/shard_map/ppermute | solution.py:208
  105.6 1.9 %collective-permute-start.18 = (f32[256,256]{1,0:T(8,128)S(1)}, f32[256,256]{1,0:T(8,128)}, u32[]{:S(2)}, u32[]{:S(2)}) collective-permute-start(f32[256,256]{1,0:T(8,128)S(1)} %broadcast_select_fusion.5.have0), channel_id=1, source_target_pairs={{0,1},{1,2},{2,3},{3,4},{4,5},{5,6},{6,7},{7,8},{8,9},{9,10},{10,1... | collective-permute-start | bytes 786440 | tf_op jit(solution)/shard_map/ppermute | solution.py:223
  107.5 1.0 broadcast_select_fusion.2.have1
  108.5 5.1 %collective-permute-start.19 = (f32[256,256]{1,0:T(8,128)S(1)}, f32[256,256]{1,0:T(8,128)}, u32[]{:S(2)}, u32[]{:S(2)}) collective-permute-start(f32[256,256]{1,0:T(8,128)S(1)} %broadcast_select_fusion.2.have1), channel_id=1, source_target_pairs={{0,15},{1,0},{2,1},{3,2},{4,3},{5,4},{6,5},{7,6},{8,7},{9,8},{10,9... | collective-permute-start | bytes 786440 | tf_op jit(solution)/shard_map/ppermute | solution.py:223
  113.7 9.1 %shard_map.28 = (bf16[3,2,256,256]{3,2,1,0:T(8,128)(2,1)S(1)}, f32[256,256]{1,0:T(8,128)S(1)}, bf16[4,256,512]{2,1,0:T(8,128)(2,1)S(1)}, bf16[4,256,512]{2,1,0:T(8,128)(2,1)S(1)}) custom-call(s32[3]{0:T(128)S(1)} %pad_add_fusion.ids, s32[2,64]{1,0:T(2,128)S(1)} %copy-done.1, f32[32,24,256]{2,1,0:T(8,128)S(1)} %all-to-all-done.1.raw, ...), custom_call_target="tpu_custom_call" | custom-call | flops 10000000000 | bytes 4194304 | tf_op jit(solution)/shard_map/pallas_call | solution.py:257
  122.8 5.8 %shard_map.29 = f32[2,4,256,256]{3,2,1,0:T(8,128)} custom-call(s32[3]{0:T(128)S(1)} %pad_add_fusion.ids, s32[2,64]{1,0:T(2,128)S(1)} %copy-done.1, bf16[3,2,256,256]{3,2,1,0:T(8,128)(2,1)S(1)} %get-tuple-element.9.inv, f32[256,256]{1,0:T(8,128)S(1)} %get-tuple-element.10.low, bf16[4,256,512]{2,1,0:T(8,128)(2,1)S(1)} %get-tuple-element.11.high, ...), custom_call_target="tpu_custom_call" | custom-call | flops 3000000000 | bytes 8388608 | tf_op jit(solution)/shard_map/pallas_call | solution.py:271
  (40 shorter events, 2.0 us)
Async XLA Ops:
  1.9 28.8 %collective-permute-start.9 = (f32[2,64,256]{2,1,0:T(8,128)S(1)}, f32[2,64,256]{2,1,0:T(8,128)S(1)}, u32[]{:S(2)}, u32[]{:S(2)}) collective-permute-start(f32[2,64,256]{2,1,0:T(8,128)S(1)} %get-tuple-element.22), channel_id=1, source_target_pairs={{0,96},{1,224},{16,97},{17,225},{32,98},{33,226},{48,99},{49,227},... | collective-permute-start | bytes 393224 | tf_op jit(solution)/shard_map/ppermute | solution.py:232
  13.7 17.0 %collective-permute-start.8 = (f32[2,64,256]{2,1,0:T(8,128)S(1)}, f32[2,64,256]{2,1,0:T(8,128)S(1)}, u32[]{:S(2)}, u32[]{:S(2)}) collective-permute-start(f32[2,64,256]{2,1,0:T(8,128)S(1)} %get-tuple-element.23), channel_id=1, source_target_pairs={{0,64},{1,192},{16,65},{17,193},{32,66},{33,194},{48,67},{49,195},... | collective-permute-start | bytes 393224 | tf_op jit(solution)/shard_map/ppermute | solution.py:232
  15.0 15.7 %collective-permute-start.6 = (f32[2,64,256]{2,1,0:T(8,128)S(1)}, f32[2,64,256]{2,1,0:T(8,128)S(1)}, u32[]{:S(2)}, u32[]{:S(2)}) collective-permute-start(f32[2,64,256]{2,1,0:T(8,128)S(1)} %get-tuple-element.21), channel_id=1, source_target_pairs={{0,0},{1,128},{16,1},{17,129},{32,2},{33,130},{48,3},{49,131},{64,... | collective-permute-start | bytes 393224 | tf_op jit(solution)/shard_map/ppermute | solution.py:232
  16.3 14.4 %collective-permute-start.7 = (f32[2,64,256]{2,1,0:T(8,128)S(1)}, f32[2,64,256]{2,1,0:T(8,128)S(1)}, u32[]{:S(2)}, u32[]{:S(2)}) collective-permute-start(f32[2,64,256]{2,1,0:T(8,128)S(1)} %get-tuple-element.20), channel_id=1, source_target_pairs={{0,32},{1,160},{16,33},{17,161},{32,34},{33,162},{48,35},{49,163},... | collective-permute-start | bytes 393224 | tf_op jit(solution)/shard_map/ppermute | solution.py:232
  17.6 32.3 %all-to-all-start = ((f32[32,8,256]{2,1,0:T(8,128)}), f32[32,8,256]{2,1,0:T(8,128)S(1)}, u32[]{:S(2)}, u32[]{:S(2)}) async-start(f32[32,8,256]{2,1,0:T(8,128)} %get-tuple-element.19), calls=%async_computation | async-start | bytes 524288 | tf_op jit(solution)/shard_map/all_to_all | solution.py:203
  30.7 21.8 %collective-permute-start.10 = (f32[64,256]{1,0:T(8,128)S(1)}, f32[64,256]{1,0:T(8,128)S(1)}, u32[]{:S(2)}, u32[]{:S(2)}) collective-permute-start(f32[64,256]{1,0:T(8,128)S(1)} %slice_bitcast_fusion.5), channel_id=1, source_target_pairs={{0,16},{16,0},{32,48},{48,32},{64,80},{80,64},{96,112},{112,96},{1... | collective-permute-start | bytes 196616 | tf_op jit(solution)/shard_map/ppermute | solution.py:233
  32.8 39.1 %collective-permute-start.15 = (f32[256,256]{1,0:T(8,128)S(1)}, f32[256,256]{1,0:T(8,128)S(1)}, u32[]{:S(2)}, u32[]{:S(2)}) collective-permute-start(f32[256,256]{1,0:T(8,128)S(1)} %get-tuple-element.15), channel_id=1, source_target_pairs={{0,10},{1,11},{16,26},{17,27},{32,42},{33,43},{48,58},{49,59},{64,... | collective-permute-start | bytes 786440 | tf_op jit(solution)/shard_map/ppermute | solution.py:208
  48.5 23.5 %collective-permute-start.12 = (f32[256,256]{1,0:T(8,128)S(1)}, f32[256,256]{1,0:T(8,128)S(1)}, u32[]{:S(2)}, u32[]{:S(2)}) collective-permute-start(f32[256,256]{1,0:T(8,128)S(1)} %get-tuple-element.17), channel_id=1, source_target_pairs={{0,6},{1,7},{16,22},{17,23},{32,38},{33,39},{48,54},{49,55},{64,70... | collective-permute-start | bytes 786440 | tf_op jit(solution)/shard_map/ppermute | solution.py:208
  49.9 17.4 %collective-permute-start.2 = (f32[2,8,256]{2,1,0:T(8,128)S(1)}, f32[2,8,256]{2,1,0:T(8,128)S(1)}, u32[]{:S(2)}, u32[]{:S(2)}) collective-permute-start(f32[2,8,256]{2,1,0:T(8,128)S(1)} %slice.61), channel_id=1, source_target_pairs={{0,8},{1,9},{16,24},{17,25},{32,40},{33,41},{48,56},{49,57},{64,72... | collective-permute-start | bytes 49160 | tf_op jit(solution)/shard_map/ppermute | solution.py:234
  51.2 16.2 %collective-permute-start = (f32[2,8,256]{2,1,0:T(8,128)S(1)}, f32[2,8,256]{2,1,0:T(8,128)S(1)}, u32[]{:S(2)}, u32[]{:S(2)}) collective-permute-start(f32[2,8,256]{2,1,0:T(8,128)S(1)} %slice.61), channel_id=1, source_target_pairs={{0,4},{1,5},{16,20},{17,21},{32,36},{33,37},{48,52},{49,53},{64,68... | collective-permute-start | bytes 49160 | tf_op jit(solution)/shard_map/ppermute | solution.py:234
  52.5 14.9 %collective-permute-start.1 = (f32[2,8,256]{2,1,0:T(8,128)S(1)}, f32[2,8,256]{2,1,0:T(8,128)S(1)}, u32[]{:S(2)}, u32[]{:S(2)}) collective-permute-start(f32[2,8,256]{2,1,0:T(8,128)S(1)} %slice.61), channel_id=1, source_target_pairs={{0,12},{1,13},{16,28},{17,29},{32,44},{33,45},{48,60},{49,61},{64,... | collective-permute-start | bytes 49160 | tf_op jit(solution)/shard_map/ppermute | solution.py:234
  54.9 27.4 %all-to-all-start.2 = ((f32[16,64,256]{2,1,0:T(8,128)}), f32[16,64,256]{2,1,0:T(8,128)S(1)}, u32[]{:S(2)}, u32[]{:S(2)}) async-start(f32[16,64,256]{2,1,0:T(8,128)} %broadcast_in_dim.5), calls=%async_computation.2 | async-start | bytes 2097152 | tf_op jit(solution)/shard_map/all_to_all | solution.py:247
  67.4 9.7 %collective-permute-start.3 = (f32[2,8,256]{2,1,0:T(8,128)S(1)}, f32[2,8,256]{2,1,0:T(8,128)S(1)}, u32[]{:S(2)}, u32[]{:S(2)}) collective-permute-start(f32[2,8,256]{2,1,0:T(8,128)S(1)} %add_select_fusion), channel_id=1, source_target_pairs={{0,1},{1,0},{2,3},{3,2},{4,5},{5,4},{6,7},{7,6},{8,9},{9,8},{10,11... | collective-permute-start | bytes 49160 | tf_op jit(solution)/shard_map/ppermute | solution.py:239
  69.3 7.7 %collective-permute-start.4 = (f32[2,8,256]{2,1,0:T(8,128)S(1)}, f32[2,8,256]{2,1,0:T(8,128)S(1)}, u32[]{:S(2)}, u32[]{:S(2)}) collective-permute-start(f32[2,8,256]{2,1,0:T(8,128)S(1)} %add_select_fusion), channel_id=1, source_target_pairs={{0,2},{1,3},{4,6},{5,7},{8,10},{9,11},{12,14},{13,15},{16,18},{17,... | collective-permute-start | bytes 49160 | tf_op jit(solution)/shard_map/ppermute | solution.py:237
  70.6 6.4 %collective-permute-start.5 = (f32[2,8,256]{2,1,0:T(8,128)S(1)}, f32[2,8,256]{2,1,0:T(8,128)S(1)}, u32[]{:S(2)}, u32[]{:S(2)}) collective-permute-start(f32[2,8,256]{2,1,0:T(8,128)S(1)} %add_select_fusion), channel_id=1, source_target_pairs={{0,15},{1,2},{4,3},{5,6},{8,7},{9,10},{12,11},{13,14},{16,31},{17,... | collective-permute-start | bytes 49160 | tf_op jit(solution)/shard_map/ppermute | solution.py:238
  73.0 19.0 %copy-start.2 = (f32[256,256]{1,0:T(8,128)}, f32[256,256]{1,0:T(8,128)S(1)}, u32[]{:S(2)}) copy-start(f32[256,256]{1,0:T(8,128)S(1)} %get-tuple-element.14) | copy-start | bytes 786436
  73.1 19.0 %collective-permute-start.13 = (f32[256,256]{1,0:T(8,128)S(1)}, f32[256,256]{1,0:T(8,128)}, u32[]{:S(2)}, u32[]{:S(2)}) collective-permute-start(f32[256,256]{1,0:T(8,128)S(1)} %get-tuple-element.14), channel_id=1, source_target_pairs={{0,2},{1,3},{6,10},{7,11},{16,18},{17,19},{22,26},{23,27},{32,34},... | collective-permute-start | bytes 786440 | tf_op jit(solution)/shard_map/ppermute | solution.py:208
  75.0 20.0 %collective-permute-start.16 = (f32[256,256]{1,0:T(8,128)S(1)}, f32[256,256]{1,0:T(8,128)}, u32[]{:S(2)}, u32[]{:S(2)}) collective-permute-start(f32[256,256]{1,0:T(8,128)S(1)} %get-tuple-element.13), channel_id=1, source_target_pairs={{0,14},{1,15},{10,6},{11,7},{16,30},{17,31},{26,22},{27,23},{32,46... | collective-permute-start | bytes 786440 | tf_op jit(solution)/shard_map/ppermute | solution.py:208
  83.2 30.5 %copy-start.1 = (s32[2,64]{1,0:T(2,128)S(1)}, s32[2,64]{1,0:T(2,128)}, u32[]{:S(2)}) copy-start(s32[2,64]{1,0:T(2,128)} %struct.3) | copy-start | bytes 1540
  83.2 30.5 %all-to-all-start.1 = ((f32[32,24,256]{2,1,0:T(8,128)}), f32[32,24,256]{2,1,0:T(8,128)S(1)}, u32[]{:S(2)}, u32[]{:S(2)}) async-start(f32[32,24,256]{2,1,0:T(8,128)} %broadcast_in_dim.4), calls=%async_computation.1 | async-start | bytes 1572864 | tf_op jit(solution)/shard_map/all_to_all | solution.py:250
  90.0 23.7 %collective-permute-start.11 = (f32[4,256,256]{2,1,0:T(8,128)S(1)}, f32[4,256,256]{2,1,0:T(8,128)S(1)}, u32[]{:S(2)}, u32[]{:S(2)}) collective-permute-start(f32[4,256,256]{2,1,0:T(8,128)S(1)} %bitcast.34), channel_id=1, source_target_pairs={{0,16},{16,0},{32,48},{48,32},{64,80},{80,64},{96,112},{112,96},{1... | collective-permute-start | bytes 3145736 | tf_op jit(solution)/shard_map/ppermute | solution.py:248
  93.0 12.5 %collective-permute-start.14 = (f32[256,256]{1,0:T(8,128)S(1)}, f32[256,256]{1,0:T(8,128)}, u32[]{:S(2)}, u32[]{:S(2)}) collective-permute-start(f32[256,256]{1,0:T(8,128)S(1)} %broadcast_select_fusion.4), channel_id=1, source_target_pairs={{0,14},{1,15},{2,4},{3,5},{6,8},{7,9},{10,12},{11,13},{16,30},{17,... | collective-permute-start | bytes 786440 | tf_op jit(solution)/shard_map/ppermute | solution.py:208
  95.8 11.8 %collective-permute-start.17 = (f32[256,256]{1,0:T(8,128)}, f32[256,256]{1,0:T(8,128)}, u32[]{:S(2)}, u32[]{:S(2)}) collective-permute-start(f32[256,256]{1,0:T(8,128)} %broadcast_select_fusion.1), channel_id=1, source_target_pairs={{0,2},{1,3},{6,4},{7,5},{10,8},{11,9},{14,12},{15,13},{16,18},{17,... | collective-permute-start | bytes 786440 | tf_op jit(solution)/shard_map/ppermute | solution.py:208
  105.6 17.2 %collective-permute-start.18 = (f32[256,256]{1,0:T(8,128)S(1)}, f32[256,256]{1,0:T(8,128)}, u32[]{:S(2)}, u32[]{:S(2)}) collective-permute-start(f32[256,256]{1,0:T(8,128)S(1)} %broadcast_select_fusion.5.have0), channel_id=1, source_target_pairs={{0,1},{1,2},{2,3},{3,4},{4,5},{5,6},{6,7},{7,8},{8,9},{9,10},{10,1... | collective-permute-start | bytes 786440 | tf_op jit(solution)/shard_map/ppermute | solution.py:223
  108.5 14.3 %collective-permute-start.19 = (f32[256,256]{1,0:T(8,128)S(1)}, f32[256,256]{1,0:T(8,128)}, u32[]{:S(2)}, u32[]{:S(2)}) collective-permute-start(f32[256,256]{1,0:T(8,128)S(1)} %broadcast_select_fusion.2.have1), channel_id=1, source_target_pairs={{0,15},{1,0},{2,1},{3,2},{4,3},{5,4},{6,5},{7,6},{8,7},{9,8},{10,9... | collective-permute-start | bytes 786440 | tf_op jit(solution)/shard_map/ppermute | solution.py:223
  113.7 9.1 %copy-start = (f32[2,1,4,1,256,256]{5,4,3,2,1,0:T(8,128)S(1)}, f32[2,1,4,1,256,256]{5,4,3,2,1,0:T(8,128)}, u32[]{:S(2)}) copy-start(f32[2,1,4,1,256,256]{5,4,3,2,1,0:T(8,128)} %param.2) | copy-start | bytes 6291460

commit v5 on v4

--- a/solution.py
+++ b/solution.py
@@ -140,46 +140,54 @@
         rest[:, :, k * n:(k + 1) * n] = bottom.reshape(4, n, n)
 
 
-def tail_kernel(ids, struct, inv, low, high, rest, have0, have1, near0, near1, mat, out, row_high, row_rest):
+def tail_kernel(ids, struct, inv, low, high, rest, have0, have1, near0, near1, mat, out, row_high, row_rest, held, came, left):
     row, col = ids[0], ids[1]
     even = lax.rem(col, 2) == 0
     n = mat.shape[-1]
+    spots = [(p, q) for p in range(2) for q in range(4)]
+    reads = {s: pltpu.make_async_copy(mat.at[s], held.at[s], came.at[s]) for s in spots}
+    writes = {s: pltpu.make_async_copy(held.at[s], out.at[s], left.at[s]) for s in spots}
+    for s in spots:
+        reads[s].start()
     inv0, p10, inv1 = ((inv[k, 0], inv[k, 1]) for k in range(3))
-    for p, (have, near) in enumerate(((have0, near0), (have1, near1))):
+    have = jnp.concatenate([have0[...], have1[...]])
+    near = jnp.concatenate([near0[...], near1[...]])
+
+    def keep(k):
+        return jnp.concatenate([jnp.full((n, 1), struct[k, p * 32 + row].astype(jnp.float32)) for p in range(2)])
+
+    both = solve(jnp.where(even, have, near), jnp.where(even, near, have), keep(0), keep(1), inv0, p10, inv1)
+    for k in range(2):
+        top, bottom = parts(both[k])
+        row_high[:, k * n:(k + 1) * n] = top
+        row_rest[:, k * n:(k + 1) * n] = bottom
+    for p, q in spots:
         i = p * 32 + row
-        a0 = jnp.where(even, have[...], near[...])
-        a1 = jnp.where(even, near[...], have[...])
-        keep0 = struct[0, i].astype(jnp.float32)
-        keep1 = struct[1, i].astype(jnp.float32)
-        both = solve(a0, a1, keep0, keep1, inv0, p10, inv1)
-        for k in range(2):
-            top, bottom = parts(both[k])
-            row_high[:, k * n:(k + 1) * n] = top
-            row_rest[:, k * n:(k + 1) * n] = bottom
-        for q in range(4):
-            j = q * 16 + col
-
-            @pl.when(i < j)
+        j = q * 16 + col
+        rows = slice(p * n, (p + 1) * n)
+        reads[p, q].wait()
+
+        @pl.when(i >= j)
+        def _():
+            held[p, q] = held[p, q] - mul_parts((row_high[rows], row_rest[rows]), (high[q], rest[q]), BOTH)
+
+        if q == 0:
+            @pl.when((col == 0) & (i > 0))
             def _():
-                out[p, q] = mat[p, q]
-
-            @pl.when(i >= j)
+                held[p, 0] = both[0][rows]
+
+            @pl.when((col == 1) & (i > 1))
             def _():
-                left = (row_high[...], row_rest[...])
-                out[p, q] = mat[p, q] - mul_parts(left, (high[q], rest[q]), BOTH)
-
-        @pl.when((col == 0) & (i > 0))
-        def _():
-            out[p, 0] = both[0]
-
-        @pl.when((col == 1) & (i > 1))
-        def _():
-            out[p, 0] = both[1]
-
-        if p == 0:
+                held[p, 0] = both[1][rows]
+
+        if p == 0 and q == 0:
             @pl.when((col < 2) & (row == col))
             def _():
-                out[p, 0] = low[...]
+                held[0, 0] = low[...]
+
+        writes[p, q].start()
+    for s in spots:
+        writes[s].wait()
 
 
 def after(a, *values):
@@ -271,9 +279,11 @@
     result = pl.pallas_call(
         tail_kernel,
         out_shape=jax.ShapeDtypeStruct(blocks.shape, jnp.float32),
-        in_specs=[smem] * 2 + [vmem] * 9,
-        out_specs=vmem,
-        scratch_shapes=[pltpu.VMEM((width, 2 * width), jnp.bfloat16)] * 2,
+        in_specs=[smem] * 2 + [vmem] * 8 + [pl.BlockSpec(memory_space=pl.ANY)],
+        out_specs=pl.BlockSpec(memory_space=pl.ANY),
+        scratch_shapes=[pltpu.VMEM((lbr * width, 2 * width), jnp.bfloat16)] * 2
+        + [pltpu.VMEM(blocks.shape, jnp.float32)]
+        + [pltpu.SemaphoreType.DMA((lbr, lbc))] * 2,
         compiler_params=params,
         cost_estimate=pl.CostEstimate(flops=3 * 10**9, bytes_accessed=2**23, transcendentals=0),
     )(ids, structure, inv, low, high, rest, *rows, blocks)

time: 130 us -> 129 us (level)
  no operation moved by 1% of the time
where the time goes in v5:
time: 129 us; the launch traced here: 128 us
  starting transfers between devices  95.1 us (74%)
  Pallas kernels  14.1 us (11%)
  waiting for transfers between devices  10.1 us (8%)
  other arithmetic  4.06 us (3%)
  local copies, waits for them, and re-layouts  3.87 us (3%)
    ppermute x6, starting transfers between devices, spread(): lax.ppermute(a, 'col', sorted((((s + c) % ncol, (t + c) % ncol) for s, t...  27.7 us
    ppermute x4, starting transfers between devices, on_device(): lax.ppermute(both[:, k * quarter:(k + 1) * quarter], ('row', 'col'), pairs)  15.7 us
    all_to_all x1, starting transfers between devices, scatter(): lax.all_to_all(block.reshape(nrow, width // nrow, width), 'row', 0, 0)[0:2]  13 us
    all_to_all x1, starting transfers between devices, on_device(): lax.all_to_all(own, 'row', 0, 0, axis_index_groups=groups)  12.4 us
    pallas_call x1, Pallas kernels, on_device(): pl.pallas_call(head_kernel, out_shape=[jax.ShapeDtypeStruct((3, 2, width,...  9.09 us
    ppermute x2, starting transfers between devices, on_device(): lax.ppermute(a, 'col', [(s, (s + d) % ncol) for s in range(ncol)])  7.06 us
    all_to_all x1, starting transfers between devices, on_device(): raw = lax.all_to_all(raw, 'row', 0, 0)  6.75 us
    all_to_all x1, waiting for transfers between devices, on_device(): lax.all_to_all(own, 'row', 0, 0, axis_index_groups=groups)  5.16 us
  transfers between devices with their start and end apart: 23, of which 2 were waited for; matrix products, arithmetic and copies ran while one was open for 5% of the time, Pallas kernels for 7%

profile of v5, /device:TPU:6, one launch (start us, length us, event | category | flops | bytes accessed | tf_op | source)
XLA Modules:
  0.0 127.9 jit_solution(18221483962456110556)
XLA Ops:
  0.0 1.8 %slice_bitcast_fusion = (f32[256,256]{1,0:T(8,128)S(1)}, f32[1,256,256]{2,1,0:T(8,128)S(1)}, f32[256,256]{1,0:T(8,128)S(1)}, f32[1,256,256]{2,1,0:T(8,128)S(1)}, f32[32,8,256]{2,1,0:T(8,128)}) fusion(f32[2,4,256,256]{3,2,1,0:T(8,128)} %bitcast.36), kind=kLoop, calls=%fused_computation.6 | loop fusion | bytes 1835008 | tf_op jit(solution)/shard_map/squeeze | solution.py:208
  1.9 11.8 %collective-permute-start.9 = (f32[2,64,256]{2,1,0:T(8,128)S(1)}, f32[2,64,256]{2,1,0:T(8,128)S(1)}, u32[]{:S(2)}, u32[]{:S(2)}) collective-permute-start(f32[2,64,256]{2,1,0:T(8,128)S(1)} %get-tuple-element.22), channel_id=1, source_target_pairs={{0,96},{1,224},{16,97},{17,225},{32,98},{33,226},{48,99},{49,227},... | collective-permute-start | bytes 393224 | tf_op jit(solution)/shard_map/ppermute | solution.py:240
  13.7 1.3 %collective-permute-start.8 = (f32[2,64,256]{2,1,0:T(8,128)S(1)}, f32[2,64,256]{2,1,0:T(8,128)S(1)}, u32[]{:S(2)}, u32[]{:S(2)}) collective-permute-start(f32[2,64,256]{2,1,0:T(8,128)S(1)} %get-tuple-element.23), channel_id=1, source_target_pairs={{0,64},{1,192},{16,65},{17,193},{32,66},{33,194},{48,67},{49,195},... | collective-permute-start | bytes 393224 | tf_op jit(solution)/shard_map/ppermute | solution.py:240
  15.0 1.3 %collective-permute-start.6 = (f32[2,64,256]{2,1,0:T(8,128)S(1)}, f32[2,64,256]{2,1,0:T(8,128)S(1)}, u32[]{:S(2)}, u32[]{:S(2)}) collective-permute-start(f32[2,64,256]{2,1,0:T(8,128)S(1)} %get-tuple-element.21), channel_id=1, source_target_pairs={{0,0},{1,128},{16,1},{17,129},{32,2},{33,130},{48,3},{49,131},{64,... | collective-permute-start | bytes 393224 | tf_op jit(solution)/shard_map/ppermute | solution.py:240
  16.3 1.3 %collective-permute-start.7 = (f32[2,64,256]{2,1,0:T(8,128)S(1)}, f32[2,64,256]{2,1,0:T(8,128)S(1)}, u32[]{:S(2)}, u32[]{:S(2)}) collective-permute-start(f32[2,64,256]{2,1,0:T(8,128)S(1)} %get-tuple-element.20), channel_id=1, source_target_pairs={{0,32},{1,160},{16,33},{17,161},{32,34},{33,162},{48,35},{49,163},... | collective-permute-start | bytes 393224 | tf_op jit(solution)/shard_map/ppermute | solution.py:240
  17.6 13.0 %all-to-all-start = ((f32[32,8,256]{2,1,0:T(8,128)}), f32[32,8,256]{2,1,0:T(8,128)S(1)}, u32[]{:S(2)}, u32[]{:S(2)}) async-start(f32[32,8,256]{2,1,0:T(8,128)} %get-tuple-element.19), calls=%async_computation | async-start | bytes 524288 | tf_op jit(solution)/shard_map/all_to_all | solution.py:211
  30.7 2.1 %collective-permute-start.10 = (f32[64,256]{1,0:T(8,128)S(1)}, f32[64,256]{1,0:T(8,128)S(1)}, u32[]{:S(2)}, u32[]{:S(2)}) collective-permute-start(f32[64,256]{1,0:T(8,128)S(1)} %slice_bitcast_fusion.5), channel_id=1, source_target_pairs={{0,16},{16,0},{32,48},{48,32},{64,80},{80,64},{96,112},{112,96},{1... | collective-permute-start | bytes 196616 | tf_op jit(solution)/shard_map/ppermute | solution.py:241
  32.8 15.6 %collective-permute-start.15 = (f32[256,256]{1,0:T(8,128)S(1)}, f32[256,256]{1,0:T(8,128)S(1)}, u32[]{:S(2)}, u32[]{:S(2)}) collective-permute-start(f32[256,256]{1,0:T(8,128)S(1)} %get-tuple-element.15), channel_id=1, source_target_pairs={{0,10},{1,11},{16,26},{17,27},{32,42},{33,43},{48,58},{49,59},{64,... | collective-permute-start | bytes 786440 | tf_op jit(solution)/shard_map/ppermute | solution.py:216
  48.5 1.3 %collective-permute-start.12 = (f32[256,256]{1,0:T(8,128)S(1)}, f32[256,256]{1,0:T(8,128)S(1)}, u32[]{:S(2)}, u32[]{:S(2)}) collective-permute-start(f32[256,256]{1,0:T(8,128)S(1)} %get-tuple-element.17), channel_id=1, source_target_pairs={{0,6},{1,7},{16,22},{17,23},{32,38},{33,39},{48,54},{49,55},{64,70... | collective-permute-start | bytes 786440 | tf_op jit(solution)/shard_map/ppermute | solution.py:216
  49.9 1.3 %collective-permute-start.2 = (f32[2,8,256]{2,1,0:T(8,128)S(1)}, f32[2,8,256]{2,1,0:T(8,128)S(1)}, u32[]{:S(2)}, u32[]{:S(2)}) collective-permute-start(f32[2,8,256]{2,1,0:T(8,128)S(1)} %slice.61), channel_id=1, source_target_pairs={{0,8},{1,9},{16,24},{17,25},{32,40},{33,41},{48,56},{49,57},{64,72... | collective-permute-start | bytes 49160 | tf_op jit(solution)/shard_map/ppermute | solution.py:242
  51.2 1.3 %collective-permute-start = (f32[2,8,256]{2,1,0:T(8,128)S(1)}, f32[2,8,256]{2,1,0:T(8,128)S(1)}, u32[]{:S(2)}, u32[]{:S(2)}) collective-permute-start(f32[2,8,256]{2,1,0:T(8,128)S(1)} %slice.61), channel_id=1, source_target_pairs={{0,4},{1,5},{16,20},{17,21},{32,36},{33,37},{48,52},{49,53},{64,68... | collective-permute-start | bytes 49160 | tf_op jit(solution)/shard_map/ppermute | solution.py:242
  52.5 1.3 %collective-permute-start.1 = (f32[2,8,256]{2,1,0:T(8,128)S(1)}, f32[2,8,256]{2,1,0:T(8,128)S(1)}, u32[]{:S(2)}, u32[]{:S(2)}) collective-permute-start(f32[2,8,256]{2,1,0:T(8,128)S(1)} %slice.61), channel_id=1, source_target_pairs={{0,12},{1,13},{16,28},{17,29},{32,44},{33,45},{48,60},{49,61},{64,... | collective-permute-start | bytes 49160 | tf_op jit(solution)/shard_map/ppermute | solution.py:242
  53.8 1.1 broadcast_in_dim.5
  54.9 12.4 %all-to-all-start.2 = ((f32[16,64,256]{2,1,0:T(8,128)}), f32[16,64,256]{2,1,0:T(8,128)S(1)}, u32[]{:S(2)}, u32[]{:S(2)}) async-start(f32[16,64,256]{2,1,0:T(8,128)} %broadcast_in_dim.5), calls=%async_computation.2 | async-start | bytes 2097152 | tf_op jit(solution)/shard_map/all_to_all | solution.py:255
  67.4 1.9 %collective-permute-start.3 = (f32[2,8,256]{2,1,0:T(8,128)S(1)}, f32[2,8,256]{2,1,0:T(8,128)S(1)}, u32[]{:S(2)}, u32[]{:S(2)}) collective-permute-start(f32[2,8,256]{2,1,0:T(8,128)S(1)} %add_select_fusion), channel_id=1, source_target_pairs={{0,1},{1,0},{2,3},{3,2},{4,5},{5,4},{6,7},{7,6},{8,9},{9,8},{10,11... | collective-permute-start | bytes 49160 | tf_op jit(solution)/shard_map/ppermute | solution.py:247
  69.3 1.3 %collective-permute-start.4 = (f32[2,8,256]{2,1,0:T(8,128)S(1)}, f32[2,8,256]{2,1,0:T(8,128)S(1)}, u32[]{:S(2)}, u32[]{:S(2)}) collective-permute-start(f32[2,8,256]{2,1,0:T(8,128)S(1)} %add_select_fusion), channel_id=1, source_target_pairs={{0,2},{1,3},{4,6},{5,7},{8,10},{9,11},{12,14},{13,15},{16,18},{17,... | collective-permute-start | bytes 49160 | tf_op jit(solution)/shard_map/ppermute | solution.py:245
  70.6 1.3 %collective-permute-start.5 = (f32[2,8,256]{2,1,0:T(8,128)S(1)}, f32[2,8,256]{2,1,0:T(8,128)S(1)}, u32[]{:S(2)}, u32[]{:S(2)}) collective-permute-start(f32[2,8,256]{2,1,0:T(8,128)S(1)} %add_select_fusion), channel_id=1, source_target_pairs={{0,15},{1,2},{4,3},{5,6},{8,7},{9,10},{12,11},{13,14},{16,31},{17,... | collective-permute-start | bytes 49160 | tf_op jit(solution)/shard_map/ppermute | solution.py:246
  71.9 1.1 broadcast_select_fusion
  73.1 2.0 %collective-permute-start.13 = (f32[256,256]{1,0:T(8,128)S(1)}, f32[256,256]{1,0:T(8,128)}, u32[]{:S(2)}, u32[]{:S(2)}) collective-permute-start(f32[256,256]{1,0:T(8,128)S(1)} %get-tuple-element.14), channel_id=1, source_target_pairs={{0,2},{1,3},{6,10},{7,11},{16,18},{17,19},{22,26},{23,27},{32,34},... | collective-permute-start | bytes 786440 | tf_op jit(solution)/shard_map/ppermute | solution.py:216
  75.0 2.0 %collective-permute-start.16 = (f32[256,256]{1,0:T(8,128)S(1)}, f32[256,256]{1,0:T(8,128)}, u32[]{:S(2)}, u32[]{:S(2)}) collective-permute-start(f32[256,256]{1,0:T(8,128)S(1)} %get-tuple-element.13), channel_id=1, source_target_pairs={{0,14},{1,15},{10,6},{11,7},{16,30},{17,31},{26,22},{27,23},{32,46... | collective-permute-start | bytes 786440 | tf_op jit(solution)/shard_map/ppermute | solution.py:216
  77.1 5.2 %all-to-all-done.2 = f32[16,64,256]{2,1,0:T(8,128)S(1)} async-done(((f32[16,64,256]{2,1,0:T(8,128)}), f32[16,64,256]{2,1,0:T(8,128)S(1)}, u32[]{:S(2)}, u32[]{:S(2)}) %all-to-all-start.2) | async-done | bytes 1048608 | tf_op jit(solution)/shard_map/all_to_all | solution.py:255
  83.2 6.8 %all-to-all-start.1 = ((f32[32,24,256]{2,1,0:T(8,128)}), f32[32,24,256]{2,1,0:T(8,128)S(1)}, u32[]{:S(2)}, u32[]{:S(2)}) async-start(f32[32,24,256]{2,1,0:T(8,128)} %broadcast_in_dim.4), calls=%async_computation.1 | async-start | bytes 1572864 | tf_op jit(solution)/shard_map/all_to_all | solution.py:258
  90.0 2.1 %collective-permute-start.11 = (f32[4,256,256]{2,1,0:T(8,128)S(1)}, f32[4,256,256]{2,1,0:T(8,128)S(1)}, u32[]{:S(2)}, u32[]{:S(2)}) collective-permute-start(f32[4,256,256]{2,1,0:T(8,128)S(1)} %bitcast.34), channel_id=1, source_target_pairs={{0,16},{16,0},{32,48},{48,32},{64,80},{80,64},{96,112},{112,96},{1... | collective-permute-start | bytes 3145736 | tf_op jit(solution)/shard_map/ppermute | solution.py:256
  92.0 1.0 broadcast_select_fusion.4
  93.0 2.0 %collective-permute-start.14 = (f32[256,256]{1,0:T(8,128)S(1)}, f32[256,256]{1,0:T(8,128)}, u32[]{:S(2)}, u32[]{:S(2)}) collective-permute-start(f32[256,256]{1,0:T(8,128)S(1)} %broadcast_select_fusion.4), channel_id=1, source_target_pairs={{0,14},{1,15},{2,4},{3,5},{6,8},{7,9},{10,12},{11,13},{16,30},{17,... | collective-permute-start | bytes 786440 | tf_op jit(solution)/shard_map/ppermute | solution.py:216
  95.8 4.8 %collective-permute-start.17 = (f32[256,256]{1,0:T(8,128)}, f32[256,256]{1,0:T(8,128)}, u32[]{:S(2)}, u32[]{:S(2)}) collective-permute-start(f32[256,256]{1,0:T(8,128)} %broadcast_select_fusion.1), channel_id=1, source_target_pairs={{0,2},{1,3},{6,4},{7,5},{10,8},{11,9},{14,12},{15,13},{16,18},{17,... | collective-permute-start | bytes 786440 | tf_op jit(solution)/shard_map/ppermute | solution.py:216
  100.7 4.9 %collective-permute-done.14 = f32[256,256]{1,0:T(8,128)} collective-permute-done((f32[256,256]{1,0:T(8,128)S(1)}, f32[256,256]{1,0:T(8,128)}, u32[]{:S(2)}, u32[]{:S(2)}) %collective-permute-start.14) | collective-permute-done | bytes 262176 | tf_op jit(solution)/shard_map/ppermute | solution.py:216
  105.6 1.9 %collective-permute-start.18 = (f32[256,256]{1,0:T(8,128)S(1)}, f32[256,256]{1,0:T(8,128)}, u32[]{:S(2)}, u32[]{:S(2)}) collective-permute-start(f32[256,256]{1,0:T(8,128)S(1)} %broadcast_select_fusion.5.have0), channel_id=1, source_target_pairs={{0,1},{1,2},{2,3},{3,4},{4,5},{5,6},{6,7},{7,8},{8,9},{9,10},{10,1... | collective-permute-start | bytes 786440 | tf_op jit(solution)/shard_map/ppermute | solution.py:231
  107.5 1.0 broadcast_select_fusion.2.have1
  108.5 5.1 %collective-permute-start.19 = (f32[256,256]{1,0:T(8,128)S(1)}, f32[256,256]{1,0:T(8,128)}, u32[]{:S(2)}, u32[]{:S(2)}) collective-permute-start(f32[256,256]{1,0:T(8,128)S(1)} %broadcast_select_fusion.2.have1), channel_id=1, source_target_pairs={{0,15},{1,0},{2,1},{3,2},{4,3},{5,4},{6,5},{7,6},{8,7},{9,8},{10,9... | collective-permute-start | bytes 786440 | tf_op jit(solution)/shard_map/ppermute | solution.py:231
  113.7 9.1 %shard_map.28 = (bf16[3,2,256,256]{3,2,1,0:T(8,128)(2,1)S(1)}, f32[256,256]{1,0:T(8,128)S(1)}, bf16[4,256,512]{2,1,0:T(8,128)(2,1)S(1)}, bf16[4,256,512]{2,1,0:T(8,128)(2,1)S(1)}) custom-call(s32[3]{0:T(128)S(1)} %pad_add_fusion.ids, s32[2,64]{1,0:T(2,128)S(1)} %copy-done.1, f32[32,24,256]{2,1,0:T(8,128)S(1)} %all-to-all-done.1.raw, ...), custom_call_target="tpu_custom_call" | custom-call | flops 10000000000 | bytes 4194304 | tf_op jit(solution)/shard_map/pallas_call | solution.py:265
  122.8 5.1 %shard_map.29 = f32[2,4,256,256]{3,2,1,0:T(8,128)} custom-call(s32[3]{0:T(128)S(1)} %pad_add_fusion.ids, s32[2,64]{1,0:T(2,128)S(1)} %copy-done.1, bf16[3,2,256,256]{3,2,1,0:T(8,128)(2,1)S(1)} %get-tuple-element.9.inv, f32[256,256]{1,0:T(8,128)S(1)} %get-tuple-element.10.low, bf16[4,256,512]{2,1,0:T(8,128)(2,1)S(1)} %get-tuple-element.11.high, ...), custom_call_target="tpu_custom_call" | custom-call | flops 3000000000 | bytes 8388608 | tf_op jit(solution)/shard_map/pallas_call | solution.py:279
  (40 shorter events, 2.0 us)
Async XLA Ops:
  1.9 28.8 %collective-permute-start.9 = (f32[2,64,256]{2,1,0:T(8,128)S(1)}, f32[2,64,256]{2,1,0:T(8,128)S(1)}, u32[]{:S(2)}, u32[]{:S(2)}) collective-permute-start(f32[2,64,256]{2,1,0:T(8,128)S(1)} %get-tuple-element.22), channel_id=1, source_target_pairs={{0,96},{1,224},{16,97},{17,225},{32,98},{33,226},{48,99},{49,227},... | collective-permute-start | bytes 393224 | tf_op jit(solution)/shard_map/ppermute | solution.py:240
  13.7 17.0 %collective-permute-start.8 = (f32[2,64,256]{2,1,0:T(8,128)S(1)}, f32[2,64,256]{2,1,0:T(8,128)S(1)}, u32[]{:S(2)}, u32[]{:S(2)}) collective-permute-start(f32[2,64,256]{2,1,0:T(8,128)S(1)} %get-tuple-element.23), channel_id=1, source_target_pairs={{0,64},{1,192},{16,65},{17,193},{32,66},{33,194},{48,67},{49,195},... | collective-permute-start | bytes 393224 | tf_op jit(solution)/shard_map/ppermute | solution.py:240
  15.0 15.7 %collective-permute-start.6 = (f32[2,64,256]{2,1,0:T(8,128)S(1)}, f32[2,64,256]{2,1,0:T(8,128)S(1)}, u32[]{:S(2)}, u32[]{:S(2)}) collective-permute-start(f32[2,64,256]{2,1,0:T(8,128)S(1)} %get-tuple-element.21), channel_id=1, source_target_pairs={{0,0},{1,128},{16,1},{17,129},{32,2},{33,130},{48,3},{49,131},{64,... | collective-permute-start | bytes 393224 | tf_op jit(solution)/shard_map/ppermute | solution.py:240
  16.3 14.4 %collective-permute-start.7 = (f32[2,64,256]{2,1,0:T(8,128)S(1)}, f32[2,64,256]{2,1,0:T(8,128)S(1)}, u32[]{:S(2)}, u32[]{:S(2)}) collective-permute-start(f32[2,64,256]{2,1,0:T(8,128)S(1)} %get-tuple-element.20), channel_id=1, source_target_pairs={{0,32},{1,160},{16,33},{17,161},{32,34},{33,162},{48,35},{49,163},... | collective-permute-start | bytes 393224 | tf_op jit(solution)/shard_map/ppermute | solution.py:240
  17.6 32.3 %all-to-all-start = ((f32[32,8,256]{2,1,0:T(8,128)}), f32[32,8,256]{2,1,0:T(8,128)S(1)}, u32[]{:S(2)}, u32[]{:S(2)}) async-start(f32[32,8,256]{2,1,0:T(8,128)} %get-tuple-element.19), calls=%async_computation | async-start | bytes 524288 | tf_op jit(solution)/shard_map/all_to_all | solution.py:211
  30.7 21.8 %collective-permute-start.10 = (f32[64,256]{1,0:T(8,128)S(1)}, f32[64,256]{1,0:T(8,128)S(1)}, u32[]{:S(2)}, u32[]{:S(2)}) collective-permute-start(f32[64,256]{1,0:T(8,128)S(1)} %slice_bitcast_fusion.5), channel_id=1, source_target_pairs={{0,16},{16,0},{32,48},{48,32},{64,80},{80,64},{96,112},{112,96},{1... | collective-permute-start | bytes 196616 | tf_op jit(solution)/shard_map/ppermute | solution.py:241
  32.8 39.1 %collective-permute-start.15 = (f32[256,256]{1,0:T(8,128)S(1)}, f32[256,256]{1,0:T(8,128)S(1)}, u32[]{:S(2)}, u32[]{:S(2)}) collective-permute-start(f32[256,256]{1,0:T(8,128)S(1)} %get-tuple-element.15), channel_id=1, source_target_pairs={{0,10},{1,11},{16,26},{17,27},{32,42},{33,43},{48,58},{49,59},{64,... | collective-permute-start | bytes 786440 | tf_op jit(solution)/shard_map/ppermute | solution.py:216
  48.5 23.5 %collective-permute-start.12 = (f32[256,256]{1,0:T(8,128)S(1)}, f32[256,256]{1,0:T(8,128)S(1)}, u32[]{:S(2)}, u32[]{:S(2)}) collective-permute-start(f32[256,256]{1,0:T(8,128)S(1)} %get-tuple-element.17), channel_id=1, source_target_pairs={{0,6},{1,7},{16,22},{17,23},{32,38},{33,39},{48,54},{49,55},{64,70... | collective-permute-start | bytes 786440 | tf_op jit(solution)/shard_map/ppermute | solution.py:216
  49.9 17.4 %collective-permute-start.2 = (f32[2,8,256]{2,1,0:T(8,128)S(1)}, f32[2,8,256]{2,1,0:T(8,128)S(1)}, u32[]{:S(2)}, u32[]{:S(2)}) collective-permute-start(f32[2,8,256]{2,1,0:T(8,128)S(1)} %slice.61), channel_id=1, source_target_pairs={{0,8},{1,9},{16,24},{17,25},{32,40},{33,41},{48,56},{49,57},{64,72... | collective-permute-start | bytes 49160 | tf_op jit(solution)/shard_map/ppermute | solution.py:242
  51.2 16.2 %collective-permute-start = (f32[2,8,256]{2,1,0:T(8,128)S(1)}, f32[2,8,256]{2,1,0:T(8,128)S(1)}, u32[]{:S(2)}, u32[]{:S(2)}) collective-permute-start(f32[2,8,256]{2,1,0:T(8,128)S(1)} %slice.61), channel_id=1, source_target_pairs={{0,4},{1,5},{16,20},{17,21},{32,36},{33,37},{48,52},{49,53},{64,68... | collective-permute-start | bytes 49160 | tf_op jit(solution)/shard_map/ppermute | solution.py:242
  52.5 14.9 %collective-permute-start.1 = (f32[2,8,256]{2,1,0:T(8,128)S(1)}, f32[2,8,256]{2,1,0:T(8,128)S(1)}, u32[]{:S(2)}, u32[]{:S(2)}) collective-permute-start(f32[2,8,256]{2,1,0:T(8,128)S(1)} %slice.61), channel_id=1, source_target_pairs={{0,12},{1,13},{16,28},{17,29},{32,44},{33,45},{48,60},{49,61},{64,... | collective-permute-start | bytes 49160 | tf_op jit(solution)/shard_map/ppermute | solution.py:242
  54.9 27.4 %all-to-all-start.2 = ((f32[16,64,256]{2,1,0:T(8,128)}), f32[16,64,256]{2,1,0:T(8,128)S(1)}, u32[]{:S(2)}, u32[]{:S(2)}) async-start(f32[16,64,256]{2,1,0:T(8,128)} %broadcast_in_dim.5), calls=%async_computation.2 | async-start | bytes 2097152 | tf_op jit(solution)/shard_map/all_to_all | solution.py:255
  67.4 9.7 %collective-permute-start.3 = (f32[2,8,256]{2,1,0:T(8,128)S(1)}, f32[2,8,256]{2,1,0:T(8,128)S(1)}, u32[]{:S(2)}, u32[]{:S(2)}) collective-permute-start(f32[2,8,256]{2,1,0:T(8,128)S(1)} %add_select_fusion), channel_id=1, source_target_pairs={{0,1},{1,0},{2,3},{3,2},{4,5},{5,4},{6,7},{7,6},{8,9},{9,8},{10,11... | collective-permute-start | bytes 49160 | tf_op jit(solution)/shard_map/ppermute | solution.py:247
  69.3 7.7 %collective-permute-start.4 = (f32[2,8,256]{2,1,0:T(8,128)S(1)}, f32[2,8,256]{2,1,0:T(8,128)S(1)}, u32[]{:S(2)}, u32[]{:S(2)}) collective-permute-start(f32[2,8,256]{2,1,0:T(8,128)S(1)} %add_select_fusion), channel_id=1, source_target_pairs={{0,2},{1,3},{4,6},{5,7},{8,10},{9,11},{12,14},{13,15},{16,18},{17,... | collective-permute-start | bytes 49160 | tf_op jit(solution)/shard_map/ppermute | solution.py:245
  70.6 6.4 %collective-permute-start.5 = (f32[2,8,256]{2,1,0:T(8,128)S(1)}, f32[2,8,256]{2,1,0:T(8,128)S(1)}, u32[]{:S(2)}, u32[]{:S(2)}) collective-permute-start(f32[2,8,256]{2,1,0:T(8,128)S(1)} %add_select_fusion), channel_id=1, source_target_pairs={{0,15},{1,2},{4,3},{5,6},{8,7},{9,10},{12,11},{13,14},{16,31},{17,... | collective-permute-start | bytes 49160 | tf_op jit(solution)/shard_map/ppermute | solution.py:246
  73.0 19.0 %copy-start.2 = (f32[256,256]{1,0:T(8,128)}, f32[256,256]{1,0:T(8,128)S(1)}, u32[]{:S(2)}) copy-start(f32[256,256]{1,0:T(8,128)S(1)} %get-tuple-element.14) | copy-start | bytes 786436
  73.1 19.0 %collective-permute-start.13 = (f32[256,256]{1,0:T(8,128)S(1)}, f32[256,256]{1,0:T(8,128)}, u32[]{:S(2)}, u32[]{:S(2)}) collective-permute-start(f32[256,256]{1,0:T(8,128)S(1)} %get-tuple-element.14), channel_id=1, source_target_pairs={{0,2},{1,3},{6,10},{7,11},{16,18},{17,19},{22,26},{23,27},{32,34},... | collective-permute-start | bytes 786440 | tf_op jit(solution)/shard_map/ppermute | solution.py:216
  75.0 20.0 %collective-permute-start.16 = (f32[256,256]{1,0:T(8,128)S(1)}, f32[256,256]{1,0:T(8,128)}, u32[]{:S(2)}, u32[]{:S(2)}) collective-permute-start(f32[256,256]{1,0:T(8,128)S(1)} %get-tuple-element.13), channel_id=1, source_target_pairs={{0,14},{1,15},{10,6},{11,7},{16,30},{17,31},{26,22},{27,23},{32,46... | collective-permute-start | bytes 786440 | tf_op jit(solution)/shard_map/ppermute | solution.py:216
  83.2 30.5 %copy-start.1 = (s32[2,64]{1,0:T(2,128)S(1)}, s32[2,64]{1,0:T(2,128)}, u32[]{:S(2)}) copy-start(s32[2,64]{1,0:T(2,128)} %struct.3) | copy-start | bytes 1540
  83.2 30.5 %all-to-all-start.1 = ((f32[32,24,256]{2,1,0:T(8,128)}), f32[32,24,256]{2,1,0:T(8,128)S(1)}, u32[]{:S(2)}, u32[]{:S(2)}) async-start(f32[32,24,256]{2,1,0:T(8,128)} %broadcast_in_dim.4), calls=%async_computation.1 | async-start | bytes 1572864 | tf_op jit(solution)/shard_map/all_to_all | solution.py:258
  90.0 23.7 %collective-permute-start.11 = (f32[4,256,256]{2,1,0:T(8,128)S(1)}, f32[4,256,256]{2,1,0:T(8,128)S(1)}, u32[]{:S(2)}, u32[]{:S(2)}) collective-permute-start(f32[4,256,256]{2,1,0:T(8,128)S(1)} %bitcast.34), channel_id=1, source_target_pairs={{0,16},{16,0},{32,48},{48,32},{64,80},{80,64},{96,112},{112,96},{1... | collective-permute-start | bytes 3145736 | tf_op jit(solution)/shard_map/ppermute | solution.py:256
  93.0 12.5 %collective-permute-start.14 = (f32[256,256]{1,0:T(8,128)S(1)}, f32[256,256]{1,0:T(8,128)}, u32[]{:S(2)}, u32[]{:S(2)}) collective-permute-start(f32[256,256]{1,0:T(8,128)S(1)} %broadcast_select_fusion.4), channel_id=1, source_target_pairs={{0,14},{1,15},{2,4},{3,5},{6,8},{7,9},{10,12},{11,13},{16,30},{17,... | collective-permute-start | bytes 786440 | tf_op jit(solution)/shard_map/ppermute | solution.py:216
  95.8 11.8 %collective-permute-start.17 = (f32[256,256]{1,0:T(8,128)}, f32[256,256]{1,0:T(8,128)}, u32[]{:S(2)}, u32[]{:S(2)}) collective-permute-start(f32[256,256]{1,0:T(8,128)} %broadcast_select_fusion.1), channel_id=1, source_target_pairs={{0,2},{1,3},{6,4},{7,5},{10,8},{11,9},{14,12},{15,13},{16,18},{17,... | collective-permute-start | bytes 786440 | tf_op jit(solution)/shard_map/ppermute | solution.py:216
  105.6 17.2 %collective-permute-start.18 = (f32[256,256]{1,0:T(8,128)S(1)}, f32[256,256]{1,0:T(8,128)}, u32[]{:S(2)}, u32[]{:S(2)}) collective-permute-start(f32[256,256]{1,0:T(8,128)S(1)} %broadcast_select_fusion.5.have0), channel_id=1, source_target_pairs={{0,1},{1,2},{2,3},{3,4},{4,5},{5,6},{6,7},{7,8},{8,9},{9,10},{10,1... | collective-permute-start | bytes 786440 | tf_op jit(solution)/shard_map/ppermute | solution.py:231
  108.5 14.3 %collective-permute-start.19 = (f32[256,256]{1,0:T(8,128)S(1)}, f32[256,256]{1,0:T(8,128)}, u32[]{:S(2)}, u32[]{:S(2)}) collective-permute-start(f32[256,256]{1,0:T(8,128)S(1)} %broadcast_select_fusion.2.have1), channel_id=1, source_target_pairs={{0,15},{1,0},{2,1},{3,2},{4,3},{5,4},{6,5},{7,6},{8,7},{9,8},{10,9... | collective-permute-start | bytes 786440 | tf_op jit(solution)/shard_map/ppermute | solution.py:231
  113.7 9.1 %copy-start = (f32[2,1,4,1,256,256]{5,4,3,2,1,0:T(8,128)S(1)}, f32[2,1,4,1,256,256]{5,4,3,2,1,0:T(8,128)}, u32[]{:S(2)}) copy-start(f32[2,1,4,1,256,256]{5,4,3,2,1,0:T(8,128)} %param.2) | copy-start | bytes 6291460
